TPU v7x, 32 devices: a whole 2x2x4 slice. The times are simulated.
32 devices in a mesh: member: 2 (over x), horiz: 16 (over z, y, core).
Axes of the slice: x: 2, y: 2, z: 4, core: 2. Of those that a mesh axis runs over, the one named last changes fastest.
Arguments:
- perturbation: float32 [16, 80, 4, 1920], P('member', 'horiz'), parts along dimension 0, may hold values from -36 to 36
- base_state: float32 [8, 80, 4, 1920], P(None, 'horiz'), may hold values from -6 to 6
- target_state: float32 [8, 80, 4, 1920], P(None, 'horiz'), may hold values from -6 to 6
- cost_weight: float32 [80, 1920], P('horiz'), may hold values from 0.5 to 6
- diffusivity: float32 [80, 1920], P('horiz'), may hold values from 0.04 to 0.2
- chan_mix: float32 [8, 4, 4], replicated, may hold values from -3 to 3
- coupler_mix: float32 [4, 4], replicated, may hold values from -3 to 3
- owner_mix: float32 [16, 80, 80], P('horiz'), may hold values from -0.625 to 0.625
- air_temp: float32 [2, 16, 80, 128], P(None, 'horiz'), may hold values from -6 to 6
- wind_speed: float32 [2, 16, 80, 128], P(None, 'horiz'), may hold values from 2 to 12
- wet_list: int32 [16, 75], P('horiz'), may hold values from -1 to 74, as said below
- wet_owner: int32 [16, 75], P('horiz'), may hold values from -1 to 15, as said below
- remap_src: int32 [240], P('horiz'), may hold values from 0 to 79, as said below
- remap_tgt: int32 [240], P('horiz'), may hold values from 0 to 31, as said below
- remap_weight: float32 [240], P('horiz'), may hold values from 0.2 to 0.8
Outputs:
- new_perturbation: float32 [16, 80, 4, 1920], P('member', 'horiz'), parts along dimension 0
There are 2 independent parts, one for each index of `member`. A program takes and returns all parts, laid end to end along the dimension named above; an argument that names none is the same for every part. Nothing has to cross between parts.
Inputs may be any that keep to these rules, and one draw needn't show every extreme that they name: Each row of wet_list names distinct tiles, valid entries first and -1 after them; wet_owner is -1 exactly where wet_list is. Every device lists at least 37 wet tiles and some device lists all 75. Within one device's list no owner appears more than 5 times, and some owner appears exactly 5 times in every device's list. `wet_owner`: see wet_list. `remap_src`: the source row of each entry is one of the rows of the device that holds the entry. `remap_tgt`: each entry's latitude row differs from (2 times its source row) // 5 by at most 1.
All inputs are finite; a program needn't handle non-finite values.
Results may differ from a plain program's by a relative error of at most 0.0001.
Values sent between devices are 32-bit elements; how exact they have to be, the bound alone decides.
No kernel may reach another device: no remote copies, remote signals or barrier semaphores. Data moves between devices by JAX's collectives and lax.ppermute only.
A program may use at most 64 MiB of HBM per device.

v0:
```python
import jax
import jax.numpy as jnp
from jax import lax
from jax.sharding import PartitionSpec as P

LAT_DEV = 2


KAPPA_V = 0.1
TIME_STEP = 0.3
FLUX_RATE = 0.05
FEEDBACK = 0.5
ASCENT = 0.5
EPSILON = 1e-06
HIGHEST = lax.Precision.HIGHEST


def with_halo(block, sides, width):
    for axis, dim in sides:
        count = lax.axis_size(axis)
        forward = [(i, i + 1) for i in range(count - 1)]
        backward = [(target, source) for source, target in forward]
        low = lax.ppermute(
            lax.slice_in_dim(block, block.shape[dim] - width, None, axis=dim), axis, forward
        )
        high = lax.ppermute(lax.slice_in_dim(block, 0, width, axis=dim), axis, backward)
        block = jnp.concatenate([low, block, high], axis=dim)
    return block


def channel_drive(ocean_field, chan_mix):
    return jnp.tanh(jnp.einsum("lck,ljkx->ljcx", chan_mix, ocean_field, precision=HIGHEST))


def level_diff(ocean_field):
    padded = jnp.pad(ocean_field, ((1, 1), (0, 0), (0, 0), (0, 0)))
    return padded[2:] + padded[:-2] - 2.0 * ocean_field


def horiz_lap(ocean_field):
    padded = with_halo(ocean_field, (("horiz", 1),), 1)
    return (
        padded[:, 2:]
        + padded[:, :-2]
        + jnp.roll(ocean_field, -1, axis=3)
        + jnp.roll(ocean_field, 1, axis=3)
        - 4.0 * ocean_field
    )


def owner_flux(arrived, air_field, wind_field, mixing, coupler_mix):
    cell_shape = arrived.shape
    flat = arrived.reshape((cell_shape[0] * cell_shape[1],) + cell_shape[2:])
    mixed = jnp.tanh(jnp.einsum("pq,qcx->pcx", mixing, flat, precision=HIGHEST))
    air_flat = air_field.reshape(flat.shape[0], flat.shape[2])
    wind_flat = wind_field.reshape(flat.shape[0], flat.shape[2])
    contrast = (
        jnp.concatenate([(air_flat - flat[:, 0, :])[:, None, :], flat[:, 1:, :]], axis=1) + mixed
    )
    forcing = jnp.einsum("ck,pkx->pcx", coupler_mix, contrast, precision=HIGHEST)
    return (FLUX_RATE * wind_flat[:, None, :] * jnp.tanh(forcing)).reshape(cell_shape)


def flux_cotangent(arrived, cotangent, air_field, wind_field, mixing, coupler_mix):

    def forward_flux(values):
        return owner_flux(values, air_field, wind_field, mixing, coupler_mix)

    _, pullback = jax.vjp(forward_flux, arrived)
    return pullback(cotangent)[0]


def to_tiles(surface, tile_width):
    row_count, channels, cells = surface.shape
    pieces = surface.reshape(row_count, channels, cells // tile_width, tile_width).transpose(
        0, 2, 1, 3
    )
    return pieces.reshape(row_count * (cells // tile_width), channels, tile_width)


def from_tiles(tile_view, row_count):
    tile_total, channels, tile_width = tile_view.shape
    per_row = tile_total // row_count
    pieces = tile_view.reshape(row_count, per_row, channels, tile_width).transpose(0, 2, 1, 3)
    return pieces.reshape(row_count, channels, per_row * tile_width)


def route_tables(wet_row, owner_row, device_count, capacity):
    live_mask = owner_row >= 0
    onehot = (owner_row[:, None] == jnp.arange(device_count, dtype=jnp.int32)[None, :]).astype(
        jnp.int32
    )
    earlier = jnp.cumsum(onehot, axis=0) - onehot
    slot_rank = jnp.sum(earlier * onehot, axis=1)
    slot_index = jnp.where(live_mask, owner_row * capacity + slot_rank, -1)
    tile_safe = jnp.where(live_mask, wet_row, 0)
    return (live_mask, slot_index, tile_safe)


def owner_round(picked, slot_index, live_mask, device_count, capacity, owner_work):
    entry_count = picked.shape[0]
    slot_total = device_count * capacity
    select = (slot_index[None, :] == jnp.arange(slot_total, dtype=jnp.int32)[:, None]).astype(
        jnp.float32
    )
    packed = jnp.dot(
        select,
        picked.reshape(entry_count, -1),
        precision=HIGHEST,
        preferred_element_type=jnp.float32,
    )
    outgoing = packed.reshape((device_count, capacity) + picked.shape[1:])
    arrived = lax.all_to_all(outgoing, "horiz", split_axis=0, concat_axis=0, tiled=True)
    result = owner_work(arrived)
    returned = lax.all_to_all(result, "horiz", split_axis=0, concat_axis=0, tiled=True)
    flattened = returned.reshape(slot_total, -1)
    taken = flattened[jnp.maximum(slot_index, 0)] * live_mask.astype(jnp.float32)[:, None]
    return (taken.reshape((entry_count,) + result.shape[2:]), arrived)


def unpack_tiles(values, tile_safe, live_mask, tile_total):
    select = (
        (tile_safe[None, :] == jnp.arange(tile_total, dtype=jnp.int32)[:, None])
        & live_mask[None, :]
    ).astype(jnp.float32)
    placed = jnp.dot(
        select,
        values.reshape(values.shape[0], -1),
        precision=HIGHEST,
        preferred_element_type=jnp.float32,
    )
    return placed.reshape((tile_total,) + values.shape[1:])


def remap_cycle(surface, source_local, remap_tgt, remap_weight, lat_rows, middle):
    row_count = surface.shape[0]
    weighted = surface[source_local] * remap_weight[:, None]
    source_select = (
        source_local[None, :] == jnp.arange(row_count, dtype=jnp.int32)[:, None]
    ).astype(jnp.float32)
    first_lat = lax.axis_index("horiz") * lat_rows - 1
    select_rows = (
        remap_tgt[None, :] - first_lat == jnp.arange(lat_rows + 2, dtype=jnp.int32)[:, None]
    ).astype(jnp.float32)
    local_sums = jnp.dot(
        select_rows, weighted, precision=HIGHEST, preferred_element_type=jnp.float32
    )
    edge_rows = jnp.stack([local_sums[0], local_sums[-1]])
    bordered = with_halo(edge_rows, (("horiz", 0),), 1)
    own_rows = local_sums[1:-1]
    own_rows = own_rows.at[0].add(bordered[0]).at[-1].add(bordered[-1])
    processed, stored = middle(own_rows)
    extended = with_halo(processed, (("horiz", 0),), 1)
    at_targets = jnp.dot(
        select_rows.T, extended, precision=HIGHEST, preferred_element_type=jnp.float32
    )
    at_targets = at_targets * remap_weight[:, None]
    returned = jnp.dot(
        source_select, at_targets, precision=HIGHEST, preferred_element_type=jnp.float32
    )
    return (returned, stored)


def forward_middle(summed):
    atmos = jnp.tanh(summed)
    return (atmos, atmos)


def body(
    perturbation,
    base_state,
    target_state,
    cost_weight,
    diffusivity,
    chan_mix,
    coupler_mix,
    owner_mix,
    air_temp,
    wind_speed,
    wet_list,
    wet_owner,
    remap_src,
    remap_tgt,
    remap_weight,
):
    device_count = lax.axis_size("horiz")
    row_count = base_state.shape[1]
    capacity = air_temp.shape[2] // device_count
    tile_total = wet_list.shape[1]
    hour_count = air_temp.shape[0]
    tile_width = air_temp.shape[3]
    mixing = owner_mix[0]
    live_mask, slot_index, tile_safe = route_tables(
        wet_list[0], wet_owner[0], device_count, capacity
    )
    source_local = remap_src - lax.axis_index("horiz") * row_count
    coeff_field = diffusivity[None, :, None, :]
    ocean_field = base_state + perturbation
    saved = []
    for hour_index in range(hour_count):
        start_field = ocean_field
        drive = channel_drive(ocean_field, chan_mix)
        ocean_field = (
            ocean_field
            + coeff_field * horiz_lap(ocean_field)
            + KAPPA_V * level_diff(ocean_field)
            + TIME_STEP * drive
        )
        picked = (
            to_tiles(ocean_field[0], tile_width)[tile_safe]
            * live_mask.astype(jnp.float32)[:, None, None]
        )
        air_now = air_temp[hour_index, 0].reshape(device_count, capacity, tile_width)
        wind_now = wind_speed[hour_index, 0].reshape(device_count, capacity, tile_width)

        def flux_work(arrived, air_now=air_now, wind_now=wind_now):
            return owner_flux(arrived, air_now, wind_now, mixing, coupler_mix)

        flux_entries, arrived = owner_round(
            picked, slot_index, live_mask, device_count, capacity, flux_work
        )
        flux_tiles = unpack_tiles(flux_entries, tile_safe, live_mask, tile_total)
        ocean_field = ocean_field.at[0].add(from_tiles(flux_tiles, row_count))
        returned, atmos = remap_cycle(
            ocean_field[0, :, 0, :], source_local, remap_tgt, remap_weight, LAT_DEV, forward_middle
        )
        ocean_field = ocean_field.at[0, :, 0, :].add(FEEDBACK * returned)
        saved.append((start_field, drive, picked, arrived, atmos, air_now, wind_now))
    adjoint = (cost_weight * cost_weight)[None, :, None, :] * (ocean_field - target_state)
    for hour_index in reversed(range(hour_count)):
        start_field, drive, picked, arrived, atmos, air_now, wind_now = saved[hour_index]

        def adjoint_middle(summed, atmos=atmos):
            return (summed * (1.0 - atmos * atmos), atmos)

        surface_cot, _ = remap_cycle(
            FEEDBACK * adjoint[0, :, 0, :],
            source_local,
            remap_tgt,
            remap_weight,
            LAT_DEV,
            adjoint_middle,
        )
        adjoint = adjoint.at[0, :, 0, :].add(surface_cot)
        cot_entries = to_tiles(adjoint[0], tile_width)[tile_safe]

        def cot_work(got, arrived=arrived, air_now=air_now, wind_now=wind_now):
            return flux_cotangent(arrived, got, air_now, wind_now, mixing, coupler_mix)

        back_entries, _ = owner_round(
            cot_entries, slot_index, live_mask, device_count, capacity, cot_work
        )
        back_tiles = unpack_tiles(back_entries, tile_safe, live_mask, tile_total)
        adjoint = adjoint.at[0].add(from_tiles(back_tiles, row_count))
        adjoint = (
            adjoint
            + horiz_lap(coeff_field * adjoint)
            + KAPPA_V * level_diff(adjoint)
            + TIME_STEP
            * jnp.einsum(
                "lck,ljcx->ljkx", chan_mix, (1.0 - drive * drive) * adjoint, precision=HIGHEST
            )
        )
    cell_total = adjoint.size * device_count
    statistics = lax.psum(
        (
            jnp.sum(perturbation * perturbation),
            jnp.sum(perturbation * adjoint),
            jnp.sum(adjoint * adjoint),
        ),
        "horiz",
    )
    mean_pp = statistics[0] / cell_total
    mean_pg = statistics[1] / cell_total
    mean_gg = statistics[2] / cell_total
    grad_scale = lax.rsqrt(mean_gg + EPSILON)
    mean_sq = (
        mean_pp
        + 2.0 * ASCENT * grad_scale * mean_pg
        + ASCENT * ASCENT * grad_scale * grad_scale * mean_gg
    )
    stepped = perturbation + ASCENT * grad_scale * adjoint
    return stepped * lax.rsqrt(mean_sq + EPSILON)


def solution(mesh):
    placed = (
        P("member", "horiz", None, None),
        P(None, "horiz", None, None),
        P(None, "horiz", None, None),
        P("horiz", None),
        P("horiz", None),
        P(),
        P(),
        P("horiz", None, None),
        P(None, "horiz", None, None),
        P(None, "horiz", None, None),
        P("horiz", None),
        P("horiz", None),
        P("horiz"),
        P("horiz"),
        P("horiz"),
    )
    return jax.shard_map(
        body,
        mesh=mesh,
        in_specs=placed,
        out_specs=P("member", "horiz", None, None),
        check_vma=False,
    )
```

profile of v0, /device:TPU:0, one launch (start us, length us, event | category | flops | bytes accessed | tf_op | source)
XLA Modules:
  0.0 295.6 jit_solution(9869927661100436124)
XLA Ops:
  0.0 1.8 copy_add_fusion
  1.9 1.3 collective-permute-start
  3.2 3.2 %collective-permute-start.1 = (f32[8,1,4,1920]{3,0,2,1:T(8,128)S(1)}, f32[8,1,4,1920]{3,0,2,1:T(8,128)S(1)}, u32[]{:S(2)}, u32[]{:S(2)}) collective-permute-start(f32[8,1,4,1920]{3,0,2,1:T(8,128)S(1)} %get-tuple-element.234), channel_id=1, source_target_pairs={{0,1},{1,2},{2,3},{3,4},{4,5},{5,6},{6,7},{7,8},{8,9},{9,10},{10,1... | collective-permute-start | bytes 737288 | tf_op jit(solution)/shard_map/ppermute | solution.py:23
  6.4 1.9 fusion.217
  8.8 3.3 %fusion.51 = f32[8,5,1920,4]{2,3,1,0:T(4,128)} fusion(f32[8,4,4,1]{1,2,3,0:T(4,128)S(1)} %copy.229, f32[8,5,4,1920]{3,0,2,1:T(8,128)S(1)} %copy_add_fusion), kind=kOutput, calls=%fused_computation.92 | convolution fusion | flops 14745600 | bytes 2458112 | tf_op jit(solution)/shard_map/lck,ljkx->ljcx/dot_general | solution.py:32
  12.3 2.9 fusion.6
  19.0 7.9 %all-to-all-start = ((f32[16,5,4,128]{3,2,1,0:T(4,128)}), f32[16,5,4,128]{3,2,1,0:T(4,128)S(1)}, u32[]{:S(2)}, u32[]{:S(2)}) async-start(f32[16,5,4,128]{3,2,1,0:T(4,128)} %copy.175), calls=%async_computation | async-start | bytes 327680 | tf_op jit(solution)/shard_map/all_to_all | solution.py:113
  27.6 7.8 %all-to-all-done = f32[16,5,4,128]{3,2,1,0:T(4,128)S(1)} async-done(((f32[16,5,4,128]{3,2,1,0:T(4,128)}), f32[16,5,4,128]{3,2,1,0:T(4,128)S(1)}, u32[]{:S(2)}, u32[]{:S(2)}) %all-to-all-start) | async-done | bytes 163872 | tf_op jit(solution)/shard_map/all_to_all | solution.py:113
  36.9 3.5 %all-to-all-start.1 = ((f32[16,5,4,128]{3,2,1,0:T(4,128)}), f32[16,5,4,128]{3,2,1,0:T(4,128)S(1)}, u32[]{:S(2)}, u32[]{:S(2)}) async-start(f32[16,5,4,128]{3,2,1,0:T(4,128)} %bitcast.25), calls=%async_computation.1 | async-start | bytes 327680 | tf_op jit(solution)/shard_map/all_to_all | solution.py:115
  40.5 8.4 %all-to-all-done.1 = f32[16,5,4,128]{3,2,1,0:T(4,128)S(1)} async-done(((f32[16,5,4,128]{3,2,1,0:T(4,128)}), f32[16,5,4,128]{3,2,1,0:T(4,128)S(1)}, u32[]{:S(2)}, u32[]{:S(2)}) %all-to-all-start.1) | async-done | bytes 163872 | tf_op jit(solution)/shard_map/all_to_all | solution.py:115
  51.0 1.3 collective-permute-start.2
  52.3 1.3 collective-permute-start.3
  53.7 1.6 collective-permute-done.3
  55.5 3.8 %collective-permute-start.4 = (f32[1,1920]{1,0:T(1,128)S(1)}, f32[1,1920]{1,0:T(1,128)S(1)}, u32[]{:S(2)}, u32[]{:S(2)}) collective-permute-start(f32[1,1920]{1,0:T(1,128)S(1)} %get-tuple-element.251), channel_id=1, source_target_pairs={{0,1},{1,2},{2,3},{3,4},{4,5},{5,6},{6,7},{7,8},{8,9},{9,10},{10,1... | collective-permute-start | bytes 23048 | tf_op jit(solution)/shard_map/ppermute | solution.py:23
  59.3 1.3 collective-permute-start.5
  60.8 2.8 scatter-add.54
  64.9 1.3 collective-permute-start.6
  66.2 4.1 %collective-permute-start.7 = (f32[8,1,4,1920]{3,0,2,1:T(8,128)S(1)}, f32[8,1,4,1920]{3,0,2,1:T(8,128)S(1)}, u32[]{:S(2)}, u32[]{:S(2)}) collective-permute-start(f32[8,1,4,1920]{3,0,2,1:T(8,128)S(1)} %get-tuple-element.228), channel_id=1, source_target_pairs={{0,1},{1,2},{2,3},{3,4},{4,5},{5,6},{6,7},{7,8},{8,9},{9,10},{10,1... | collective-permute-start | bytes 737288 | tf_op jit(solution)/shard_map/ppermute | solution.py:23
  70.3 2.3 fusion.49
  72.7 1.9 fusion.11
  74.6 1.7 slice_reduce_fusion.2
  77.8 18.7 %all_to_all.40 = f32[16,5,4,128]{3,2,1,0:T(4,128)S(1)} all-to-all(f32[16,5,4,128]{3,2,1,0:T(4,128)S(1)} %copy.189), channel_id=1, replica_groups=mesh['member'=2,'horiz'=16] {'horiz'}, dimensions={0} | all-to-all | bytes 327680 | tf_op jit(solution)/shard_map/all_to_all | solution.py:113
  97.3 11.1 %all_to_all.41 = f32[16,5,4,128]{3,2,1,0:T(4,128)S(1)} all-to-all(f32[16,5,4,128]{3,2,1,0:T(4,128)S(1)} %bitcast.281), channel_id=1, replica_groups=mesh['member'=2,'horiz'=16] {'horiz'}, dimensions={0} | all-to-all | bytes 327680 | tf_op jit(solution)/shard_map/all_to_all | solution.py:115
  109.8 1.5 slice_add_fusion.2
  112.3 1.3 collective-permute-start.8
  113.6 1.3 collective-permute-start.9
  115.0 1.6 collective-permute-done.9
  116.8 3.8 %collective-permute-start.10 = (f32[1,1920]{1,0:T(1,128)S(1)}, f32[1,1920]{1,0:T(1,128)S(1)}, u32[]{:S(2)}, u32[]{:S(2)}) collective-permute-start(f32[1,1920]{1,0:T(1,128)S(1)} %get-tuple-element.249), channel_id=1, source_target_pairs={{0,1},{1,2},{2,3},{3,4},{4,5},{5,6},{6,7},{7,8},{8,9},{9,10},{10,1... | collective-permute-start | bytes 23048 | tf_op jit(solution)/shard_map/ppermute | solution.py:23
  120.6 1.3 collective-permute-start.11
  121.9 3.3 %scatter-add.60 = f32[8,5,4,1920]{3,0,2,1:T(8,128)} dynamic-update-slice(f32[8,5,4,1920]{3,0,2,1:T(8,128)} %fusion.11, f32[1,5,4,1920]{3,0,2,1:T(1,128)S(1)} %slice_add_fusion.2, s32[]{:T(128)} %constant.398.clone.1, s32[]{:T(128)} %constant.398.clone.1, s32[]{:T(128)} %constant.398.clone.1, s32[]{:T(128)} %constant.398.clone.1) | dynamic-update-slice | bytes 307204 | tf_op jit(solution)/shard_map/scatter-add | solution.py:223
  125.7 1.8 scatter-add.65
  127.5 1.8 fusion.48
  130.4 3.0 %collective-permute-start.12 = (f32[1,1920]{1,0:T(1,128)S(1)}, f32[1,1920]{1,0:T(1,128)S(1)}, u32[]{:S(2)}, u32[]{:S(2)}) collective-permute-start(f32[1,1920]{1,0:T(1,128)S(1)} %get-tuple-element.240), channel_id=1, source_target_pairs={{0,1},{1,2},{2,3},{3,4},{4,5},{5,6},{6,7},{7,8},{8,9},{9,10},{10,1... | collective-permute-start | bytes 23048 | tf_op jit(solution)/shard_map/ppermute | solution.py:23
  133.5 1.3 collective-permute-start.13
  134.9 3.1 %collective-permute-done.13 = f32[1,1920]{1,0:T(1,128)S(1)} collective-permute-done((f32[1,1920]{1,0:T(1,128)S(1)}, f32[1,1920]{1,0:T(1,128)S(1)}, u32[]{:S(2)}, u32[]{:S(2)}) %collective-permute-start.13) | collective-permute-done | bytes 7712 | tf_op jit(solution)/shard_map/ppermute | solution.py:26
  138.1 4.3 %collective-permute-start.14 = (f32[1,1920]{1,0:T(1,128)S(1)}, f32[1,1920]{1,0:T(1,128)S(1)}, u32[]{:S(2)}, u32[]{:S(2)}) collective-permute-start(f32[1,1920]{1,0:T(1,128)S(1)} %get-tuple-element.247), channel_id=1, source_target_pairs={{0,1},{1,2},{2,3},{3,4},{4,5},{5,6},{6,7},{7,8},{8,9},{9,10},{10,1... | collective-permute-start | bytes 23048 | tf_op jit(solution)/shard_map/ppermute | solution.py:23
  142.5 1.3 collective-permute-start.15
  143.8 1.8 collective-permute-done.15
  146.8 1.5 gather_fusion.7
  150.4 17.1 %all_to_all.42 = f32[16,5,4,128]{3,2,1,0:T(4,128)S(1)} all-to-all(f32[16,5,4,128]{3,2,1,0:T(4,128)S(1)} %copy.199), channel_id=1, replica_groups=mesh['member'=2,'horiz'=16] {'horiz'}, dimensions={0} | all-to-all | bytes 327680 | tf_op jit(solution)/shard_map/all_to_all | solution.py:113
  169.2 11.1 %all_to_all.43 = f32[16,5,4,128]{3,2,1,0:T(4,128)S(1)} all-to-all(f32[16,5,4,128]{3,2,1,0:T(4,128)S(1)} %bitcast.297), channel_id=1, replica_groups=mesh['member'=2,'horiz'=16] {'horiz'}, dimensions={0} | all-to-all | bytes 327680 | tf_op jit(solution)/shard_map/all_to_all | solution.py:115
  181.9 2.8 scatter-add.71
  186.2 1.3 collective-permute-start.16
  187.5 3.0 %collective-permute-start.17 = (f32[8,1,4,1920]{3,0,2,1:T(8,128)S(1)}, f32[8,1,4,1920]{3,0,2,1:T(8,128)S(1)}, u32[]{:S(2)}, u32[]{:S(2)}) collective-permute-start(f32[8,1,4,1920]{3,0,2,1:T(8,128)S(1)} %get-tuple-element.222), channel_id=1, source_target_pairs={{0,1},{1,2},{2,3},{3,4},{4,5},{5,6},{6,7},{7,8},{8,9},{9,10},{10,1... | collective-permute-start | bytes 737288 | tf_op jit(solution)/shard_map/ppermute | solution.py:23
  190.5 2.3 fusion.46
  194.9 3.9 %collective-permute-start.18 = (f32[1,1920]{1,0:T(1,128)S(1)}, f32[1,1920]{1,0:T(1,128)S(1)}, u32[]{:S(2)}, u32[]{:S(2)}) collective-permute-start(f32[1,1920]{1,0:T(1,128)S(1)} %get-tuple-element.238), channel_id=1, source_target_pairs={{0,1},{1,2},{2,3},{3,4},{4,5},{5,6},{6,7},{7,8},{8,9},{9,10},{10,1... | collective-permute-start | bytes 23048 | tf_op jit(solution)/shard_map/ppermute | solution.py:23
  198.8 1.3 collective-permute-start.19
  200.2 3.6 %collective-permute-done.19 = f32[1,1920]{1,0:T(1,128)S(1)} collective-permute-done((f32[1,1920]{1,0:T(1,128)S(1)}, f32[1,1920]{1,0:T(1,128)S(1)}, u32[]{:S(2)}, u32[]{:S(2)}) %collective-permute-start.19) | collective-permute-done | bytes 7712 | tf_op jit(solution)/shard_map/ppermute | solution.py:26
  204.0 4.3 %collective-permute-start.20 = (f32[1,1920]{1,0:T(1,128)S(1)}, f32[1,1920]{1,0:T(1,128)S(1)}, u32[]{:S(2)}, u32[]{:S(2)}) collective-permute-start(f32[1,1920]{1,0:T(1,128)S(1)} %get-tuple-element.245), channel_id=1, source_target_pairs={{0,1},{1,2},{2,3},{3,4},{4,5},{5,6},{6,7},{7,8},{8,9},{9,10},{10,1... | collective-permute-start | bytes 23048 | tf_op jit(solution)/shard_map/ppermute | solution.py:23
  208.3 1.3 collective-permute-start.21
  209.6 1.8 collective-permute-done.21
  214.0 15.1 %all_to_all.44 = f32[16,5,4,128]{3,2,1,0:T(4,128)S(1)} all-to-all(f32[16,5,4,128]{3,2,1,0:T(4,128)S(1)} %copy.211), channel_id=1, replica_groups=mesh['member'=2,'horiz'=16] {'horiz'}, dimensions={0} | all-to-all | bytes 327680 | tf_op jit(solution)/shard_map/all_to_all | solution.py:113
  230.7 3.5 %all-to-all-start.7 = ((f32[16,5,4,128]{3,2,1,0:T(4,128)}), f32[16,5,4,128]{3,2,1,0:T(4,128)S(1)}, u32[]{:S(2)}, u32[]{:S(2)}) async-start(f32[16,5,4,128]{3,2,1,0:T(4,128)} %bitcast.73), calls=%async_computation.7 | async-start | bytes 327680 | tf_op jit(solution)/shard_map/all_to_all | solution.py:115
  234.3 1.3 multiply_reduce_fusion.1
  235.6 7.1 %all-to-all-done.7 = f32[16,5,4,128]{3,2,1,0:T(4,128)S(1)} async-done(((f32[16,5,4,128]{3,2,1,0:T(4,128)}), f32[16,5,4,128]{3,2,1,0:T(4,128)S(1)}, u32[]{:S(2)}, u32[]{:S(2)}) %all-to-all-start.7) | async-done | bytes 163872 | tf_op jit(solution)/shard_map/all_to_all | solution.py:115
  244.2 2.8 scatter-add.79
  247.1 1.5 broadcast_multiply_fusion
  249.0 1.3 collective-permute-start.22
  250.3 3.3 %collective-permute-start.23 = (f32[8,1,4,1920]{3,0,2,1:T(8,128)S(1)}, f32[8,1,4,1920]{3,0,2,1:T(8,128)S(1)}, u32[]{:S(2)}, u32[]{:S(2)}) collective-permute-start(f32[8,1,4,1920]{3,0,2,1:T(8,128)S(1)} %get-tuple-element.208), channel_id=1, source_target_pairs={{0,1},{1,2},{2,3},{3,4},{4,5},{5,6},{6,7},{7,8},{8,9},{9,10},{10,1... | collective-permute-start | bytes 737288 | tf_op jit(solution)/shard_map/ppermute | solution.py:23
  253.6 2.3 fusion.44
  256.0 2.8 multiply_reduce_fusion
  258.8 31.9 %all-reduce.8 = (f32[]{:T(128)}, f32[]{:T(128)}, f32[]{:T(128)}) all-reduce(f32[]{:T(128)} %multiply_reduce_fusion.1, f32[]{:T(128)} %get-tuple-element.198, f32[]{:T(128)} %get-tuple-element.197), channel_id=1, replica_groups=mesh['member'=2,'horiz'=16] {'horiz'}, use_global_device_ids=true, to_apply=%region_5.6 | all-reduce | flops 3 | bytes 24 | tf_op jit(solution)/shard_map/psum | solution.py:265
  292.8 1.4 add_multiply_fusion
  294.2 1.3 copy.223
  (284 shorter events, 32.9 us)
Async XLA Ops:
  0.0 35.4 %copy-start = (f32[1,80,80]{2,1,0:T(8,128)S(1)}, f32[1,80,80]{2,1,0:T(8,128)}, u32[]{:S(2)}) copy-start(f32[1,80,80]{2,1,0:T(8,128)} %param.54) | copy-start | bytes 76804
  1.9 10.4 %collective-permute-start = (f32[8,1,4,1920]{3,0,2,1:T(8,128)S(1)}, f32[8,1,4,1920]{3,0,2,1:T(8,128)S(1)}, u32[]{:S(2)}, u32[]{:S(2)}) collective-permute-start(f32[8,1,4,1920]{3,0,2,1:T(8,128)S(1)} %get-tuple-element.233), channel_id=1, source_target_pairs={{1,0},{2,1},{3,2},{4,3},{5,4},{6,5},{7,6},{8,7},{9,8},{10,9},{11,1... | collective-permute-start | bytes 737288 | tf_op jit(solution)/shard_map/ppermute | solution.py:26
  3.2 5.1 %copy-start.39 = (s32[1,75]{1,0:T(1,128)S(1)}, s32[1,75]{1,0:T(1,128)}, u32[]{:S(2)}) copy-start(s32[1,75]{1,0:T(1,128)} %param.58) | copy-start | bytes 904
  3.2 5.5 %copy-start.40 = (s32[1,75]{1,0:T(1,128)S(1)}, s32[1,75]{1,0:T(1,128)}, u32[]{:S(2)}) copy-start(s32[1,75]{1,0:T(1,128)} %param.57) | copy-start | bytes 904
  3.2 5.5 %copy-start.38 = (f32[8,4,4]{0,2,1:T(4,128)S(1)}, f32[8,4,4]{0,2,1:T(4,128)}, u32[]{:S(2)}) copy-start(f32[8,4,4]{0,2,1:T(4,128)} %param.52) | copy-start | bytes 1540
  3.2 9.1 %collective-permute-start.1 = (f32[8,1,4,1920]{3,0,2,1:T(8,128)S(1)}, f32[8,1,4,1920]{3,0,2,1:T(8,128)S(1)}, u32[]{:S(2)}, u32[]{:S(2)}) collective-permute-start(f32[8,1,4,1920]{3,0,2,1:T(8,128)S(1)} %get-tuple-element.234), channel_id=1, source_target_pairs={{0,1},{1,2},{2,3},{3,4},{4,5},{5,6},{6,7},{7,8},{8,9},{9,10},{10,1... | collective-permute-start | bytes 737288 | tf_op jit(solution)/shard_map/ppermute | solution.py:23
  8.2 69.0 %copy-start.21 = (f32[75]{0:T(128)}, f32[75]{0:T(128)S(1)}, u32[]{:S(2)}) copy-start(f32[75]{0:T(128)S(1)} %compare_convert_fusion) | copy-start | bytes 904
  8.7 40.9 %copy-start.24 = (s32[75]{0:T(128)}, s32[75]{0:T(128)S(1)}, u32[]{:S(2)}) copy-start(s32[75]{0:T(128)S(1)} %get-tuple-element.253) | copy-start | bytes 904
  8.7 68.7 %copy-start.27 = (s32[75]{0:T(128)}, s32[75]{0:T(128)S(1)}, u32[]{:S(2)}) copy-start(s32[75]{0:T(128)S(1)} %get-tuple-element.254) | copy-start | bytes 904
  8.7 40.9 %copy-start.35 = (pred[75]{0:T(512)(128)(4,1)}, pred[75]{0:T(512)(128)(4,1)S(1)}, u32[]{:S(2)}) copy-start(pred[75]{0:T(512)(128)(4,1)S(1)} %fusion.194) | copy-start | bytes 229
  8.8 61.5 %copy-start.5 = (f32[8,4,4,1]{1,2,3,0:T(4,128)}, f32[8,4,4,1]{1,2,3,0:T(4,128)S(1)}, u32[]{:S(2)}) copy-start(f32[8,4,4,1]{1,2,3,0:T(4,128)S(1)} %copy.229) | copy-start | bytes 1540
  8.8 3.3 %copy-start.41 = (s32[15]{0:T(128)S(1)}, s32[15]{0:T(128)}, u32[]{:S(2)}) copy-start(s32[15]{0:T(128)} %param.59) | copy-start | bytes 184
  8.8 3.5 %copy-start.4 = (f32[5,1920]{1,0:T(8,128)S(1)}, f32[5,1920]{1,0:T(8,128)}, u32[]{:S(2)}) copy-start(f32[5,1920]{1,0:T(8,128)} %param.51) | copy-start | bytes 115204
  12.2 51.7 %copy-start.29 = (s32[15]{0:T(128)}, s32[15]{0:T(128)S(1)}, u32[]{:S(2)}) copy-start(s32[15]{0:T(128)S(1)} %get-tuple-element.204) | copy-start | bytes 184
  12.2 64.3 %copy-start.32 = (s32[1024]{0:T(1024)}, s32[1024]{0:T(1024)S(1)}, u32[]{:S(2)}) copy-start(s32[1024]{0:T(1024)S(1)} %pad_clamp_fusion.2) | copy-start | bytes 12292
  17.0 9.9 %copy-start.13 = (f32[2,1,80,128]{3,2,1,0:T(8,128)S(1)}, f32[2,1,80,128]{3,2,1,0:T(8,128)}, u32[]{:S(2)}) copy-start(f32[2,1,80,128]{3,2,1,0:T(8,128)} %param.56) | copy-start | bytes 245764
  17.8 17.6 %copy-start.14 = (f32[2,1,80,128]{3,2,1,0:T(8,128)S(1)}, f32[2,1,80,128]{3,2,1,0:T(8,128)}, u32[]{:S(2)}) copy-start(f32[2,1,80,128]{3,2,1,0:T(8,128)} %param.55) | copy-start | bytes 245764
  18.0 17.8 %copy-start.16 = (f32[4,4]{1,0:T(4,128)S(1)}, f32[4,4]{1,0:T(4,128)}, u32[]{:S(2)}) copy-start(f32[4,4]{1,0:T(4,128)} %param.53) | copy-start | bytes 196
  19.0 16.4 %all-to-all-start = ((f32[16,5,4,128]{3,2,1,0:T(4,128)}), f32[16,5,4,128]{3,2,1,0:T(4,128)S(1)}, u32[]{:S(2)}, u32[]{:S(2)}) async-start(f32[16,5,4,128]{3,2,1,0:T(4,128)} %copy.175), calls=%async_computation | async-start | bytes 327680 | tf_op jit(solution)/shard_map/all_to_all | solution.py:113
  26.9 13.5 %copy-start.42 = (s32[15]{0:T(128)S(1)}, s32[15]{0:T(128)}, u32[]{:S(2)}) copy-start(s32[15]{0:T(128)} %param.60) | copy-start | bytes 184
  26.9 21.9 %copy-start.33 = (s32[1024]{0:T(1024)}, s32[1024]{0:T(1024)S(1)}, u32[]{:S(2)}) copy-start(s32[1024]{0:T(1024)S(1)} %pad_clamp_fusion.1) | copy-start | bytes 12292
  27.6 21.3 %copy-start.7 = (f32[80,128]{1,0:T(8,128)}, f32[80,128]{1,0:T(8,128)S(1)}, u32[]{:S(2)}) copy-start(f32[80,128]{1,0:T(8,128)S(1)} %get-tuple-element.236) | copy-start | bytes 122884
  36.9 12.0 %all-to-all-start.1 = ((f32[16,5,4,128]{3,2,1,0:T(4,128)}), f32[16,5,4,128]{3,2,1,0:T(4,128)S(1)}, u32[]{:S(2)}, u32[]{:S(2)}) async-start(f32[16,5,4,128]{3,2,1,0:T(4,128)} %bitcast.25), calls=%async_computation.1 | async-start | bytes 327680 | tf_op jit(solution)/shard_map/all_to_all | solution.py:115
  40.4 9.7 %copy-start.34 = (s32[1024]{0:T(1024)}, s32[1024]{0:T(1024)S(1)}, u32[]{:S(2)}) copy-start(s32[1024]{0:T(1024)S(1)} %pad_clamp_fusion) | copy-start | bytes 12292
  40.5 23.2 %copy-start.18 = (s32[15]{0:T(128)}, s32[15]{0:T(128)S(1)}, u32[]{:S(2)}) copy-start(s32[15]{0:T(128)S(1)} %broadcast_subtract_fusion) | copy-start | bytes 184
  51.0 2.6 collective-permute-start.2
  52.3 3.1 %collective-permute-start.3 = (f32[1,1920]{1,0:T(1,128)S(1)}, f32[1,1920]{1,0:T(1,128)S(1)}, u32[]{:S(2)}, u32[]{:S(2)}) collective-permute-start(f32[1,1920]{1,0:T(1,128)S(1)} %get-tuple-element.243), channel_id=1, source_target_pairs={{1,0},{2,1},{3,2},{4,3},{5,4},{6,5},{7,6},{8,7},{9,8},{10,9},{11,1... | collective-permute-start | bytes 23048 | tf_op jit(solution)/shard_map/ppermute | solution.py:26
  55.5 9.3 %copy-start.11 = (f32[2,1920]{1,0:T(2,128)}, f32[2,1920]{1,0:T(2,128)S(1)}, u32[]{:S(2)}) copy-start(f32[2,1920]{1,0:T(2,128)S(1)} %scatter-add.56) | copy-start | bytes 46084
  55.5 8.1 %collective-permute-start.4 = (f32[1,1920]{1,0:T(1,128)S(1)}, f32[1,1920]{1,0:T(1,128)S(1)}, u32[]{:S(2)}, u32[]{:S(2)}) collective-permute-start(f32[1,1920]{1,0:T(1,128)S(1)} %get-tuple-element.251), channel_id=1, source_target_pairs={{0,1},{1,2},{2,3},{3,4},{4,5},{5,6},{6,7},{7,8},{8,9},{9,10},{10,1... | collective-permute-start | bytes 23048 | tf_op jit(solution)/shard_map/ppermute | solution.py:23
  59.3 4.3 %collective-permute-start.5 = (f32[1,1920]{1,0:T(1,128)S(1)}, f32[1,1920]{1,0:T(1,128)S(1)}, u32[]{:S(2)}, u32[]{:S(2)}) collective-permute-start(f32[1,1920]{1,0:T(1,128)S(1)} %get-tuple-element.252), channel_id=1, source_target_pairs={{1,0},{2,1},{3,2},{4,3},{5,4},{6,5},{7,6},{8,7},{9,8},{10,9},{11,1... | collective-permute-start | bytes 23048 | tf_op jit(solution)/shard_map/ppermute | solution.py:26
  64.9 7.8 %collective-permute-start.6 = (f32[8,1,4,1920]{3,0,2,1:T(8,128)S(1)}, f32[8,1,4,1920]{3,0,2,1:T(8,128)S(1)}, u32[]{:S(2)}, u32[]{:S(2)}) collective-permute-start(f32[8,1,4,1920]{3,0,2,1:T(8,128)S(1)} %get-tuple-element.227), channel_id=1, source_target_pairs={{1,0},{2,1},{3,2},{4,3},{5,4},{6,5},{7,6},{8,7},{9,8},{10,9},{11,1... | collective-permute-start | bytes 737288 | tf_op jit(solution)/shard_map/ppermute | solution.py:26
  66.2 6.5 %collective-permute-start.7 = (f32[8,1,4,1920]{3,0,2,1:T(8,128)S(1)}, f32[8,1,4,1920]{3,0,2,1:T(8,128)S(1)}, u32[]{:S(2)}, u32[]{:S(2)}) collective-permute-start(f32[8,1,4,1920]{3,0,2,1:T(8,128)S(1)} %get-tuple-element.228), channel_id=1, source_target_pairs={{0,1},{1,2},{2,3},{3,4},{4,5},{5,6},{6,7},{7,8},{8,9},{9,10},{10,1... | collective-permute-start | bytes 737288 | tf_op jit(solution)/shard_map/ppermute | solution.py:23
  77.2 19.3 %copy-start.15 = (f32[2,1,80,128]{3,2,1,0:T(8,128)S(1)}, f32[2,1,80,128]{3,2,1,0:T(8,128)}, u32[]{:S(2)}) copy-start(f32[2,1,80,128]{3,2,1,0:T(8,128)} %param.55) | copy-start | bytes 245764
  77.4 19.4 %copy-start.9 = (f32[80,128]{1,0:T(8,128)S(1)}, f32[80,128]{1,0:T(8,128)}, u32[]{:S(2)}) copy-start(f32[80,128]{1,0:T(8,128)} %get-tuple-element.235) | copy-start | bytes 122884
  96.8 12.3 %copy-start.22 = (f32[75]{0:T(128)S(1)}, f32[75]{0:T(128)}, u32[]{:S(2)}) copy-start(f32[75]{0:T(128)} %copy-done.21) | copy-start | bytes 904
  96.8 12.3 %copy-start.25 = (s32[75]{0:T(128)S(1)}, s32[75]{0:T(128)}, u32[]{:S(2)}) copy-start(s32[75]{0:T(128)} %copy-done.24) | copy-start | bytes 904
  96.9 12.3 %copy-start.36 = (pred[75]{0:T(512)(128)(4,1)S(1)}, pred[75]{0:T(512)(128)(4,1)}, u32[]{:S(2)}) copy-start(pred[75]{0:T(512)(128)(4,1)} %copy-done.35) | copy-start | bytes 229
  109.6 12.3 %copy-start.10 = (f32[5,1920]{1,0:T(8,128)S(1)}, f32[5,1920]{1,0:T(8,128)}, u32[]{:S(2)}) copy-start(f32[5,1920]{1,0:T(8,128)} %param.50) | copy-start | bytes 115204
  111.3 14.2 %copy-start.30 = (s32[15]{0:T(128)S(1)}, s32[15]{0:T(128)}, u32[]{:S(2)}) copy-start(s32[15]{0:T(128)} %copy-done.29) | copy-start | bytes 184
  112.3 2.6 collective-permute-start.8
  113.6 3.1 %collective-permute-start.9 = (f32[1,1920]{1,0:T(1,128)S(1)}, f32[1,1920]{1,0:T(1,128)S(1)}, u32[]{:S(2)}, u32[]{:S(2)}) collective-permute-start(f32[1,1920]{1,0:T(1,128)S(1)} %get-tuple-element.241), channel_id=1, source_target_pairs={{1,0},{2,1},{3,2},{4,3},{5,4},{6,5},{7,6},{8,7},{9,8},{10,9},{11,1... | collective-permute-start | bytes 23048 | tf_op jit(solution)/shard_map/ppermute | solution.py:26
  116.8 8.4 %collective-permute-start.10 = (f32[1,1920]{1,0:T(1,128)S(1)}, f32[1,1920]{1,0:T(1,128)S(1)}, u32[]{:S(2)}, u32[]{:S(2)}) collective-permute-start(f32[1,1920]{1,0:T(1,128)S(1)} %get-tuple-element.249), channel_id=1, source_target_pairs={{0,1},{1,2},{2,3},{3,4},{4,5},{5,6},{6,7},{7,8},{8,9},{9,10},{10,1... | collective-permute-start | bytes 23048 | tf_op jit(solution)/shard_map/ppermute | solution.py:23
  120.6 4.6 %collective-permute-start.11 = (f32[1,1920]{1,0:T(1,128)S(1)}, f32[1,1920]{1,0:T(1,128)S(1)}, u32[]{:S(2)}, u32[]{:S(2)}) collective-permute-start(f32[1,1920]{1,0:T(1,128)S(1)} %get-tuple-element.250), channel_id=1, source_target_pairs={{1,0},{2,1},{3,2},{4,3},{5,4},{6,5},{7,6},{8,7},{9,8},{10,9},{11,1... | collective-permute-start | bytes 23048 | tf_op jit(solution)/shard_map/ppermute | solution.py:26
  130.4 4.4 %collective-permute-start.12 = (f32[1,1920]{1,0:T(1,128)S(1)}, f32[1,1920]{1,0:T(1,128)S(1)}, u32[]{:S(2)}, u32[]{:S(2)}) collective-permute-start(f32[1,1920]{1,0:T(1,128)S(1)} %get-tuple-element.240), channel_id=1, source_target_pairs={{0,1},{1,2},{2,3},{3,4},{4,5},{5,6},{6,7},{7,8},{8,9},{9,10},{10,1... | collective-permute-start | bytes 23048 | tf_op jit(solution)/shard_map/ppermute | solution.py:23
  133.5 4.5 %collective-permute-start.13 = (f32[1,1920]{1,0:T(1,128)S(1)}, f32[1,1920]{1,0:T(1,128)S(1)}, u32[]{:S(2)}, u32[]{:S(2)}) collective-permute-start(f32[1,1920]{1,0:T(1,128)S(1)} %get-tuple-element.239), channel_id=1, source_target_pairs={{1,0},{2,1},{3,2},{4,3},{5,4},{6,5},{7,6},{8,7},{9,8},{10,9},{11,1... | collective-permute-start | bytes 23048 | tf_op jit(solution)/shard_map/ppermute | solution.py:26
  138.1 5.6 %collective-permute-start.14 = (f32[1,1920]{1,0:T(1,128)S(1)}, f32[1,1920]{1,0:T(1,128)S(1)}, u32[]{:S(2)}, u32[]{:S(2)}) collective-permute-start(f32[1,1920]{1,0:T(1,128)S(1)} %get-tuple-element.247), channel_id=1, source_target_pairs={{0,1},{1,2},{2,3},{3,4},{4,5},{5,6},{6,7},{7,8},{8,9},{9,10},{10,1... | collective-permute-start | bytes 23048 | tf_op jit(solution)/shard_map/ppermute | solution.py:23
  142.5 3.1 %collective-permute-start.15 = (f32[1,1920]{1,0:T(1,128)S(1)}, f32[1,1920]{1,0:T(1,128)S(1)}, u32[]{:S(2)}, u32[]{:S(2)}) collective-permute-start(f32[1,1920]{1,0:T(1,128)S(1)} %get-tuple-element.248), channel_id=1, source_target_pairs={{1,0},{2,1},{3,2},{4,3},{5,4},{6,5},{7,6},{8,7},{9,8},{10,9},{11,1... | collective-permute-start | bytes 23048 | tf_op jit(solution)/shard_map/ppermute | solution.py:26
  169.1 12.0 %copy-start.23 = (f32[75]{0:T(128)S(1)}, f32[75]{0:T(128)}, u32[]{:S(2)}) copy-start(f32[75]{0:T(128)} %copy-done.21) | copy-start | bytes 904
  169.2 12.0 %copy-start.26 = (s32[75]{0:T(128)S(1)}, s32[75]{0:T(128)}, u32[]{:S(2)}) copy-start(s32[75]{0:T(128)} %copy-done.24) | copy-start | bytes 904
  169.2 12.0 %copy-start.37 = (pred[75]{0:T(512)(128)(4,1)S(1)}, pred[75]{0:T(512)(128)(4,1)}, u32[]{:S(2)}) copy-start(pred[75]{0:T(512)(128)(4,1)} %copy-done.35) | copy-start | bytes 229
  185.7 4.8 %copy-start.6 = (f32[8,4,4,1]{1,2,3,0:T(4,128)S(1)}, f32[8,4,4,1]{1,2,3,0:T(4,128)}, u32[]{:S(2)}) copy-start(f32[8,4,4,1]{1,2,3,0:T(4,128)} %copy-done.5) | copy-start | bytes 1540
  186.2 6.8 %collective-permute-start.16 = (f32[8,1,4,1920]{3,0,2,1:T(8,128)S(1)}, f32[8,1,4,1920]{3,0,2,1:T(8,128)S(1)}, u32[]{:S(2)}, u32[]{:S(2)}) collective-permute-start(f32[8,1,4,1920]{3,0,2,1:T(8,128)S(1)} %get-tuple-element.221), channel_id=1, source_target_pairs={{1,0},{2,1},{3,2},{4,3},{5,4},{6,5},{7,6},{8,7},{9,8},{10,9},{11,1... | collective-permute-start | bytes 737288 | tf_op jit(solution)/shard_map/ppermute | solution.py:26
  187.5 5.5 %collective-permute-start.17 = (f32[8,1,4,1920]{3,0,2,1:T(8,128)S(1)}, f32[8,1,4,1920]{3,0,2,1:T(8,128)S(1)}, u32[]{:S(2)}, u32[]{:S(2)}) collective-permute-start(f32[8,1,4,1920]{3,0,2,1:T(8,128)S(1)} %get-tuple-element.222), channel_id=1, source_target_pairs={{0,1},{1,2},{2,3},{3,4},{4,5},{5,6},{6,7},{7,8},{8,9},{9,10},{10,1... | collective-permute-start | bytes 737288 | tf_op jit(solution)/shard_map/ppermute | solution.py:23
  193.8 10.2 %copy-start.12 = (f32[2,1920]{1,0:T(2,128)S(1)}, f32[2,1920]{1,0:T(2,128)}, u32[]{:S(2)}) copy-start(f32[2,1920]{1,0:T(2,128)} %copy-done.11) | copy-start | bytes 46084
  193.8 17.9 %copy-start.31 = (s32[15]{0:T(128)S(1)}, s32[15]{0:T(128)}, u32[]{:S(2)}) copy-start(s32[15]{0:T(128)} %copy-done.29) | copy-start | bytes 184
  194.9 5.2 %collective-permute-start.18 = (f32[1,1920]{1,0:T(1,128)S(1)}, f32[1,1920]{1,0:T(1,128)S(1)}, u32[]{:S(2)}, u32[]{:S(2)}) collective-permute-start(f32[1,1920]{1,0:T(1,128)S(1)} %get-tuple-element.238), channel_id=1, source_target_pairs={{0,1},{1,2},{2,3},{3,4},{4,5},{5,6},{6,7},{7,8},{8,9},{9,10},{10,1... | collective-permute-start | bytes 23048 | tf_op jit(solution)/shard_map/ppermute | solution.py:23
  198.8 5.1 %collective-permute-start.19 = (f32[1,1920]{1,0:T(1,128)S(1)}, f32[1,1920]{1,0:T(1,128)S(1)}, u32[]{:S(2)}, u32[]{:S(2)}) collective-permute-start(f32[1,1920]{1,0:T(1,128)S(1)} %get-tuple-element.237), channel_id=1, source_target_pairs={{1,0},{2,1},{3,2},{4,3},{5,4},{6,5},{7,6},{8,7},{9,8},{10,9},{11,1... | collective-permute-start | bytes 23048 | tf_op jit(solution)/shard_map/ppermute | solution.py:26
  204.0 5.6 %collective-permute-start.20 = (f32[1,1920]{1,0:T(1,128)S(1)}, f32[1,1920]{1,0:T(1,128)S(1)}, u32[]{:S(2)}, u32[]{:S(2)}) collective-permute-start(f32[1,1920]{1,0:T(1,128)S(1)} %get-tuple-element.245), channel_id=1, source_target_pairs={{0,1},{1,2},{2,3},{3,4},{4,5},{5,6},{6,7},{7,8},{8,9},{9,10},{10,1... | collective-permute-start | bytes 23048 | tf_op jit(solution)/shard_map/ppermute | solution.py:23
  208.3 3.1 %collective-permute-start.21 = (f32[1,1920]{1,0:T(1,128)S(1)}, f32[1,1920]{1,0:T(1,128)S(1)}, u32[]{:S(2)}, u32[]{:S(2)}) collective-permute-start(f32[1,1920]{1,0:T(1,128)S(1)} %get-tuple-element.246), channel_id=1, source_target_pairs={{1,0},{2,1},{3,2},{4,3},{5,4},{6,5},{7,6},{8,7},{9,8},{10,9},{11,1... | collective-permute-start | bytes 23048 | tf_op jit(solution)/shard_map/ppermute | solution.py:26
  212.7 16.4 %copy-start.8 = (f32[80,128]{1,0:T(8,128)S(1)}, f32[80,128]{1,0:T(8,128)}, u32[]{:S(2)}) copy-start(f32[80,128]{1,0:T(8,128)} %copy-done.7) | copy-start | bytes 122884
  229.1 5.1 %copy-start.1 = (f32[8,5,4,1920]{3,2,1,0:T(4,128)S(1)}, f32[8,5,4,1920]{3,2,1,0:T(4,128)}, u32[]{:S(2)}) copy-start(f32[8,5,4,1920]{3,2,1,0:T(4,128)} %param.47) | copy-start | bytes 3686404
  230.7 12.0 %all-to-all-start.7 = ((f32[16,5,4,128]{3,2,1,0:T(4,128)}), f32[16,5,4,128]{3,2,1,0:T(4,128)S(1)}, u32[]{:S(2)}, u32[]{:S(2)}) async-start(f32[16,5,4,128]{3,2,1,0:T(4,128)} %bitcast.73), calls=%async_computation.7 | async-start | bytes 327680 | tf_op jit(solution)/shard_map/all_to_all | solution.py:115
  249.0 7.0 %collective-permute-start.22 = (f32[8,1,4,1920]{3,0,2,1:T(8,128)S(1)}, f32[8,1,4,1920]{3,0,2,1:T(8,128)S(1)}, u32[]{:S(2)}, u32[]{:S(2)}) collective-permute-start(f32[8,1,4,1920]{3,0,2,1:T(8,128)S(1)} %get-tuple-element.207), channel_id=1, source_target_pairs={{1,0},{2,1},{3,2},{4,3},{5,4},{6,5},{7,6},{8,7},{9,8},{10,9},{11,1... | collective-permute-start | bytes 737288 | tf_op jit(solution)/shard_map/ppermute | solution.py:26
  250.3 5.7 %collective-permute-start.23 = (f32[8,1,4,1920]{3,0,2,1:T(8,128)S(1)}, f32[8,1,4,1920]{3,0,2,1:T(8,128)S(1)}, u32[]{:S(2)}, u32[]{:S(2)}) collective-permute-start(f32[8,1,4,1920]{3,0,2,1:T(8,128)S(1)} %get-tuple-element.208), channel_id=1, source_target_pairs={{0,1},{1,2},{2,3},{3,4},{4,5},{5,6},{6,7},{7,8},{8,9},{9,10},{10,1... | collective-permute-start | bytes 737288 | tf_op jit(solution)/shard_map/ppermute | solution.py:23
  (6 other events, 9.3 us)
where the time goes:
time: 297 us; the launch traced here: 296 us
  blocking collectives  105 us (35%)
  starting transfers between devices  69.8 us (24%)
  local copies, waits for them, and re-layouts  39.3 us (13%)
  waiting for transfers between devices  36.9 us (12%)
  other arithmetic  20.9 us (7%)
  matrix products  19.5 us (7%)
  between operations  4.16 us (1%)
    all_to_all x3, blocking collectives, owner_round(): lax.all_to_all(outgoing, 'horiz', split_axis=0, concat_axis=0, tiled=True)  50.8 us
    ppermute x12, starting transfers between devices, with_halo(): lax.ppermute(lax.slice_in_dim(block, block.shape[dim] - width, None, axis...  39.3 us
    psum x1, blocking collectives, body(): lax.psum((jnp.sum(perturbation * perturbation), jnp.sum(perturbation * ad...  31.9 us
    all_to_all x2, blocking collectives, owner_round(): lax.all_to_all(result, 'horiz', split_axis=0, concat_axis=0, tiled=True)  22.1 us
    ppermute x12, starting transfers between devices, with_halo(): lax.ppermute(lax.slice_in_dim(block, 0, width, axis=dim), axis, backward)  15.5 us
    all_to_all x2, waiting for transfers between devices, owner_round(): lax.all_to_all(result, 'horiz', split_axis=0, concat_axis=0, tiled=True)  15.5 us
    ppermute x12, waiting for transfers between devices, with_halo(): lax.ppermute(lax.slice_in_dim(block, 0, width, axis=dim), axis, backward)  13.6 us
    all_to_all x1, starting transfers between devices, owner_round(): lax.all_to_all(outgoing, 'horiz', split_axis=0, concat_axis=0, tiled=True)  7.94 us
  transfers between devices with their start and end apart: 27, of which 9 were waited for; matrix products, arithmetic and copies ran while one was open for 7% of the time, Pallas kernels for 0%

commit v1 on v0

v1 whole, which is shorter than its diff:
```python
import functools

import jax
import jax.numpy as jnp
from jax import lax
from jax.experimental import pallas as pl
from jax.experimental.pallas import tpu as pltpu
from jax.sharding import PartitionSpec as P

LAT_DEV = 2
NEAR_LAT = LAT_DEV + 2
CHANNELS = 4
LEVELS = 8
WIDTH = 128
SUBLANES = 8

KAPPA_V = 0.1
TIME_STEP = 0.3
FLUX_RATE = 0.05
FEEDBACK = 0.5
ASCENT = 0.5
EPSILON = 1e-06
HIGHEST = lax.Precision.HIGHEST
VMEM_BYTES = 32 * 1024 * 1024


class Sizes:
    def __init__(self, devices, capacity, rows, cells):
        self.devices = devices
        self.capacity = capacity
        self.slots = devices * capacity
        self.rows = rows
        self.cells = cells
        self.row_tiles = cells // WIDTH
        self.tiles = rows * self.row_tiles
        self.pitch = -(-self.row_tiles // SUBLANES) * SUBLANES
        self.flat_rows = rows * self.pitch
        self.own_rows = CHANNELS * capacity
        self.chunk = -(-(self.own_rows + 2 * capacity) // SUBLANES) * SUBLANES
        self.edge_rows = CHANNELS * self.row_tiles * LEVELS
        self.surface_rows = CHANNELS * (self.tiles + 1)


def cols(tile):
    return slice(tile * WIDTH, (tile + 1) * WIDTH)


def lanes_sum(left_here, left_before, right_here, right_after, lane):
    return jnp.where(lane == 0, left_before, left_here) + jnp.where(
        lane == WIDTH - 1, right_after, right_here
    )


def levels_sum(field, sub):
    return jnp.where(sub == 0, 0.0, pltpu.roll(field, 1, 0)) + jnp.where(
        sub == LEVELS - 1, 0.0, pltpu.roll(field, LEVELS - 1, 0)
    )


def row_tiles_of(sz, ref, row):
    return ref[pl.ds(row * CHANNELS * sz.row_tiles, sz.row_tiles, stride=CHANNELS), :]


def put_row_tiles(sz, ref, row, value):
    ref[pl.ds(row * CHANNELS * sz.row_tiles, sz.row_tiles, stride=CHANNELS), :] = value


def load_edges(sz, padded, low, high):
    for side, edge in ((0, low), (sz.rows + 1, high)):
        for channel in range(CHANNELS):
            for tile in range(sz.row_tiles):
                at = (channel * sz.row_tiles + tile) * LEVELS
                padded[side, channel, :, cols(tile)] = edge[at : at + LEVELS, :]


def load_surface_row(sz, target, row, source, base):
    for tile in range(sz.row_tiles):
        for channel in range(CHANNELS):
            at = base + tile * CHANNELS + channel
            target[row, channel, 0:1, cols(tile)] = source[pl.ds(at, 1), :]


def forward_kernel(sz, first, last, *refs):
    refs = list(refs)
    field, low, high, diffusivity, mix, table = refs[:6]
    refs = refs[6:]
    if not first:
        surface, low_surface, high_surface = refs[:3]
        refs = refs[3:]
    if last:
        target, weight_sq = refs[:2]
        refs = refs[2:]
    out, drive, new_surface, packed, send_low, send_high, padded = refs

    load_edges(sz, padded, low, high)
    padded[1 : sz.rows + 1] = field[...]
    if not first:
        load_surface_row(sz, padded, 0, low_surface, 0)
        load_surface_row(sz, padded, sz.rows + 1, high_surface, 0)

        def fill(row, carry):
            load_surface_row(sz, padded, row + 1, surface, row * sz.row_tiles * CHANNELS)
            return carry

        lax.fori_loop(0, sz.rows, fill, 0)

    lane = lax.broadcasted_iota(jnp.int32, (LEVELS, WIDTH), 1)
    sub = lax.broadcasted_iota(jnp.int32, (LEVELS, WIDTH), 0)
    count = sz.row_tiles

    def one_row(row, carry):
        here = [[padded[row + 1, c, :, cols(t)] for t in range(count)] for c in range(CHANNELS)]
        for t in range(count):
            coeff = jnp.broadcast_to(diffusivity[row, 0:1, cols(t)], (LEVELS, WIDTH))
            for c in range(CHANNELS):
                mixed = mix[c * CHANNELS] * here[0][t]
                for k in range(1, CHANNELS):
                    mixed = mixed + mix[c * CHANNELS + k] * here[k][t]
                bent = jnp.tanh(mixed)
                drive[row, c, :, cols(t)] = bent
                field_here = here[c][t]
                around = lanes_sum(
                    pltpu.roll(field_here, 1, 1),
                    pltpu.roll(here[c][(t - 1) % count], 1, 1),
                    pltpu.roll(field_here, WIDTH - 1, 1),
                    pltpu.roll(here[c][(t + 1) % count], WIDTH - 1, 1),
                    lane,
                )
                around = around + (padded[row, c, :, cols(t)] + padded[row + 2, c, :, cols(t)])
                stepped = (
                    field_here
                    + coeff * (around - 4.0 * field_here)
                    + KAPPA_V * (levels_sum(field_here, sub) - 2.0 * field_here)
                    + TIME_STEP * bent
                )
                new_surface[pl.ds((row * count + t) * CHANNELS + c, 1), :] = stepped[0:1, :]
                flat_row = sz.edge_rows + row * sz.pitch + t
                if c == 0:
                    send_low[pl.ds(flat_row, 1), :] = stepped[0:1, :]
                    send_high[pl.ds(flat_row, 1), :] = stepped[0:1, :]
                if last:
                    scale = jnp.broadcast_to(weight_sq[row, 0:1, cols(t)], (LEVELS, WIDTH))
                    stepped = scale * (stepped - target[row, c, :, cols(t)])
                out[row, c, :, cols(t)] = stepped
        return carry

    lax.fori_loop(0, sz.rows, one_row, 0)
    new_surface[CHANNELS * sz.tiles :, :] = jnp.zeros((CHANNELS, WIDTH), jnp.float32)
    store_edges(sz, out, diffusivity if last else None, send_low, send_high)
    for slot in range(sz.slots):
        at = pl.multiple_of(table[slot] * CHANNELS, CHANNELS)
        packed[slot * CHANNELS : (slot + 1) * CHANNELS, :] = new_surface[pl.ds(at, CHANNELS), :]


def store_edges(sz, field, diffusivity, send_low, send_high):
    for row, send in ((0, send_low), (sz.rows - 1, send_high)):
        for channel in range(CHANNELS):
            for tile in range(sz.row_tiles):
                value = field[row, channel, :, cols(tile)]
                if diffusivity is not None:
                    value = value * jnp.broadcast_to(
                        diffusivity[row, 0:1, cols(tile)], (LEVELS, WIDTH)
                    )
                at = (channel * sz.row_tiles + tile) * LEVELS
                send[at : at + LEVELS, :] = value


def owner_kernel(sz, arrived, mixing, air, wind, bulk, flux, mixed_slope, flux_slope, flat, first):
    slots = sz.slots
    values = [arrived[pl.ds(c, slots, stride=CHANNELS), :] for c in range(CHANNELS)]
    mixed = jnp.tanh(
        jnp.dot(
            mixing[...],
            jnp.concatenate(values, axis=1),
            precision=HIGHEST,
            preferred_element_type=jnp.float32,
        )
    )
    contrast = []
    for c in range(CHANNELS):
        mixed_here = mixed[:, cols(c)]
        mixed_slope[c] = 1.0 - mixed_here * mixed_here
        contrast.append((air[...] - values[0] if c == 0 else values[c]) + mixed_here)
    rate = FLUX_RATE * wind[...]
    for c in range(CHANNELS):
        forcing = bulk[c, 0] * contrast[0]
        for k in range(1, CHANNELS):
            forcing = forcing + bulk[c, k] * contrast[k]
        bent = jnp.tanh(forcing)
        flux_slope[c] = rate * (1.0 - bent * bent)
        one = rate * bent
        flat[pl.ds(c, slots, stride=CHANNELS), :] = one
        if c == 0:
            first[...] = one
    flux[...] = jnp.zeros(flux.shape, jnp.float32)
    cap = sz.capacity
    for d in range(sz.devices):
        at = d * sz.chunk
        flux[at : at + sz.own_rows, :] = flat[d * sz.own_rows : (d + 1) * sz.own_rows, :]
        at = at + sz.own_rows
        if d > 0:
            flux[at : at + cap, :] = first[(d - 1) * cap : d * cap, :]
        if d < sz.devices - 1:
            flux[at + cap : at + 2 * cap, :] = first[(d + 1) * cap : (d + 2) * cap, :]


def owner_back_kernel(sz, arrived, mixing, mixed_slope, flux_slope, bulk, back, flat, extra):
    slots, cap = sz.slots, sz.capacity
    for d in range(sz.devices):
        at = d * sz.chunk
        flat[d * sz.own_rows : (d + 1) * sz.own_rows, :] = arrived[at : at + sz.own_rows, :]
        more = jnp.zeros((cap, WIDTH), jnp.float32)
        if d < sz.devices - 1:
            at = (d + 1) * sz.chunk + sz.own_rows
            more = more + arrived[at : at + cap, :]
        if d > 0:
            at = (d - 1) * sz.chunk + sz.own_rows + cap
            more = more + arrived[at : at + cap, :]
        extra[d * cap : (d + 1) * cap, :] = more
    forced = []
    for c in range(CHANNELS):
        got = flat[pl.ds(c, slots, stride=CHANNELS), :]
        if c == 0:
            got = got + extra[...]
        forced.append(flux_slope[c] * got)
    direct = []
    for k in range(CHANNELS):
        total = bulk[0, k] * forced[0]
        for c in range(1, CHANNELS):
            total = total + bulk[c, k] * forced[c]
        direct.append(total)
    through = lax.dot_general(
        mixing[...],
        jnp.concatenate([direct[k] * mixed_slope[k] for k in range(CHANNELS)], axis=1),
        (((0,), (0,)), ((), ())),
        precision=HIGHEST,
        preferred_element_type=jnp.float32,
    )
    for k in range(CHANNELS):
        sign = -1.0 if k == 0 else 1.0
        back[pl.ds(k, slots, stride=CHANNELS), :] = through[:, cols(k)] + sign * direct[k]


def weigh(remap, lat, rows_at, values):
    total = remap[lat, rows_at] * values[0]
    for index in range(1, len(values)):
        total = total + remap[lat, rows_at + index] * values[index]
    return total


def scatter_lats(remap, row_at, lats):
    total = remap[0, row_at] * lats[0]
    for lat in range(1, NEAR_LAT):
        total = total + remap[lat, row_at] * lats[lat]
    return total


def spread_back(sz, surface, slope, remap, tables, packed, near_low, near_high, send_low, send_high, base):
    rows, pitch, count = sz.rows, sz.pitch, sz.row_tiles
    own = [row_tiles_of(sz, surface, row) for row in range(rows)]
    lats = []
    for lat in range(NEAR_LAT):
        partial = FEEDBACK * weigh(remap, lat, rows, own)
        send = send_low if lat < LAT_DEV else send_high
        at = base + (lat % LAT_DEV) * pitch
        send[at : at + count, :] = partial
        lats.append(slope[lat * pitch : lat * pitch + count, :] * partial)
    for row in range(rows):
        put_row_tiles(sz, surface, row, own[row] + scatter_lats(remap, rows + row, lats))
        near_low[row * pitch : row * pitch + count, :] = scatter_lats(remap, row, lats)
        near_high[row * pitch : row * pitch + count, :] = scatter_lats(remap, 2 * rows + row, lats)
    blank = jnp.zeros((SUBLANES, WIDTH), jnp.float32)
    near_low[sz.flat_rows :, :] = blank
    near_high[sz.flat_rows :, :] = blank
    packed[...] = jnp.zeros(packed.shape, jnp.float32)
    cap = sz.capacity
    for slot in range(sz.slots):
        owner, rank = slot // cap, slot % cap
        at = owner * sz.chunk + rank * CHANNELS
        tile = pl.multiple_of(tables[0, slot] * CHANNELS, CHANNELS)
        packed[at : at + CHANNELS, :] = surface[pl.ds(tile, CHANNELS), :]
        at = owner * sz.chunk + sz.own_rows + rank
        packed[at : at + 1, :] = near_low[pl.ds(tables[1, slot], 1), :]
        packed[at + cap : at + cap + 1, :] = near_high[pl.ds(tables[2, slot], 1), :]


def surface_kernel(sz, last, *refs):
    refs = list(refs)
    flux, before, from_low, from_high, tables, remap = refs[:6]
    refs = refs[6:]
    if last:
        target, weight_sq = refs[:2]
        surface, slope, packed, send_low, send_high, near_low, near_high = refs[2:]
    else:
        surface, slope, send_low, send_high, near_low, near_high = refs
    rows, pitch, count, cap = sz.rows, sz.pitch, sz.row_tiles, sz.capacity
    surface[...] = before[...]
    for near, source in ((near_low, from_low), (near_high, from_high)):
        near[...] = source[sz.edge_rows :, :]
    for slot in range(sz.slots):
        owner, rank = slot // cap, slot % cap
        at = owner * sz.chunk + rank * CHANNELS
        tile = pl.multiple_of(tables[0, slot] * CHANNELS, CHANNELS)
        surface[pl.ds(tile, CHANNELS), :] = (
            before[pl.ds(tile, CHANNELS), :] + flux[at : at + CHANNELS, :]
        )
        at = owner * sz.chunk + sz.own_rows + rank
        for near, source, which in ((near_low, from_low, 1), (near_high, from_high, 2)):
            row = tables[which, slot]
            near[pl.ds(row, 1), :] = source[pl.ds(sz.edge_rows + row, 1), :] + flux[at : at + 1, :]
            at = at + cap
    surface[CHANNELS * sz.tiles :, :] = jnp.zeros((CHANNELS, WIDTH), jnp.float32)
    low = [near_low[row * pitch : row * pitch + count, :] for row in range(rows)]
    own = [row_tiles_of(sz, surface, row) for row in range(rows)]
    high = [near_high[row * pitch : row * pitch + count, :] for row in range(rows)]
    air = []
    for lat in range(NEAR_LAT):
        one = jnp.tanh(weigh(remap, lat, 0, low + own + high))
        slope[lat * pitch : lat * pitch + count, :] = 1.0 - one * one
        air.append(one)
    for row in range(rows):
        fed = own[row] + FEEDBACK * scatter_lats(remap, rows + row, air)
        put_row_tiles(sz, surface, row, fed)
    if last:
        end = CHANNELS * sz.tiles
        surface[0:end, :] = weight_sq[...] * (surface[0:end, :] - target[...])
        spread_back(
            sz, surface, slope, remap, tables, packed, near_low, near_high, send_low, send_high, 0
        )
    else:
        width = CHANNELS * count
        send_low[...] = surface[0:width, :]
        send_high[...] = surface[(rows - 1) * width : rows * width, :]


def merge_kernel(
    sz, recv_at, back, before, slope, from_low, from_high, tables, remap, diffusivity, surface, send_low, send_high
):
    rows, pitch, count = sz.rows, sz.pitch, sz.row_tiles
    surface[...] = before[...]
    for slot in range(sz.slots):
        tile = pl.multiple_of(tables[0, slot] * CHANNELS, CHANNELS)
        surface[pl.ds(tile, CHANNELS), :] = (
            before[pl.ds(tile, CHANNELS), :] + back[slot * CHANNELS : (slot + 1) * CHANNELS, :]
        )
    surface[CHANNELS * sz.tiles :, :] = jnp.zeros((CHANNELS, WIDTH), jnp.float32)
    lats = []
    for lat in range(NEAR_LAT):
        source = from_low if lat < LAT_DEV else from_high
        at = recv_at + (lat % LAT_DEV) * pitch
        lats.append(slope[lat * pitch : lat * pitch + count, :] * source[at : at + count, :])
    for row in range(rows):
        own = row_tiles_of(sz, surface, row)
        put_row_tiles(sz, surface, row, own + scatter_lats(remap, rows + row, lats))
    width = CHANNELS * count
    send_low[...] = diffusivity[0:width, :] * surface[0:width, :]
    send_high[...] = (
        diffusivity[(rows - 1) * width : rows * width, :]
        * surface[(rows - 1) * width : rows * width, :]
    )


def backward_kernel(sz, last, *refs):
    refs = list(refs)
    field, surface, low, high, low_surface, high_surface, drive, diffusivity, mix = refs[:9]
    refs = refs[9:]
    if last:
        perturbation, out, sums, local, padded = refs
    else:
        tables, remap, slope, out, new_surface, packed, send_low, send_high = refs[:8]
        local, padded, near_low, near_high = refs[8:]
    count = sz.row_tiles
    load_edges(sz, padded, low, high)
    load_surface_row(sz, padded, 0, low_surface, 0)
    load_surface_row(sz, padded, sz.rows + 1, high_surface, 0)
    local[...] = field[...]

    def fill(row, carry):
        load_surface_row(sz, local, row, surface, row * count * CHANNELS)
        for t in range(count):
            coeff = jnp.broadcast_to(diffusivity[row, 0:1, cols(t)], (LEVELS, WIDTH))
            for c in range(CHANNELS):
                padded[row + 1, c, :, cols(t)] = coeff * local[row, c, :, cols(t)]
        return carry

    lax.fori_loop(0, sz.rows, fill, 0)
    lane = lax.broadcasted_iota(jnp.int32, (LEVELS, WIDTH), 1)
    sub = lax.broadcasted_iota(jnp.int32, (LEVELS, WIDTH), 0)

    def one_row(row, carry):
        scaled = [[padded[row + 1, c, :, cols(t)] for t in range(count)] for c in range(CHANNELS)]
        for t in range(count):
            here, bent = [], []
            for c in range(CHANNELS):
                value = local[row, c, :, cols(t)]
                one = drive[row, c, :, cols(t)]
                here.append(value)
                bent.append((1.0 - one * one) * value)
            for c in range(CHANNELS):
                mixed = mix[c] * bent[0]
                for k in range(1, CHANNELS):
                    mixed = mixed + mix[k * CHANNELS + c] * bent[k]
                around = lanes_sum(
                    pltpu.roll(scaled[c][t], 1, 1),
                    pltpu.roll(scaled[c][(t - 1) % count], 1, 1),
                    pltpu.roll(scaled[c][t], WIDTH - 1, 1),
                    pltpu.roll(scaled[c][(t + 1) % count], WIDTH - 1, 1),
                    lane,
                )
                around = around + (padded[row, c, :, cols(t)] + padded[row + 2, c, :, cols(t)])
                stepped = (
                    here[c]
                    + (around - 4.0 * scaled[c][t])
                    + KAPPA_V * (levels_sum(here[c], sub) - 2.0 * here[c])
                    + TIME_STEP * mixed
                )
                out[row, c, :, cols(t)] = stepped
                if last:
                    start = perturbation[row, c, :, cols(t)]
                    carry = (
                        carry[0] + start * start,
                        carry[1] + start * stepped,
                        carry[2] + stepped * stepped,
                    )
                else:
                    new_surface[pl.ds((row * count + t) * CHANNELS + c, 1), :] = stepped[0:1, :]
        return carry

    blank = jnp.zeros((LEVELS, WIDTH), jnp.float32)
    totals = lax.fori_loop(0, sz.rows, one_row, (blank, blank, blank) if last else 0)
    if last:
        row = lax.broadcasted_iota(jnp.int32, (LEVELS, WIDTH), 0)
        held = blank
        for index in range(3):
            held = jnp.where(row == index, jnp.sum(totals[index], axis=0, keepdims=True), held)
        sums[...] = held
    else:
        new_surface[CHANNELS * sz.tiles :, :] = jnp.zeros((CHANNELS, WIDTH), jnp.float32)
        store_edges(sz, out, diffusivity, send_low, send_high)
        spread_back(
            sz,
            new_surface,
            slope,
            remap,
            tables,
            packed,
            near_low,
            near_high,
            send_low,
            send_high,
            sz.edge_rows,
        )


def call(kernel, name, inputs, outputs, scratch=()):
    def spec(where):
        return pl.BlockSpec(memory_space=where)

    return pl.pallas_call(
        kernel,
        name=name,
        in_specs=[spec(pltpu.SMEM if small else pltpu.VMEM) for _, small in inputs],
        out_specs=[spec(pltpu.VMEM) for _ in outputs],
        out_shape=[jax.ShapeDtypeStruct(shape, jnp.float32) for shape in outputs],
        scratch_shapes=[pltpu.VMEM(shape, jnp.float32) for shape in scratch],
        compiler_params=pltpu.CompilerParams(vmem_limit_bytes=VMEM_BYTES),
    )(*[array for array, _ in inputs])


def big(*arrays):
    return [(array, False) for array in arrays]


def small(*arrays):
    return [(array, True) for array in arrays]


def slot_tiles(wet_row, owner_row, capacity, slots, tiles):
    entries = owner_row.shape[0]
    order = jnp.arange(entries, dtype=jnp.int32)
    same = (owner_row[:, None] == owner_row[None, :]) & (order[None, :] < order[:, None])
    rank = jnp.sum(same.astype(jnp.int32), axis=1)
    slot = jnp.where(owner_row >= 0, owner_row * capacity + rank, -1)
    match = slot[None, :] == jnp.arange(slots, dtype=jnp.int32)[:, None]
    found = jnp.max(jnp.where(match, wet_row[None, :] + 1, 0), axis=1)
    return jnp.where(found > 0, found - 1, tiles)


def to_bulk(field):
    return field.transpose(1, 2, 0, 3)


def to_edge(sz, row):
    split = row.reshape(LEVELS, CHANNELS, sz.row_tiles, WIDTH).transpose(1, 2, 0, 3)
    return split.reshape(sz.edge_rows, WIDTH)


def to_surface(sz, rows):
    split = rows.reshape(sz.rows, CHANNELS, sz.row_tiles, WIDTH).transpose(0, 2, 1, 3)
    return split.reshape(CHANNELS * sz.tiles, WIDTH)


def swap(low, high):
    count = lax.axis_size("horiz")
    upward = [(i, i + 1) for i in range(count - 1)]
    downward = [(target, source) for source, target in upward]
    return lax.ppermute(high, "horiz", upward), lax.ppermute(low, "horiz", downward)


def exchange(array, devices):
    rows = array.shape[0] // devices
    split = array.reshape(devices, rows // CHANNELS, CHANNELS, WIDTH)
    moved = lax.all_to_all(split, "horiz", split_axis=0, concat_axis=0, tiled=True)
    return moved.reshape(array.shape)


def body(
    perturbation,
    base_state,
    target_state,
    cost_weight,
    diffusivity,
    chan_mix,
    coupler_mix,
    owner_mix,
    air_temp,
    wind_speed,
    wet_list,
    wet_owner,
    remap_src,
    remap_tgt,
    remap_weight,
):
    devices = lax.axis_size("horiz")
    hours = air_temp.shape[0]
    sz = Sizes(devices, air_temp.shape[2] // devices, base_state.shape[1], base_state.shape[3])
    me = lax.axis_index("horiz")
    mixing = owner_mix[0]
    rows = sz.rows

    tile_of = slot_tiles(wet_list[0], wet_owner[0], sz.capacity, sz.slots, sz.tiles)
    row_of = jnp.where(
        tile_of < sz.tiles,
        (tile_of // sz.row_tiles) * sz.pitch + tile_of % sz.row_tiles,
        sz.flat_rows,
    )
    lat_hit = (
        remap_tgt[None, :] - (me * LAT_DEV - 1) == jnp.arange(NEAR_LAT, dtype=jnp.int32)[:, None]
    )
    row_hit = remap_src[None, :] - me * rows == jnp.arange(rows, dtype=jnp.int32)[:, None]
    own_remap = jnp.sum(
        jnp.where(lat_hit[:, None, :] & row_hit[None, :, :], remap_weight[None, None, :], 0.0),
        axis=2,
    )
    facts = jnp.concatenate(
        [(sz.flat_rows - row_of).astype(jnp.float32), own_remap.reshape(-1)]
    )
    fact_rows = -(-facts.shape[0] // (WIDTH * SUBLANES)) * SUBLANES
    facts = jnp.pad(facts, (0, fact_rows * WIDTH - facts.shape[0])).reshape(fact_rows, WIDTH)

    start = [perturbation[:, row] + base_state[:, row] for row in (0, rows - 1)]
    sends = [jnp.concatenate([to_edge(sz, one), facts]) for one in start]
    from_low, from_high = swap(*sends)

    def facts_of(got):
        line = got[sz.edge_rows :].reshape(-1)
        table = sz.flat_rows - line[: sz.slots].astype(jnp.int32)
        return table, line[sz.slots : sz.slots + NEAR_LAT * rows].reshape(NEAR_LAT, rows)

    low_table, low_remap = facts_of(from_low)
    high_table, high_remap = facts_of(from_high)
    tables = jnp.stack([tile_of, low_table, high_table])
    blank = jnp.zeros((LAT_DEV, rows), jnp.float32)
    remap = jnp.concatenate(
        [
            jnp.concatenate([low_remap[LAT_DEV:], blank]),
            own_remap,
            jnp.concatenate([blank, high_remap[:LAT_DEV]]),
        ],
        axis=1,
    )
    mix = jnp.broadcast_to(
        chan_mix.transpose(1, 2, 0).reshape(CHANNELS * CHANNELS, LEVELS, 1),
        (CHANNELS * CHANNELS, LEVELS, WIDTH),
    )
    weight_sq = cost_weight * cost_weight
    start_pert = to_bulk(perturbation)
    field = start_pert + to_bulk(base_state)
    target = to_bulk(target_state)
    target_surface = to_surface(sz, target_state[0])

    def all_channels(array):
        return to_surface(sz, jnp.broadcast_to(array[:, None, :], (rows, CHANNELS, sz.cells)))

    weight_surface = all_channels(weight_sq)
    diffusivity_surface = all_channels(diffusivity)
    diffusivity = diffusivity.reshape(rows, 1, sz.cells)
    weight_sq = weight_sq.reshape(rows, 1, sz.cells)

    whole = (rows, CHANNELS, LEVELS, sz.cells)
    wider = (rows + 2, CHANNELS, LEVELS, sz.cells)
    surface_shape = (sz.surface_rows, WIDTH)
    narrow = (CHANNELS * sz.slots, WIDTH)
    wide = (devices * sz.chunk, WIDTH)
    slope_shape = (NEAR_LAT * sz.pitch, WIDTH)
    near = (sz.flat_rows + SUBLANES, WIDTH)
    lats = (LAT_DEV * sz.pitch, WIDTH)
    row_surface = (CHANNELS * sz.row_tiles, WIDTH)
    by_slot = (CHANNELS, sz.slots, WIDTH)

    saved = []
    edges = (from_low, from_high)
    surface = None
    for hour in range(hours):
        first, last = hour == 0, hour == hours - 1
        inputs = big(field, *edges, diffusivity, mix) + small(tile_of)
        if not first:
            inputs += big(surface, *surface_edges)
        if last:
            inputs += big(target, weight_sq)
        edge_send = (sz.edge_rows + sz.flat_rows + SUBLANES, WIDTH)
        field, drive, surface, packed, *sends = call(
            functools.partial(forward_kernel, sz, first, last),
            "step",
            inputs,
            [whole, whole, surface_shape, narrow, edge_send, edge_send],
            [wider],
        )
        arrived = exchange(packed, devices)
        edges = swap(*sends)
        flux, mixed_slope, flux_slope = call(
            functools.partial(owner_kernel, sz),
            "owners",
            big(arrived, mixing, air_temp[hour, 0], wind_speed[hour, 0]) + small(coupler_mix),
            [wide, by_slot, by_slot],
            [narrow, (sz.slots, WIDTH)],
        )
        flux = exchange(flux, devices)
        inputs = big(flux, surface, *edges) + small(tables, remap)
        if last:
            surface, slope, packed, *sends = call(
                functools.partial(surface_kernel, sz, True),
                "surface",
                inputs + big(target_surface, weight_surface),
                [surface_shape, slope_shape, wide, lats, lats],
                [near, near],
            )
        else:
            surface, slope, *sends = call(
                functools.partial(surface_kernel, sz, False),
                "surface",
                inputs,
                [surface_shape, slope_shape, row_surface, row_surface],
                [near, near],
            )
            surface_edges = swap(*sends)
        saved.append((drive, slope, mixed_slope, flux_slope))

    lat_at = 0
    for hour in reversed(range(hours)):
        drive, slope, mixed_slope, flux_slope = saved[hour]
        arrived = exchange(packed, devices)
        got = swap(*sends)
        back = call(
            functools.partial(owner_back_kernel, sz),
            "owners_back",
            big(arrived, mixing, mixed_slope, flux_slope) + small(coupler_mix),
            [narrow],
            [narrow, (sz.slots, WIDTH)],
        )[0]
        back = exchange(back, devices)
        if hour < hours - 1:
            edges = got
        surface, *row_sends = call(
            functools.partial(merge_kernel, sz, lat_at),
            "merge",
            big(back, surface, slope, *got) + small(tables, remap) + big(diffusivity_surface),
            [surface_shape, row_surface, row_surface],
        )
        surface_edges = swap(*row_sends)
        inputs = big(field, surface, *edges, *surface_edges, drive, diffusivity, mix)
        if hour > 0:
            lat_at = sz.edge_rows
            edge_send = (sz.edge_rows + lats[0], WIDTH)
            field, surface, packed, *sends = call(
                functools.partial(backward_kernel, sz, False),
                "step_back",
                inputs + small(tables, remap) + big(saved[hour - 1][1]),
                [whole, surface_shape, wide, edge_send, edge_send],
                [whole, wider, near, near],
            )
        else:
            gradient, sums = call(
                functools.partial(backward_kernel, sz, True),
                "step_back_sums",
                inputs + big(start_pert),
                [whole, (LEVELS, WIDTH)],
                [whole, wider],
            )

    local = jnp.pad(jnp.sum(sums, axis=1), (0, WIDTH - LEVELS))
    everyones = lax.all_to_all(
        jnp.broadcast_to(local, (devices, WIDTH)), "horiz", split_axis=0, concat_axis=0, tiled=True
    )
    cell_total = perturbation.size * devices
    statistics = jnp.sum(everyones, axis=0) / cell_total
    mean_pp, mean_pg, mean_gg = statistics[0], statistics[1], statistics[2]
    grad_scale = lax.rsqrt(mean_gg + EPSILON)
    mean_sq = (
        mean_pp
        + 2.0 * ASCENT * grad_scale * mean_pg
        + ASCENT * ASCENT * grad_scale * grad_scale * mean_gg
    )
    stepped = perturbation + ASCENT * grad_scale * gradient.transpose(2, 0, 1, 3)
    return stepped * lax.rsqrt(mean_sq + EPSILON)


def solution(mesh):
    placed = (
        P("member", "horiz", None, None),
        P(None, "horiz", None, None),
        P(None, "horiz", None, None),
        P("horiz", None),
        P("horiz", None),
        P(),
        P(),
        P("horiz", None, None),
        P(None, "horiz", None, None),
        P(None, "horiz", None, None),
        P("horiz", None),
        P("horiz", None),
        P("horiz"),
        P("horiz"),
        P("horiz"),
    )
    return jax.shard_map(
        body,
        mesh=mesh,
        in_specs=placed,
        out_specs=P("member", "horiz", None, None),
        check_vma=False,
    )
```

time: 297 us -> 208 us (0.70)
  blocking collectives: 105 us -> 65.6 us
  matrix products: 19.5 us -> 0 us
  local copies, waits for them, and re-layouts: 39.3 us -> 20 us
  Pallas kernels: 0 us -> 18.8 us
  starting transfers between devices: 69.8 us -> 56.7 us
  other arithmetic: 20.9 us -> 9.93 us
  waiting for transfers between devices: 36.9 us -> 32.3 us
    psum x1 -> x0, blocking collectives: 31.9 us -> none  [body(): lax.psum((jnp.sum(perturbation * perturbation), jnp.sum(perturbation * ad...]
    ppermute x24 -> x16, starting transfers between devices: 54.8 us -> 31.2 us  [the longest x8 20.6 us: swap(): lax.ppermute(high, 'horiz', upward)]
    dot_general x32 -> x0, matrix products: 19.5 us -> none  [the longest x2 5.63 us: channel_drive(): jnp.einsum('lck,ljkx->ljcx', chan_mix, ocean_field, precision=HIGHEST)]
    pallas_call x0 -> x12, Pallas kernels: none -> 18.8 us  [call(): pl.pallas_call(kernel, name=name, in_specs=[spec(pltpu.SMEM if small else...]
    scatter-add x16 -> x0, local copies, waits for them, and re-layouts: 14.9 us -> none  [the longest x2 6.07 us: body(): ocean_field = ocean_field.at[0].add(from_tiles(flux_tiles, row_count))]
    unnamed x102 -> x68, local copies, waits for them, and re-layouts: 2.25 us -> 13.3 us
    all_to_all x3 -> x5, starting transfers between devices: 15 us -> 25.6 us  [exchange(): lax.all_to_all(split, 'horiz', split_axis=0, concat_axis=0, tiled=True)]
    gather x12 -> x0, local copies, waits for them, and re-layouts: 9.44 us -> none  [the longest x4 3.06 us: owner_round(): flattened[jnp.maximum(slot_index, 0)]]
  transfers between devices with their start and end apart: 27 -> 21, of which waited for: 9 -> 12; matrix products, arithmetic and copies ran while one was open for 7% -> 4% of each run, Pallas kernels for 0% -> 0%
where the time goes in v1:
time: 208 us; the launch traced here: 207 us
  blocking collectives  65.6 us (32%)
  starting transfers between devices  56.7 us (27%)
  waiting for transfers between devices  32.3 us (16%)
  local copies, waits for them, and re-layouts  20 us (10%)
  Pallas kernels  18.8 us (9%)
  other arithmetic  9.93 us (5%)
  between operations  3.26 us (2%)
    all_to_all x3, blocking collectives, exchange(): lax.all_to_all(split, 'horiz', split_axis=0, concat_axis=0, tiled=True)  51.2 us
    all_to_all x5, starting transfers between devices, exchange(): lax.all_to_all(split, 'horiz', split_axis=0, concat_axis=0, tiled=True)  25.6 us
    ppermute x8, starting transfers between devices, swap(): lax.ppermute(high, 'horiz', upward)  20.6 us
    pallas_call x12, Pallas kernels, call(): pl.pallas_call(kernel, name=name, in_specs=[spec(pltpu.SMEM if small else...  18.8 us
    all_to_all x5, waiting for transfers between devices, exchange(): lax.all_to_all(split, 'horiz', split_axis=0, concat_axis=0, tiled=True)  16.2 us
    ppermute x8, waiting for transfers between devices, swap(): lax.ppermute(low, 'horiz', downward)  16 us
    all_to_all x1, blocking collectives, body(): lax.all_to_all(jnp.broadcast_to(local, (devices, WIDTH)), 'horiz', split_...  14.5 us
    unnamed x68, local copies, waits for them, and re-layouts  13.3 us
  transfers between devices with their start and end apart: 21, of which 12 were waited for; matrix products, arithmetic and copies ran while one was open for 4% of the time, Pallas kernels for 0%

profile of v1, /device:TPU:0, one launch (start us, length us, event | category | flops | bytes accessed | tf_op | source)
XLA Modules:
  0.0 206.6 jit_solution(9949427908169945213)
XLA Ops:
  1.3 0.7 select_reduce_fusion.1
  2.3 0.9 convert_reduce_fusion
  4.0 1.4 slice_add_fusion
  6.2 2.5 %collective-permute-start = (f32[488,128]{1,0:T(8,128)S(1)}, f32[488,128]{1,0:T(8,128)S(1)}, u32[]{:S(2)}, u32[]{:S(2)}) collective-permute-start(f32[488,128]{1,0:T(8,128)S(1)} %get-tuple-element.94), channel_id=1, source_target_pairs={{0,1},{1,2},{2,3},{3,4},{4,5},{5,6},{6,7},{7,8},{8,9},{9,10},{10,1... | collective-permute-start | bytes 749576 | tf_op jit(solution)/shard_map/ppermute | solution.py:507
  8.7 1.4 collective-permute-start.1
  10.5 3.9 %collective-permute-done.1.refs_2_ = f32[488,128]{1,0:T(8,128)S(1)} collective-permute-done((f32[488,128]{1,0:T(8,128)S(1)}, f32[488,128]{1,0:T(8,128)S(1)}, u32[]{:S(2)}, u32[]{:S(2)}) %collective-permute-start.1) | collective-permute-done | bytes 249888 | tf_op jit(solution)/shard_map/ppermute | solution.py:507
  14.5 2.7 %step.2 = (f32[5,4,8,1920]{3,2,1,0:T(8,128)S(1)}, f32[5,4,8,1920]{3,2,1,0:T(8,128)S(1)}, f32[304,128]{1,0:T(8,128)S(1)}, f32[320,128]{1,0:T(8,128)}, f32[568,128]{1,0:T(8,128)S(1)}, /*index=5*/f32[568,128]{1,0:T(8,128)S(1)}) custom-call(f32[5,4,8,1920]{3,2,1,0:T(8,128)S(1)} %bitcast_add_fusion.1.refs_0_, f32[488,128]{1,0:T(8,128)S(1)} %collective-permute-done.refs_1_, ...), custom_call_target="tpu_custom_call" | custom-call | tf_op jit(solution)/shard_map/step/pallas_call | solution.py:459
  17.9 0.7 copy-done.20
  19.3 10.1 %all-to-all-start = ((f32[16,5,4,128]{3,2,1,0:T(4,128)}), f32[16,5,4,128]{3,2,1,0:T(4,128)S(1)}, u32[]{:S(2)}, u32[]{:S(2)}) async-start(f32[16,5,4,128]{3,2,1,0:T(4,128)} %bitcast.15), calls=%async_computation | async-start | bytes 327680 | tf_op jit(solution)/shard_map/all_to_all | solution.py:513
  29.4 2.3 %collective-permute-start.2 = (f32[568,128]{1,0:T(8,128)}, f32[568,128]{1,0:T(8,128)S(1)}, u32[]{:S(2)}, u32[]{:S(2)}) collective-permute-start(f32[568,128]{1,0:T(8,128)} %copy-done.21), channel_id=1, source_target_pairs={{0,1},{1,2},{2,3},{3,4},{4,5},{5,6},{6,7},{7,8},{8,9},{9,10},{10,1... | collective-permute-start | bytes 872456 | tf_op jit(solution)/shard_map/ppermute | solution.py:507
  31.7 1.3 collective-permute-start.3
  34.8 3.0 %all-to-all-done = f32[16,5,4,128]{3,2,1,0:T(4,128)S(1)} async-done(((f32[16,5,4,128]{3,2,1,0:T(4,128)}), f32[16,5,4,128]{3,2,1,0:T(4,128)S(1)}, u32[]{:S(2)}, u32[]{:S(2)}) %all-to-all-start) | async-done | bytes 163872 | tf_op jit(solution)/shard_map/all_to_all | solution.py:513
  37.9 1.0 owners.2
  38.8 0.7 copy-done.8
  40.9 4.9 %all-to-all-start.1 = ((f32[16,8,4,128]{3,2,1,0:T(4,128)}), f32[16,8,4,128]{3,2,1,0:T(4,128)S(1)}, u32[]{:S(2)}, u32[]{:S(2)}) async-start(f32[16,8,4,128]{3,2,1,0:T(4,128)} %bitcast.87), calls=%async_computation.1 | async-start | bytes 524288 | tf_op jit(solution)/shard_map/all_to_all | solution.py:513
  46.7 1.3 slice.81
  47.9 0.8 select_maximum_fusion.1.refs_5_.remap.refs_10_
  49.3 6.5 %all-to-all-done.1 = f32[16,8,4,128]{3,2,1,0:T(4,128)S(1)} async-done(((f32[16,8,4,128]{3,2,1,0:T(4,128)}), f32[16,8,4,128]{3,2,1,0:T(4,128)S(1)}, u32[]{:S(2)}, u32[]{:S(2)}) %all-to-all-start.1) | async-done | bytes 262176 | tf_op jit(solution)/shard_map/all_to_all | solution.py:513
  55.9 0.9 copy-done.16
  56.8 0.9 surface.2
  57.7 1.8 collective-permute-start.4
  59.4 1.3 collective-permute-start.5
  60.7 0.9 mul.52
  61.8 0.7 collective-permute-done.5.refs_8_
  62.5 2.3 %step.3 = (f32[5,4,8,1920]{3,2,1,0:T(8,128)S(1)}, f32[5,4,8,1920]{3,2,1,0:T(8,128)S(1)}, f32[304,128]{1,0:T(8,128)S(1)}, f32[320,128]{1,0:T(8,128)S(1)}, f32[568,128]{1,0:T(8,128)S(1)}, /*index=5*/f32[568,128]{1,0:T(8,128)S(1)}) custom-call(f32[5,4,8,1920]{3,2,1,0:T(8,128)S(1)} %get-tuple-element.45.refs_0_, ...), custom_call_target="tpu_custom_call" | custom-call | tf_op jit(solution)/shard_map/step/pallas_call | solution.py:459
  64.9 1.0 copy-done
  65.9 1.1 copy-done.2
  67.0 15.2 %all_to_all.46 = f32[16,5,4,128]{3,2,1,0:T(4,128)S(1)} all-to-all(f32[16,5,4,128]{3,2,1,0:T(4,128)S(1)} %bitcast.90), channel_id=1, replica_groups=mesh['member'=2,'horiz'=16] {'horiz'}, dimensions={0} | all-to-all | bytes 327680 | tf_op jit(solution)/shard_map/all_to_all | solution.py:513
  82.1 1.7 owners.3
  83.8 3.5 %all-to-all-start.3 = ((f32[16,8,4,128]{3,2,1,0:T(4,128)}), f32[16,8,4,128]{3,2,1,0:T(4,128)S(1)}, u32[]{:S(2)}, u32[]{:S(2)}) async-start(f32[16,8,4,128]{3,2,1,0:T(4,128)} %bitcast.32), calls=%async_computation.3 | async-start | bytes 524288 | tf_op jit(solution)/shard_map/all_to_all | solution.py:513
  87.4 2.2 %collective-permute-start.6 = (f32[568,128]{1,0:T(8,128)}, f32[568,128]{1,0:T(8,128)S(1)}, u32[]{:S(2)}, u32[]{:S(2)}) collective-permute-start(f32[568,128]{1,0:T(8,128)} %copy-done.23), channel_id=1, source_target_pairs={{0,1},{1,2},{2,3},{3,4},{4,5},{5,6},{6,7},{7,8},{8,9},{9,10},{10,1... | collective-permute-start | bytes 872456 | tf_op jit(solution)/shard_map/ppermute | solution.py:507
  89.6 1.3 collective-permute-start.7
  91.2 3.1 %collective-permute-done.7.refs_3_ = f32[568,128]{1,0:T(8,128)S(1)} collective-permute-done((f32[568,128]{1,0:T(8,128)}, f32[568,128]{1,0:T(8,128)S(1)}, u32[]{:S(2)}, u32[]{:S(2)}) %collective-permute-start.7) | collective-permute-done | bytes 290848 | tf_op jit(solution)/shard_map/ppermute | solution.py:507
  94.4 3.0 %all-to-all-done.3 = f32[16,8,4,128]{3,2,1,0:T(4,128)S(1)} async-done(((f32[16,8,4,128]{3,2,1,0:T(4,128)}), f32[16,8,4,128]{3,2,1,0:T(4,128)S(1)}, u32[]{:S(2)}, u32[]{:S(2)}) %all-to-all-start.3) | async-done | bytes 262176 | tf_op jit(solution)/shard_map/all_to_all | solution.py:513
  97.4 1.1 surface.3
  98.5 17.9 %all_to_all.47 = f32[16,8,4,128]{3,2,1,0:T(4,128)S(1)} all-to-all(f32[16,8,4,128]{3,2,1,0:T(4,128)S(1)} %bitcast.89), channel_id=1, replica_groups=mesh['member'=2,'horiz'=16] {'horiz'}, dimensions={0} | all-to-all | bytes 524288 | tf_op jit(solution)/shard_map/all_to_all | solution.py:513
  116.4 1.6 owners_back.2
  118.0 3.5 %all-to-all-start.5 = ((f32[16,5,4,128]{3,2,1,0:T(4,128)}), f32[16,5,4,128]{3,2,1,0:T(4,128)S(1)}, u32[]{:S(2)}, u32[]{:S(2)}) async-start(f32[16,5,4,128]{3,2,1,0:T(4,128)} %bitcast.37), calls=%async_computation.5 | async-start | bytes 327680 | tf_op jit(solution)/shard_map/all_to_all | solution.py:513
  121.5 2.2 %collective-permute-start.8 = (f32[32,128]{1,0:T(8,128)S(1)}, f32[32,128]{1,0:T(8,128)S(1)}, u32[]{:S(2)}, u32[]{:S(2)}) collective-permute-start(f32[32,128]{1,0:T(8,128)S(1)} %get-tuple-element.65), channel_id=1, source_target_pairs={{0,1},{1,2},{2,3},{3,4},{4,5},{5,6},{6,7},{7,8},{8,9},{9,10},{10,1... | collective-permute-start | bytes 49160 | tf_op jit(solution)/shard_map/ppermute | solution.py:507
  123.7 1.3 collective-permute-start.9
  125.2 2.8 %collective-permute-done.9.from_high = f32[32,128]{1,0:T(8,128)S(1)} collective-permute-done((f32[32,128]{1,0:T(8,128)S(1)}, f32[32,128]{1,0:T(8,128)S(1)}, u32[]{:S(2)}, u32[]{:S(2)}) %collective-permute-start.9) | collective-permute-done | bytes 16416 | tf_op jit(solution)/shard_map/ppermute | solution.py:507
  127.9 2.0 all-to-all-done.5
  130.7 2.4 %collective-permute-start.10 = (f32[60,128]{1,0:T(8,128)S(1)}, f32[60,128]{1,0:T(8,128)S(1)}, u32[]{:S(2)}, u32[]{:S(2)}) collective-permute-start(f32[60,128]{1,0:T(8,128)S(1)} %get-tuple-element.68), channel_id=1, source_target_pairs={{0,1},{1,2},{2,3},{3,4},{4,5},{5,6},{6,7},{7,8},{8,9},{9,10},{10,1... | collective-permute-start | bytes 92168 | tf_op jit(solution)/shard_map/ppermute | solution.py:507
  133.0 1.3 collective-permute-start.11
  134.3 1.8 collective-permute-done.11.refs_5_
  136.1 1.3 copy-done.1
  137.4 1.3 copy-done.3
  138.7 2.5 %step_back.1 = (f32[5,4,8,1920]{3,2,1,0:T(8,128)S(1)}, f32[304,128]{1,0:T(8,128)S(1)}, f32[512,128]{1,0:T(8,128)S(1)}, f32[512,128]{1,0:T(8,128)S(1)}, f32[512,128]{1,0:T(8,128)S(1)}) custom-call(f32[5,4,8,1920]{3,2,1,0:T(8,128)S(1)} %copy-done.1, f32[304,128]{1,0:T(8,128)S(1)} %get-tuple-element.67.refs_1_, f32[568,128]{1,0:T(8,128)S(1)} %collective-permute-done.6.refs_2_, ...), custom_call_target="tpu_custom_call" | custom-call | tf_op jit(solution)/shard_map/step_back/pallas_call | solution.py:459
  141.3 1.0 copy-done.4
  142.3 18.1 %all_to_all.48 = f32[16,8,4,128]{3,2,1,0:T(4,128)S(1)} all-to-all(f32[16,8,4,128]{3,2,1,0:T(4,128)S(1)} %bitcast.88), channel_id=1, replica_groups=mesh['member'=2,'horiz'=16] {'horiz'}, dimensions={0} | all-to-all | bytes 524288 | tf_op jit(solution)/shard_map/all_to_all | solution.py:513
  160.4 1.6 owners_back.3
  162.0 3.5 %all-to-all-start.7 = ((f32[16,5,4,128]{3,2,1,0:T(4,128)}), f32[16,5,4,128]{3,2,1,0:T(4,128)S(1)}, u32[]{:S(2)}, u32[]{:S(2)}) async-start(f32[16,5,4,128]{3,2,1,0:T(4,128)} %bitcast.41), calls=%async_computation.7 | async-start | bytes 327680 | tf_op jit(solution)/shard_map/all_to_all | solution.py:513
  165.5 2.2 %collective-permute-start.12 = (f32[512,128]{1,0:T(8,128)S(1)}, f32[512,128]{1,0:T(8,128)S(1)}, u32[]{:S(2)}, u32[]{:S(2)}) collective-permute-start(f32[512,128]{1,0:T(8,128)S(1)} %get-tuple-element.77), channel_id=1, source_target_pairs={{0,1},{1,2},{2,3},{3,4},{4,5},{5,6},{6,7},{7,8},{8,9},{9,10},{10,1... | collective-permute-start | bytes 786440 | tf_op jit(solution)/shard_map/ppermute | solution.py:507
  167.7 1.3 collective-permute-start.13
  169.0 3.2 %collective-permute-done.13.from_high.refs_3_ = f32[512,128]{1,0:T(8,128)S(1)} collective-permute-done((f32[512,128]{1,0:T(8,128)S(1)}, f32[512,128]{1,0:T(8,128)S(1)}, u32[]{:S(2)}, u32[]{:S(2)}) %collective-permute-start.13) | collective-permute-done | bytes 262176 | tf_op jit(solution)/shard_map/ppermute | solution.py:507
  172.3 1.7 all-to-all-done.7
  174.7 5.0 %collective-permute-start.14 = (f32[60,128]{1,0:T(8,128)S(1)}, f32[60,128]{1,0:T(8,128)S(1)}, u32[]{:S(2)}, u32[]{:S(2)}) collective-permute-start(f32[60,128]{1,0:T(8,128)S(1)} %get-tuple-element.80), channel_id=1, source_target_pairs={{0,1},{1,2},{2,3},{3,4},{4,5},{5,6},{6,7},{7,8},{8,9},{9,10},{10,1... | collective-permute-start | bytes 92168 | tf_op jit(solution)/shard_map/ppermute | solution.py:507
  179.7 1.4 collective-permute-start.15
  181.1 1.4 copy.70
  182.9 2.0 step_back_sums.1
  184.9 1.0 copy-done.6
  186.1 14.5 %all_to_all.49 = f32[16,1,128]{2,1,0:T(1,128)S(1)} all-to-all(f32[16,1,128]{2,1,0:T(1,128)S(1)} %broadcast_in_dim.79), channel_id=1, replica_groups=mesh['member'=2,'horiz'=16] {'horiz'}, dimensions={0} | all-to-all | bytes 16384 | tf_op jit(solution)/shard_map/all_to_all | solution.py:702
  203.8 1.4 fusion
  205.3 1.3 copy.58
  (115 shorter events, 12.6 us)
Async XLA Ops:
  5.6 4.6 %copy-start.24 = (f32[8,5,4,1920]{3,2,1,0:T(4,128)S(1)}, f32[8,5,4,1920]{3,2,1,0:T(4,128)}, u32[]{:S(2)}) copy-start(f32[8,5,4,1920]{3,2,1,0:T(4,128)} %param.15) | copy-start | bytes 3686404
  5.6 4.6 %copy-start.26 = (f32[8,5,4,1920]{3,2,1,0:T(4,128)S(1)}, f32[8,5,4,1920]{3,2,1,0:T(4,128)}, u32[]{:S(2)}) copy-start(f32[8,5,4,1920]{3,2,1,0:T(4,128)} %param.16) | copy-start | bytes 3686404
  6.2 4.3 %collective-permute-start = (f32[488,128]{1,0:T(8,128)S(1)}, f32[488,128]{1,0:T(8,128)S(1)}, u32[]{:S(2)}, u32[]{:S(2)}) collective-permute-start(f32[488,128]{1,0:T(8,128)S(1)} %get-tuple-element.94), channel_id=1, source_target_pairs={{0,1},{1,2},{2,3},{3,4},{4,5},{5,6},{6,7},{7,8},{8,9},{9,10},{10,1... | collective-permute-start | bytes 749576 | tf_op jit(solution)/shard_map/ppermute | solution.py:507
  8.7 1.7 copy-start.28
  8.7 1.7 copy-start.30
  8.7 1.7 copy-start.31
  8.7 5.7 %copy-start.32 = (f32[8,4,4]{0,2,1:T(4,128)S(1)}, f32[8,4,4]{0,2,1:T(4,128)}, u32[]{:S(2)}) copy-start(f32[8,4,4]{0,2,1:T(4,128)} %param.20) | copy-start | bytes 1540
  8.7 5.7 %collective-permute-start.1 = (f32[488,128]{1,0:T(8,128)S(1)}, f32[488,128]{1,0:T(8,128)S(1)}, u32[]{:S(2)}, u32[]{:S(2)}) collective-permute-start(f32[488,128]{1,0:T(8,128)S(1)} %get-tuple-element.93), channel_id=1, source_target_pairs={{1,0},{2,1},{3,2},{4,3},{5,4},{6,5},{7,6},{8,7},{9,8},{10,9},{11,1... | collective-permute-start | bytes 749576 | tf_op jit(solution)/shard_map/ppermute | solution.py:507
  10.4 27.5 %copy-start.7 = (f32[1,80,80]{2,1,0:T(8,128)S(1)}, f32[1,80,80]{2,1,0:T(8,128)}, u32[]{:S(2)}) copy-start(f32[1,80,80]{2,1,0:T(8,128)} %param.22) | copy-start | bytes 76804
  10.4 27.5 %copy-start.19 = (f32[4,4]{1,0:T(4,128)S(1)}, f32[4,4]{1,0:T(4,128)}, u32[]{:S(2)}) copy-start(f32[4,4]{1,0:T(4,128)} %bulk.7) | copy-start | bytes 196
  10.4 6.7 %copy-start.9 = (f32[488,128]{1,0:T(8,128)}, f32[488,128]{1,0:T(8,128)S(1)}, u32[]{:S(2)}) copy-start(f32[488,128]{1,0:T(8,128)S(1)} %collective-permute-done.refs_1_) | copy-start | bytes 749572
  14.4 4.9 %copy-start.10 = (f32[488,128]{1,0:T(8,128)}, f32[488,128]{1,0:T(8,128)S(1)}, u32[]{:S(2)}) copy-start(f32[488,128]{1,0:T(8,128)S(1)} %collective-permute-done.1.refs_2_) | copy-start | bytes 749572
  17.2 0.7 copy-start.15
  17.9 0.7 copy-start.20
  18.6 0.7 copy-start.21
  19.3 18.5 %all-to-all-start = ((f32[16,5,4,128]{3,2,1,0:T(4,128)}), f32[16,5,4,128]{3,2,1,0:T(4,128)S(1)}, u32[]{:S(2)}, u32[]{:S(2)}) async-start(f32[16,5,4,128]{3,2,1,0:T(4,128)} %bitcast.15), calls=%async_computation | async-start | bytes 327680 | tf_op jit(solution)/shard_map/all_to_all | solution.py:513
  29.4 19.9 %collective-permute-start.2 = (f32[568,128]{1,0:T(8,128)}, f32[568,128]{1,0:T(8,128)S(1)}, u32[]{:S(2)}, u32[]{:S(2)}) collective-permute-start(f32[568,128]{1,0:T(8,128)} %copy-done.21), channel_id=1, source_target_pairs={{0,1},{1,2},{2,3},{3,4},{4,5},{5,6},{6,7},{7,8},{8,9},{9,10},{10,1... | collective-permute-start | bytes 872456 | tf_op jit(solution)/shard_map/ppermute | solution.py:507
  31.7 17.6 %collective-permute-start.3 = (f32[568,128]{1,0:T(8,128)}, f32[568,128]{1,0:T(8,128)S(1)}, u32[]{:S(2)}, u32[]{:S(2)}) collective-permute-start(f32[568,128]{1,0:T(8,128)} %copy-done.20), channel_id=1, source_target_pairs={{1,0},{2,1},{3,2},{4,3},{5,4},{6,5},{7,6},{8,7},{9,8},{10,9},{11,1... | collective-permute-start | bytes 872456 | tf_op jit(solution)/shard_map/ppermute | solution.py:507
  38.8 0.7 copy-start.8
  39.6 0.7 copy-start.11
  40.2 0.7 copy-start.13
  40.9 15.0 %all-to-all-start.1 = ((f32[16,8,4,128]{3,2,1,0:T(4,128)}), f32[16,8,4,128]{3,2,1,0:T(4,128)S(1)}, u32[]{:S(2)}, u32[]{:S(2)}) async-start(f32[16,8,4,128]{3,2,1,0:T(4,128)} %bitcast.87), calls=%async_computation.1 | async-start | bytes 524288 | tf_op jit(solution)/shard_map/all_to_all | solution.py:513
  55.9 0.9 copy-start.16
  56.8 4.9 %copy-start.27 = (f32[8,5,4,1920]{3,2,1,0:T(4,128)S(1)}, f32[8,5,4,1920]{3,2,1,0:T(4,128)}, u32[]{:S(2)}) copy-start(f32[8,5,4,1920]{3,2,1,0:T(4,128)} %param.17) | copy-start | bytes 3686404
  57.7 4.0 %copy-start.17 = (f32[64,128]{1,0:T(8,128)}, f32[64,128]{1,0:T(8,128)S(1)}, u32[]{:S(2)}) copy-start(f32[64,128]{1,0:T(8,128)S(1)} %get-tuple-element.71.refs_11_.slope) | copy-start | bytes 98308
  57.7 4.1 %collective-permute-start.4 = (f32[60,128]{1,0:T(8,128)S(1)}, f32[60,128]{1,0:T(8,128)S(1)}, u32[]{:S(2)}, u32[]{:S(2)}) collective-permute-start(f32[60,128]{1,0:T(8,128)S(1)} %get-tuple-element.52), channel_id=1, source_target_pairs={{0,1},{1,2},{2,3},{3,4},{4,5},{5,6},{6,7},{7,8},{8,9},{9,10},{10,1... | collective-permute-start | bytes 92168 | tf_op jit(solution)/shard_map/ppermute | solution.py:507
  59.4 3.1 %collective-permute-start.5 = (f32[60,128]{1,0:T(8,128)S(1)}, f32[60,128]{1,0:T(8,128)S(1)}, u32[]{:S(2)}, u32[]{:S(2)}) collective-permute-start(f32[60,128]{1,0:T(8,128)S(1)} %get-tuple-element.53), channel_id=1, source_target_pairs={{1,0},{2,1},{3,2},{4,3},{5,4},{6,5},{7,6},{8,7},{9,8},{10,9},{11,1... | collective-permute-start | bytes 92168 | tf_op jit(solution)/shard_map/ppermute | solution.py:507
  64.9 1.0 copy-start
  65.9 1.1 copy-start.2
  66.9 16.9 %copy-start.22 = (f32[568,128]{1,0:T(8,128)}, f32[568,128]{1,0:T(8,128)S(1)}, u32[]{:S(2)}) copy-start(f32[568,128]{1,0:T(8,128)S(1)} %get-tuple-element.59) | copy-start | bytes 872452
  66.9 16.9 %copy-start.23 = (f32[568,128]{1,0:T(8,128)}, f32[568,128]{1,0:T(8,128)S(1)}, u32[]{:S(2)}) copy-start(f32[568,128]{1,0:T(8,128)S(1)} %get-tuple-element.58) | copy-start | bytes 872452
  67.0 24.0 %slice-start = ((f32[8,5,4,1920]{3,2,1,0:T(4,128)}), f32[1,5,4,1920]{3,2,1,0:T(4,128)S(1)}, s32[]{:S(2)}) async-start(f32[8,5,4,1920]{3,2,1,0:T(4,128)} %param.17), calls=%async_computation.9 | async-start | bytes 307200 | tf_op jit(solution)/shard_map/slice | solution.py:590
  83.8 13.6 %all-to-all-start.3 = ((f32[16,8,4,128]{3,2,1,0:T(4,128)}), f32[16,8,4,128]{3,2,1,0:T(4,128)S(1)}, u32[]{:S(2)}, u32[]{:S(2)}) async-start(f32[16,8,4,128]{3,2,1,0:T(4,128)} %bitcast.32), calls=%async_computation.3 | async-start | bytes 524288 | tf_op jit(solution)/shard_map/all_to_all | solution.py:513
  87.4 3.9 %collective-permute-start.6 = (f32[568,128]{1,0:T(8,128)}, f32[568,128]{1,0:T(8,128)S(1)}, u32[]{:S(2)}, u32[]{:S(2)}) collective-permute-start(f32[568,128]{1,0:T(8,128)} %copy-done.23), channel_id=1, source_target_pairs={{0,1},{1,2},{2,3},{3,4},{4,5},{5,6},{6,7},{7,8},{8,9},{9,10},{10,1... | collective-permute-start | bytes 872456 | tf_op jit(solution)/shard_map/ppermute | solution.py:507
  89.6 4.8 %collective-permute-start.7 = (f32[568,128]{1,0:T(8,128)}, f32[568,128]{1,0:T(8,128)S(1)}, u32[]{:S(2)}, u32[]{:S(2)}) collective-permute-start(f32[568,128]{1,0:T(8,128)} %copy-done.22), channel_id=1, source_target_pairs={{1,0},{2,1},{3,2},{4,3},{5,4},{6,5},{7,6},{8,7},{9,8},{10,9},{11,1... | collective-permute-start | bytes 872456 | tf_op jit(solution)/shard_map/ppermute | solution.py:507
  97.4 27.6 %copy-start.29 = (f32[5,1920]{1,0:T(8,128)S(1)}, f32[5,1920]{1,0:T(8,128)}, u32[]{:S(2)}) copy-start(f32[5,1920]{1,0:T(8,128)} %param.19) | copy-start | bytes 115204
  116.4 19.7 %copy-start.18 = (f32[64,128]{1,0:T(8,128)S(1)}, f32[64,128]{1,0:T(8,128)}, u32[]{:S(2)}) copy-start(f32[64,128]{1,0:T(8,128)} %copy-done.17) | copy-start | bytes 98308
  118.0 11.9 %all-to-all-start.5 = ((f32[16,5,4,128]{3,2,1,0:T(4,128)}), f32[16,5,4,128]{3,2,1,0:T(4,128)S(1)}, u32[]{:S(2)}, u32[]{:S(2)}) async-start(f32[16,5,4,128]{3,2,1,0:T(4,128)} %bitcast.37), calls=%async_computation.5 | async-start | bytes 327680 | tf_op jit(solution)/shard_map/all_to_all | solution.py:513
  121.5 3.6 %collective-permute-start.8 = (f32[32,128]{1,0:T(8,128)S(1)}, f32[32,128]{1,0:T(8,128)S(1)}, u32[]{:S(2)}, u32[]{:S(2)}) collective-permute-start(f32[32,128]{1,0:T(8,128)S(1)} %get-tuple-element.65), channel_id=1, source_target_pairs={{0,1},{1,2},{2,3},{3,4},{4,5},{5,6},{6,7},{7,8},{8,9},{9,10},{10,1... | collective-permute-start | bytes 49160 | tf_op jit(solution)/shard_map/ppermute | solution.py:507
  123.7 4.2 %collective-permute-start.9 = (f32[32,128]{1,0:T(8,128)S(1)}, f32[32,128]{1,0:T(8,128)S(1)}, u32[]{:S(2)}, u32[]{:S(2)}) collective-permute-start(f32[32,128]{1,0:T(8,128)S(1)} %get-tuple-element.66), channel_id=1, source_target_pairs={{1,0},{2,1},{3,2},{4,3},{5,4},{6,5},{7,6},{8,7},{9,8},{10,9},{11,1... | collective-permute-start | bytes 49160 | tf_op jit(solution)/shard_map/ppermute | solution.py:507
  130.7 3.7 %collective-permute-start.10 = (f32[60,128]{1,0:T(8,128)S(1)}, f32[60,128]{1,0:T(8,128)S(1)}, u32[]{:S(2)}, u32[]{:S(2)}) collective-permute-start(f32[60,128]{1,0:T(8,128)S(1)} %get-tuple-element.68), channel_id=1, source_target_pairs={{0,1},{1,2},{2,3},{3,4},{4,5},{5,6},{6,7},{7,8},{8,9},{9,10},{10,1... | collective-permute-start | bytes 92168 | tf_op jit(solution)/shard_map/ppermute | solution.py:507
  133.0 3.1 %collective-permute-start.11 = (f32[60,128]{1,0:T(8,128)S(1)}, f32[60,128]{1,0:T(8,128)S(1)}, u32[]{:S(2)}, u32[]{:S(2)}) collective-permute-start(f32[60,128]{1,0:T(8,128)S(1)} %get-tuple-element.69), channel_id=1, source_target_pairs={{1,0},{2,1},{3,2},{4,3},{5,4},{6,5},{7,6},{8,7},{9,8},{10,9},{11,1... | collective-permute-start | bytes 92168 | tf_op jit(solution)/shard_map/ppermute | solution.py:507
  136.1 1.3 copy-start.1
  137.4 1.3 copy-start.3
  138.7 21.7 %copy-start.12 = (f32[4,80,128]{2,1,0:T(8,128)S(1)}, f32[4,80,128]{2,1,0:T(8,128)}, u32[]{:S(2)}) copy-start(f32[4,80,128]{2,1,0:T(8,128)} %copy-done.11) | copy-start | bytes 491524
  138.7 21.7 %copy-start.14 = (f32[4,80,128]{2,1,0:T(8,128)S(1)}, f32[4,80,128]{2,1,0:T(8,128)}, u32[]{:S(2)}) copy-start(f32[4,80,128]{2,1,0:T(8,128)} %copy-done.13) | copy-start | bytes 491524
  141.3 1.0 copy-start.4
  162.0 11.9 %all-to-all-start.7 = ((f32[16,5,4,128]{3,2,1,0:T(4,128)}), f32[16,5,4,128]{3,2,1,0:T(4,128)S(1)}, u32[]{:S(2)}, u32[]{:S(2)}) async-start(f32[16,5,4,128]{3,2,1,0:T(4,128)} %bitcast.41), calls=%async_computation.7 | async-start | bytes 327680 | tf_op jit(solution)/shard_map/all_to_all | solution.py:513
  165.5 3.5 %collective-permute-start.12 = (f32[512,128]{1,0:T(8,128)S(1)}, f32[512,128]{1,0:T(8,128)S(1)}, u32[]{:S(2)}, u32[]{:S(2)}) collective-permute-start(f32[512,128]{1,0:T(8,128)S(1)} %get-tuple-element.77), channel_id=1, source_target_pairs={{0,1},{1,2},{2,3},{3,4},{4,5},{5,6},{6,7},{7,8},{8,9},{9,10},{10,1... | collective-permute-start | bytes 786440 | tf_op jit(solution)/shard_map/ppermute | solution.py:507
  167.7 4.6 %collective-permute-start.13 = (f32[512,128]{1,0:T(8,128)S(1)}, f32[512,128]{1,0:T(8,128)S(1)}, u32[]{:S(2)}, u32[]{:S(2)}) collective-permute-start(f32[512,128]{1,0:T(8,128)S(1)} %get-tuple-element.78), channel_id=1, source_target_pairs={{1,0},{2,1},{3,2},{4,3},{5,4},{6,5},{7,6},{8,7},{9,8},{10,9},{11,1... | collective-permute-start | bytes 786440 | tf_op jit(solution)/shard_map/ppermute | solution.py:507
  174.7 7.8 %collective-permute-start.14 = (f32[60,128]{1,0:T(8,128)S(1)}, f32[60,128]{1,0:T(8,128)S(1)}, u32[]{:S(2)}, u32[]{:S(2)}) collective-permute-start(f32[60,128]{1,0:T(8,128)S(1)} %get-tuple-element.80), channel_id=1, source_target_pairs={{0,1},{1,2},{2,3},{3,4},{4,5},{5,6},{6,7},{7,8},{8,9},{9,10},{10,1... | collective-permute-start | bytes 92168 | tf_op jit(solution)/shard_map/ppermute | solution.py:507
  179.7 3.2 %copy-start.5 = (f32[5,4,8,1920]{3,2,1,0:T(8,128)S(1)}, f32[5,4,8,1920]{3,2,1,0:T(8,128)}, u32[]{:S(2)}) copy-start(f32[5,4,8,1920]{3,2,1,0:T(8,128)} %copy-done.4) | copy-start | bytes 3686404
  179.7 3.2 %collective-permute-start.15 = (f32[60,128]{1,0:T(8,128)S(1)}, f32[60,128]{1,0:T(8,128)S(1)}, u32[]{:S(2)}, u32[]{:S(2)}) collective-permute-start(f32[60,128]{1,0:T(8,128)S(1)} %get-tuple-element.81), channel_id=1, source_target_pairs={{1,0},{2,1},{3,2},{4,3},{5,4},{6,5},{7,6},{8,7},{9,8},{10,9},{11,1... | collective-permute-start | bytes 92168 | tf_op jit(solution)/shard_map/ppermute | solution.py:507
  182.9 20.9 %copy-start.25 = (f32[8,5,4,1920]{3,2,1,0:T(4,128)S(1)}, f32[8,5,4,1920]{3,2,1,0:T(4,128)}, u32[]{:S(2)}) copy-start(f32[8,5,4,1920]{3,2,1,0:T(4,128)} %param.15) | copy-start | bytes 3686404
  184.9 1.0 copy-start.6

commit v2 on v1

v2 whole, which is shorter than its diff:
```python
import functools

import jax
import jax.numpy as jnp
from jax import lax
from jax.experimental import pallas as pl
from jax.experimental.pallas import tpu as pltpu
from jax.sharding import PartitionSpec as P

LAT_DEV = 2
NEAR_LAT = LAT_DEV + 2
CHANNELS = 4
LEVELS = 8
WIDTH = 128
SUBLANES = 8

KAPPA_V = 0.1
TIME_STEP = 0.3
FLUX_RATE = 0.05
FEEDBACK = 0.5
ASCENT = 0.5
EPSILON = 1e-06
HIGHEST = lax.Precision.HIGHEST
VMEM_BYTES = 32 * 1024 * 1024


class Sizes:
    def __init__(self, devices, capacity, rows, cells):
        self.devices = devices
        self.capacity = capacity
        self.slots = devices * capacity
        self.rows = rows
        self.cells = cells
        self.row_tiles = cells // WIDTH
        self.tiles = rows * self.row_tiles
        self.row_width = CHANNELS * self.row_tiles
        self.pitch = -(-self.row_tiles // SUBLANES) * SUBLANES
        self.own_rows = CHANNELS * capacity
        self.chunk = -(-(self.own_rows + 2 * capacity) // SUBLANES) * SUBLANES
        self.slot_lines = -(-self.slots // WIDTH)
        self.facts = -(-(self.slot_lines + 1) // SUBLANES) * SUBLANES
        self.lat_lines = LAT_DEV * self.pitch
        self.whole = (rows, CHANNELS, LEVELS, cells)
        self.edge = (CHANNELS, LEVELS, cells)
        self.surface = (CHANNELS * (self.tiles + 1), WIDTH)
        self.narrow = (CHANNELS * self.slots, WIDTH)
        self.wide = (devices * self.chunk, WIDTH)
        self.slope = (NEAR_LAT * self.pitch, WIDTH)
        self.lats = (self.lat_lines, WIDTH)
        self.told = (self.lat_lines + self.facts, WIDTH)
        self.near = (-(-(self.tiles + 1) // SUBLANES) * SUBLANES, WIDTH)
        self.by_slot = (CHANNELS, self.slots, WIDTH)


class Shipped:
    def __init__(self, block, home, sems):
        self.block, self.home, self.sems = block, home, sems
        self.by_row = False
        self.started = False

    def __getitem__(self, at):
        return self.block[at]

    def __setitem__(self, at, value):
        self.block[at] = value

    def row(self, index):
        self.by_row = True
        self.started = True
        return pltpu.make_async_copy(
            self.block.at[index], self.home.at[index], self.sems.at[index]
        )

    def all(self):
        return pltpu.make_async_copy(self.block, self.home, self.sems.at[0])

    def start(self):
        self.started = True
        self.all().start()

    def finish(self, rows):
        if self.by_row:
            for index in range(rows):
                self.row(index).wait()
        else:
            self.all().wait()


def cols(tile):
    return slice(tile * WIDTH, (tile + 1) * WIDTH)


def lanes_sum(left_here, left_before, right_here, right_after, lane):
    return jnp.where(lane == 0, left_before, left_here) + jnp.where(
        lane == WIDTH - 1, right_after, right_here
    )


def levels_sum(field, sub):
    return jnp.where(sub == 0, 0.0, pltpu.roll(field, 1, 0)) + jnp.where(
        sub == LEVELS - 1, 0.0, pltpu.roll(field, LEVELS - 1, 0)
    )


def row_tiles_of(sz, ref, row):
    return ref[pl.ds(row * sz.row_width, sz.row_tiles, stride=CHANNELS), :]


def put_row_tiles(sz, ref, row, value):
    ref[pl.ds(row * sz.row_width, sz.row_tiles, stride=CHANNELS), :] = value


def near_row(sz, ref, row):
    return ref[row * sz.row_tiles : (row + 1) * sz.row_tiles, :]


def load_surface_row(sz, target, row, source, base):
    for tile in range(sz.row_tiles):
        for channel in range(CHANNELS):
            at = base + tile * CHANNELS + channel
            target[row, channel, 0:1, cols(tile)] = source[pl.ds(at, 1), :]


def tables_kernel(sz, wet_list, wet_owner, remap_src, remap_tgt, remap_weight, me, tile_of, facts, used):
    def clear(index, carry):
        tile_of[index] = sz.tiles
        return carry

    lax.fori_loop(0, tile_of.shape[0], clear, 0)

    def clear_used(index, carry):
        used[index] = 0
        return carry

    lax.fori_loop(0, sz.devices, clear_used, 0)

    def place(entry, carry):
        owner = wet_owner[0, entry]
        live = owner >= 0
        owner = jnp.maximum(owner, 0)
        rank = used[owner]
        used[owner] = rank + live.astype(jnp.int32)
        slot = jnp.where(live, owner * sz.capacity + rank, sz.slots)
        tile_of[slot] = jnp.where(live, wet_list[0, entry], sz.tiles)
        return carry

    lax.fori_loop(0, wet_list.shape[1], place, 0)
    for line in range(sz.slot_lines):

        def tell(index, carry, line=line):
            facts[line, index] = (sz.tiles - tile_of[line * WIDTH + index]).astype(jnp.float32)
            return carry

        lax.fori_loop(0, min(WIDTH, sz.slots - line * WIDTH), tell, 0)
    for index in range(NEAR_LAT * sz.rows):
        facts[sz.slot_lines, index] = 0.0

    def weigh_entry(entry, carry):
        lat = remap_tgt[entry] - (me[0] * LAT_DEV - 1)
        row = remap_src[entry] - me[0] * sz.rows
        at = lat * sz.rows + row
        facts[sz.slot_lines, at] = facts[sz.slot_lines, at] + remap_weight[entry]
        return carry

    lax.fori_loop(0, remap_src.shape[0], weigh_entry, 0)


class Remap:
    def __init__(self, sz, facts, low, high):
        self.sz, self.facts, self.low, self.high = sz, facts, low, high

    def own(self, lat, row):
        return self.facts[self.sz.slot_lines, lat * self.sz.rows + row]

    def beside(self, told, lat, row):
        return told[self.sz.lat_lines + self.sz.slot_lines, lat * self.sz.rows + row]

    def of_low(self, lat, row):
        return self.beside(self.low, lat + LAT_DEV, row)

    def of_high(self, lat, row):
        return self.beside(self.high, lat - LAT_DEV, row)

    def tile(self, told, slot):
        line = self.sz.lat_lines + slot // WIDTH
        return self.sz.tiles - told[line, slot % WIDTH].astype(jnp.int32)


def sum_of(weights, values):
    total = weights[0] * values[0]
    for weight, value in zip(weights[1:], values[1:]):
        total = total + weight * value
    return total


def own_sums(sz, remap, own, factor):
    return [
        factor * sum_of([remap.own(lat, row) for row in range(sz.rows)], own)
        for lat in range(NEAR_LAT)
    ]


def send_sums(sz, sums, send_low, send_high):
    for lat in range(NEAR_LAT):
        send = send_low if lat < LAT_DEV else send_high
        at = (lat % LAT_DEV) * sz.pitch
        send[at : at + sz.row_tiles, :] = sums[lat]


def lat_rows(sz, ref, lat):
    return ref[lat * sz.pitch : lat * sz.pitch + sz.row_tiles, :]


def told_sums(sz, from_low, from_high):
    return [
        lat_rows(sz, from_low if lat < LAT_DEV else from_high, lat % LAT_DEV)
        for lat in range(NEAR_LAT)
    ]


def forward_kernel(sz, first, last, *refs):
    refs = list(refs)
    field, low, high, diffusivity, mix, table, own_facts = refs[:7]
    refs = refs[7:]
    if first:
        facts = refs[0]
        refs = refs[1:]
    else:
        surface, low_surface, high_surface = refs[:3]
        refs = refs[3:]
    if last:
        target, weight = refs[:2]
        refs = refs[2:]
    out, drive, new_surface, packed, tell_low, tell_high, edge_low, edge_high = refs[:8]
    padded, in_sems, edge_sems = refs[8:]
    remap = Remap(sz, own_facts, None, None)

    edges = [
        pltpu.make_async_copy(low, padded.at[0], edge_sems.at[0]),
        pltpu.make_async_copy(high, padded.at[sz.rows + 1], edge_sems.at[1]),
    ]

    def arrival(row):
        return pltpu.make_async_copy(field.at[row], padded.at[row + 1], in_sems.at[row])

    edges[0].start()
    for row in range(sz.rows):
        arrival(row).start()
    edges[1].start()

    def ready(row):
        arrival(row).wait()
        if not first:
            load_surface_row(sz, padded, row + 1, surface, row * sz.row_width)

    for side in (0, 1):
        edges[side].wait()
        if not first:
            source = high_surface if side else low_surface
            load_surface_row(sz, padded, (sz.rows + 1) * side, source, 0)
    ready(0)

    lane = lax.broadcasted_iota(jnp.int32, (LEVELS, WIDTH), 1)
    sub = lax.broadcasted_iota(jnp.int32, (LEVELS, WIDTH), 0)
    count = sz.row_tiles

    def one_row(row, carry):
        @pl.when(row < sz.rows - 1)
        def _():
            ready(row + 1)

        here = [[padded[row + 1, c, :, cols(t)] for t in range(count)] for c in range(CHANNELS)]
        for t in range(count):
            coeff = jnp.broadcast_to(diffusivity[row, 0:1, cols(t)], (LEVELS, WIDTH))
            if last:
                scale = weight[row, 0:1, cols(t)]
                scale = jnp.broadcast_to(scale * scale, (LEVELS, WIDTH))
            for c in range(CHANNELS):
                mixed = mix[c * CHANNELS] * here[0][t]
                for k in range(1, CHANNELS):
                    mixed = mixed + mix[c * CHANNELS + k] * here[k][t]
                bent = jnp.tanh(mixed)
                drive[row, c, :, cols(t)] = bent
                field_here = here[c][t]
                around = lanes_sum(
                    pltpu.roll(field_here, 1, 1),
                    pltpu.roll(here[c][(t - 1) % count], 1, 1),
                    pltpu.roll(field_here, WIDTH - 1, 1),
                    pltpu.roll(here[c][(t + 1) % count], WIDTH - 1, 1),
                    lane,
                )
                around = around + (padded[row, c, :, cols(t)] + padded[row + 2, c, :, cols(t)])
                stepped = (
                    field_here
                    + coeff * (around - 4.0 * field_here)
                    + KAPPA_V * (levels_sum(field_here, sub) - 2.0 * field_here)
                    + TIME_STEP * bent
                )
                new_surface[pl.ds((row * count + t) * CHANNELS + c, 1), :] = stepped[0:1, :]
                if last:
                    stepped = scale * (stepped - target[row, c, :, cols(t)])
                out[row, c, :, cols(t)] = stepped
        drive.row(row).start()
        out.row(row).start()
        return carry

    lax.fori_loop(0, sz.rows, one_row, 0)
    new_surface[CHANNELS * sz.tiles :, :] = jnp.zeros((CHANNELS, WIDTH), jnp.float32)
    new_surface.start()
    pack_slots(sz, table, new_surface, packed)
    packed.start()
    own = [row_tiles_of(sz, new_surface.block, row) for row in range(sz.rows)]
    send_sums(sz, own_sums(sz, remap, own, 1.0), tell_low, tell_high)
    blank = facts[...] if first else jnp.zeros((sz.facts, WIDTH), jnp.float32)
    for tell in (tell_low, tell_high):
        tell[sz.lat_lines :, :] = blank
        tell.start()
    store_edges(sz, out, diffusivity if last else None, edge_low, edge_high)


def pack_slots(sz, table, surface, packed):
    for slot in range(sz.slots):
        at = pl.multiple_of(table[slot] * CHANNELS, CHANNELS)
        packed[slot * CHANNELS : (slot + 1) * CHANNELS, :] = surface[pl.ds(at, CHANNELS), :]


def store_edges(sz, field, diffusivity, send_low, send_high):
    for row, send in ((0, send_low), (sz.rows - 1, send_high)):
        for channel in range(CHANNELS):
            for tile in range(sz.row_tiles):
                value = field[row, channel, :, cols(tile)]
                if diffusivity is not None:
                    value = value * jnp.broadcast_to(
                        diffusivity[row, 0:1, cols(tile)], (LEVELS, WIDTH)
                    )
                send[channel, :, cols(tile)] = value
        send.start()


def owner_kernel(sz, arrived, mixing, air, wind, bulk, flux, mixed_slope, flux_slope, flat, first):
    slots = sz.slots
    values = [arrived[pl.ds(c, slots, stride=CHANNELS), :] for c in range(CHANNELS)]
    mixed = jnp.tanh(
        jnp.dot(
            mixing[...],
            jnp.concatenate(values, axis=1),
            precision=HIGHEST,
            preferred_element_type=jnp.float32,
        )
    )
    contrast = []
    for c in range(CHANNELS):
        mixed_here = mixed[:, cols(c)]
        mixed_slope[c] = 1.0 - mixed_here * mixed_here
        contrast.append((air[...] - values[0] if c == 0 else values[c]) + mixed_here)
    mixed_slope.start()
    rate = FLUX_RATE * wind[...]
    for c in range(CHANNELS):
        forcing = bulk[c, 0] * contrast[0]
        for k in range(1, CHANNELS):
            forcing = forcing + bulk[c, k] * contrast[k]
        bent = jnp.tanh(forcing)
        flux_slope[c] = rate * (1.0 - bent * bent)
        one = rate * bent
        flat[pl.ds(c, slots, stride=CHANNELS), :] = one
        if c == 0:
            first[...] = one
    flux_slope.start()
    cap = sz.capacity
    gap = jnp.zeros((sz.chunk - sz.own_rows, WIDTH), jnp.float32)
    for d in range(sz.devices):
        at = d * sz.chunk
        flux[at : at + sz.own_rows, :] = flat[d * sz.own_rows : (d + 1) * sz.own_rows, :]
        at = at + sz.own_rows
        flux[at : (d + 1) * sz.chunk, :] = gap
        if d > 0:
            flux[at : at + cap, :] = first[(d - 1) * cap : d * cap, :]
        if d < sz.devices - 1:
            flux[at + cap : at + 2 * cap, :] = first[(d + 1) * cap : (d + 2) * cap, :]


def owner_back_kernel(sz, arrived, mixing, mixed_slope, flux_slope, bulk, back, flat, extra):
    slots, cap = sz.slots, sz.capacity
    for d in range(sz.devices):
        at = d * sz.chunk
        flat[d * sz.own_rows : (d + 1) * sz.own_rows, :] = arrived[at : at + sz.own_rows, :]
        more = jnp.zeros((cap, WIDTH), jnp.float32)
        if d < sz.devices - 1:
            at = (d + 1) * sz.chunk + sz.own_rows
            more = more + arrived[at : at + cap, :]
        if d > 0:
            at = (d - 1) * sz.chunk + sz.own_rows + cap
            more = more + arrived[at : at + cap, :]
        extra[d * cap : (d + 1) * cap, :] = more
    forced = []
    for c in range(CHANNELS):
        got = flat[pl.ds(c, slots, stride=CHANNELS), :]
        if c == 0:
            got = got + extra[...]
        forced.append(flux_slope[c] * got)
    direct = []
    for k in range(CHANNELS):
        total = bulk[0, k] * forced[0]
        for c in range(1, CHANNELS):
            total = total + bulk[c, k] * forced[c]
        direct.append(total)
    through = lax.dot_general(
        mixing[...],
        jnp.concatenate([direct[k] * mixed_slope[k] for k in range(CHANNELS)], axis=1),
        (((0,), (0,)), ((), ())),
        precision=HIGHEST,
        preferred_element_type=jnp.float32,
    )
    for k in range(CHANNELS):
        sign = -1.0 if k == 0 else 1.0
        back.block[pl.ds(k, slots, stride=CHANNELS), :] = through[:, cols(k)] + sign * direct[k]


def spread_back(sz, surface, slope, remap, table, packed, near_low, near_high, tell_low, tell_high):
    rows, count, cap = sz.rows, sz.row_tiles, sz.capacity
    block = surface.block
    own = [row_tiles_of(sz, block, row) for row in range(rows)]
    sums = own_sums(sz, remap, own, FEEDBACK)
    send_sums(sz, sums, tell_low, tell_high)
    tell_low.start()
    tell_high.start()
    lats = [lat_rows(sz, slope, lat) * sums[lat] for lat in range(NEAR_LAT)]
    every = range(NEAR_LAT)
    for row in range(rows):
        added = sum_of([remap.own(lat, row) for lat in every], lats)
        put_row_tiles(sz, block, row, own[row] + added)
        at = row * count
        near_low[at : at + count, :] = sum_of(
            [remap.of_low(lat, row) for lat in range(LAT_DEV)], lats[:LAT_DEV]
        )
        near_high[at : at + count, :] = sum_of(
            [remap.of_high(lat, row) for lat in range(LAT_DEV, NEAR_LAT)], lats[LAT_DEV:]
        )
    rest = sz.near[0] - sz.tiles
    near_low[sz.tiles :, :] = jnp.zeros((rest, WIDTH), jnp.float32)
    near_high[sz.tiles :, :] = jnp.zeros((rest, WIDTH), jnp.float32)
    surface.start()
    gap = jnp.zeros((sz.chunk - sz.own_rows, WIDTH), jnp.float32)
    for owner in range(sz.devices):
        packed[owner * sz.chunk + sz.own_rows : (owner + 1) * sz.chunk, :] = gap
    for slot in range(sz.slots):
        owner, rank = slot // cap, slot % cap
        at = owner * sz.chunk + rank * CHANNELS
        tile = pl.multiple_of(table[slot] * CHANNELS, CHANNELS)
        packed[at : at + CHANNELS, :] = surface[pl.ds(tile, CHANNELS), :]
        at = owner * sz.chunk + sz.own_rows + rank
        packed[at : at + 1, :] = near_low[pl.ds(remap.tile(remap.low, slot), 1), :]
        at = at + cap
        packed[at : at + 1, :] = near_high[pl.ds(remap.tile(remap.high, slot), 1), :]


def surface_kernel(sz, last, *refs):
    refs = list(refs)
    flux, before, from_low, from_high, table, facts, told_low, told_high = refs[:8]
    refs = refs[8:]
    if last:
        target, weight = refs[:2]
        surface, slope, packed, tell_low, tell_high, near_low, near_high = refs[2:]
        block = surface.block
    else:
        surface, send_low, send_high, slope, near_low, near_high = refs
        block = surface
    remap = Remap(sz, facts, told_low, told_high)
    rows, cap = sz.rows, sz.capacity
    block[...] = before[...]
    near_low[...] = jnp.zeros(sz.near, jnp.float32)
    near_high[...] = jnp.zeros(sz.near, jnp.float32)
    for slot in range(sz.slots):
        owner, rank = slot // cap, slot % cap
        at = owner * sz.chunk + rank * CHANNELS
        tile = pl.multiple_of(table[slot] * CHANNELS, CHANNELS)
        block[pl.ds(tile, CHANNELS), :] = (
            before[pl.ds(tile, CHANNELS), :] + flux[at : at + CHANNELS, :]
        )
        at = owner * sz.chunk + sz.own_rows + rank
        near_low[pl.ds(remap.tile(told_low, slot), 1), :] = flux[at : at + 1, :]
        at = at + cap
        near_high[pl.ds(remap.tile(told_high, slot), 1), :] = flux[at : at + 1, :]
    block[CHANNELS * sz.tiles :, :] = jnp.zeros((CHANNELS, WIDTH), jnp.float32)
    own = [row_tiles_of(sz, block, row) for row in range(rows)]
    sums = own_sums(sz, remap, own, 1.0)
    told = told_sums(sz, from_low, from_high)
    air = []
    for lat in range(NEAR_LAT):
        if lat < LAT_DEV:
            near, weights = near_low, [remap.of_low(lat, row) for row in range(rows)]
        else:
            near, weights = near_high, [remap.of_high(lat, row) for row in range(rows)]
        more = sum_of(weights, [near_row(sz, near, row) for row in range(rows)])
        one = jnp.tanh(sums[lat] + told[lat] + more)
        slope[lat * sz.pitch : lat * sz.pitch + sz.row_tiles, :] = 1.0 - one * one
        air.append(one)
    slope.start()
    for row in range(rows):
        weights = [remap.own(lat, row) for lat in range(NEAR_LAT)]
        put_row_tiles(sz, block, row, own[row] + FEEDBACK * sum_of(weights, air))
    if last:
        end = CHANNELS * sz.tiles
        scale = weight[...]
        block[0:end, :] = scale * scale * (block[0:end, :] - target[...])
        spread_back(
            sz, surface, slope, remap, table, packed, near_low, near_high, tell_low, tell_high
        )
    else:
        send_low[...] = surface[0 : sz.row_width, :]
        send_high[...] = surface[(rows - 1) * sz.row_width : rows * sz.row_width, :]


def merge_kernel(
    sz, back, before, slope, from_low, from_high, table, facts, diffusivity, surface, send_low, send_high
):
    rows, width = sz.rows, sz.row_width
    remap = Remap(sz, facts, None, None)
    surface[...] = before[...]
    for slot in range(sz.slots):
        tile = pl.multiple_of(table[slot] * CHANNELS, CHANNELS)
        surface[pl.ds(tile, CHANNELS), :] = (
            before[pl.ds(tile, CHANNELS), :] + back[slot * CHANNELS : (slot + 1) * CHANNELS, :]
        )
    surface[CHANNELS * sz.tiles :, :] = jnp.zeros((CHANNELS, WIDTH), jnp.float32)
    told = told_sums(sz, from_low, from_high)
    lats = [lat_rows(sz, slope, lat) * told[lat] for lat in range(NEAR_LAT)]
    for row in range(rows):
        own = row_tiles_of(sz, surface, row)
        weights = [remap.own(lat, row) for lat in range(NEAR_LAT)]
        put_row_tiles(sz, surface, row, own + sum_of(weights, lats))
    send_low[...] = diffusivity[0:width, :] * surface[0:width, :]
    end = rows * width
    send_high[...] = diffusivity[end - width : end, :] * surface[end - width : end, :]


def backward_kernel(sz, last, *refs):
    refs = list(refs)
    field, surface, low, high, low_surface, high_surface, drive, diffusivity, mix = refs[:9]
    refs = refs[9:]
    if last:
        perturbation, out, sums = refs[:3]
        local, bent_all, padded, in_sems, edge_sems = refs[3:]
    else:
        table, facts, told_low, told_high, slope = refs[:5]
        out, new_surface, packed, tell_low, tell_high, edge_low, edge_high = refs[5:12]
        local, bent_all, padded, near_low, near_high, in_sems, edge_sems = refs[12:]
        remap = Remap(sz, facts, told_low, told_high)
    count = sz.row_tiles

    edges = [
        pltpu.make_async_copy(low, padded.at[0], edge_sems.at[0]),
        pltpu.make_async_copy(high, padded.at[sz.rows + 1], edge_sems.at[1]),
    ]

    def arrivals(row):
        return [
            pltpu.make_async_copy(field.at[row], local.at[row], in_sems.at[0, row]),
            pltpu.make_async_copy(drive.at[row], bent_all.at[row], in_sems.at[1, row]),
        ]

    edges[0].start()
    for row in range(sz.rows):
        for arrival in arrivals(row):
            arrival.start()
    edges[1].start()

    def ready(row):
        for arrival in arrivals(row):
            arrival.wait()
        load_surface_row(sz, local, row, surface, row * sz.row_width)
        for t in range(count):
            coeff = jnp.broadcast_to(diffusivity[row, 0:1, cols(t)], (LEVELS, WIDTH))
            for c in range(CHANNELS):
                padded[row + 1, c, :, cols(t)] = coeff * local[row, c, :, cols(t)]

    for side in (0, 1):
        edges[side].wait()
        source = high_surface if side else low_surface
        load_surface_row(sz, padded, (sz.rows + 1) * side, source, 0)
    ready(0)
    lane = lax.broadcasted_iota(jnp.int32, (LEVELS, WIDTH), 1)
    sub = lax.broadcasted_iota(jnp.int32, (LEVELS, WIDTH), 0)

    def one_row(row, carry):
        @pl.when(row < sz.rows - 1)
        def _():
            ready(row + 1)

        scaled = [[padded[row + 1, c, :, cols(t)] for t in range(count)] for c in range(CHANNELS)]
        for t in range(count):
            here, bent = [], []
            for c in range(CHANNELS):
                value = local[row, c, :, cols(t)]
                one = bent_all[row, c, :, cols(t)]
                here.append(value)
                bent.append((1.0 - one * one) * value)
            for c in range(CHANNELS):
                mixed = mix[c] * bent[0]
                for k in range(1, CHANNELS):
                    mixed = mixed + mix[k * CHANNELS + c] * bent[k]
                around = lanes_sum(
                    pltpu.roll(scaled[c][t], 1, 1),
                    pltpu.roll(scaled[c][(t - 1) % count], 1, 1),
                    pltpu.roll(scaled[c][t], WIDTH - 1, 1),
                    pltpu.roll(scaled[c][(t + 1) % count], WIDTH - 1, 1),
                    lane,
                )
                around = around + (padded[row, c, :, cols(t)] + padded[row + 2, c, :, cols(t)])
                stepped = (
                    here[c]
                    + (around - 4.0 * scaled[c][t])
                    + KAPPA_V * (levels_sum(here[c], sub) - 2.0 * here[c])
                    + TIME_STEP * mixed
                )
                out[row, c, :, cols(t)] = stepped
                if last:
                    start = perturbation[row, c, :, cols(t)]
                    carry = (
                        carry[0] + start * start,
                        carry[1] + start * stepped,
                        carry[2] + stepped * stepped,
                    )
                else:
                    new_surface[pl.ds((row * count + t) * CHANNELS + c, 1), :] = stepped[0:1, :]
        out.row(row).start()
        return carry

    blank = jnp.zeros((LEVELS, WIDTH), jnp.float32)
    totals = lax.fori_loop(0, sz.rows, one_row, (blank, blank, blank) if last else 0)
    if last:
        place = lax.broadcasted_iota(jnp.int32, sums.block.shape, 1)
        held = jnp.zeros(sums.block.shape, jnp.float32)
        for index in range(3):
            total = jnp.sum(jnp.sum(totals[index], axis=0, keepdims=True), axis=1, keepdims=True)
            held = jnp.where(place == index, total, held)
        sums[...] = held
    else:
        new_surface[CHANNELS * sz.tiles :, :] = jnp.zeros((CHANNELS, WIDTH), jnp.float32)
        spread_back(
            sz, new_surface, slope, remap, table, packed, near_low, near_high, tell_low, tell_high
        )
        packed.start()
        store_edges(sz, out, diffusivity, edge_low, edge_high)


def final_kernel(cell_total, everyones, perturbation, gradient, out, start, slope, in_sems):
    levels = start.shape[0]

    def arrivals(level):
        return [
            pltpu.make_async_copy(perturbation.at[level], start.at[level], in_sems.at[0, level]),
            pltpu.make_async_copy(gradient.at[level], slope.at[level], in_sems.at[1, level]),
        ]

    for level in range(levels):
        for arrival in arrivals(level):
            arrival.start()
    sums = jnp.sum(everyones[...], axis=0, keepdims=True) / cell_total
    place = lax.broadcasted_iota(jnp.int32, sums.shape, 1)
    means = [
        jnp.broadcast_to(
            jnp.sum(jnp.where(place == index, sums, 0.0), axis=1, keepdims=True), (1, WIDTH)
        )
        for index in range(3)
    ]
    scale = lax.rsqrt(means[2] + EPSILON)
    mean_sq = means[0] + 2.0 * ASCENT * scale * means[1] + ASCENT * ASCENT * scale * scale * means[2]
    shrink = lax.rsqrt(mean_sq + EPSILON)
    step = jnp.broadcast_to(ASCENT * scale, (CHANNELS, WIDTH))
    shrink = jnp.broadcast_to(shrink, (CHANNELS, WIDTH))
    for level in range(levels):
        for arrival in arrivals(level):
            arrival.wait()
        for row in range(start.shape[1]):
            for tile in range(start.shape[3] // WIDTH):
                value = start[level, row, :, cols(tile)] + step * slope[level, row, :, cols(tile)]
                out[level, row, :, cols(tile)] = value * shrink
        out.row(level).start()


def near_by(*arrays):
    return [(array, pltpu.VMEM) for array in arrays]


def scalars(*arrays):
    return [(array, pltpu.SMEM) for array in arrays]


def anywhere(*arrays):
    return [(array, pl.ANY) for array in arrays]


def call(kernel, name, inputs, kept=(), shipped=(), scratch=()):
    n_in, n_kept, n_out = len(inputs), len(kept), len(shipped)

    def run(*refs):
        ins = refs[: n_in + n_kept]
        homes = refs[n_in + n_kept : n_in + n_kept + n_out]
        rest = refs[n_in + n_kept + n_out :]
        outs = [
            Shipped(block, home, sems)
            for block, home, sems in zip(rest[:n_out], homes, rest[n_out : 2 * n_out])
        ]
        kernel(*ins, *outs, *rest[2 * n_out :])
        for out in outs:
            if not out.started:
                out.start()
        for out in outs:
            out.finish(out.block.shape[0])

    shapes = list(kept) + list(shipped)
    spaces = [pltpu.VMEM] * n_kept + [pltpu.HBM] * n_out
    blocks = [pltpu.VMEM(shape, jnp.float32) for shape in shipped]
    sems = [
        pltpu.SemaphoreType.DMA((shape[0] if len(shape) > 3 else 1,)) for shape in shipped
    ]
    more = [
        item if not isinstance(item, tuple) else pltpu.VMEM(item, jnp.float32) for item in scratch
    ]
    return pl.pallas_call(
        run,
        name=name,
        in_specs=[pl.BlockSpec(memory_space=space) for _, space in inputs],
        out_specs=[pl.BlockSpec(memory_space=space) for space in spaces],
        out_shape=[jax.ShapeDtypeStruct(shape, jnp.float32) for shape in shapes],
        scratch_shapes=blocks + sems + more,
        compiler_params=pltpu.CompilerParams(vmem_limit_bytes=VMEM_BYTES),
    )(*[array for array, _ in inputs])


def to_bulk(field):
    return field.transpose(1, 2, 0, 3)


def to_surface(sz, rows):
    split = rows.reshape(sz.rows, CHANNELS, sz.row_tiles, WIDTH).transpose(0, 2, 1, 3)
    return split.reshape(CHANNELS * sz.tiles, WIDTH)


def swap(low, high):
    count = lax.axis_size("horiz")
    upward = [(i, i + 1) for i in range(count - 1)]
    downward = [(target, source) for source, target in upward]
    return lax.ppermute(high, "horiz", upward), lax.ppermute(low, "horiz", downward)


def exchange(array, devices):
    rows = array.shape[0] // devices
    split = array.reshape(devices, rows // CHANNELS, CHANNELS, WIDTH)
    moved = lax.all_to_all(split, "horiz", split_axis=0, concat_axis=0, tiled=True)
    return moved.reshape(array.shape)


def body(
    perturbation,
    base_state,
    target_state,
    cost_weight,
    diffusivity,
    chan_mix,
    coupler_mix,
    owner_mix,
    air_temp,
    wind_speed,
    wet_list,
    wet_owner,
    remap_src,
    remap_tgt,
    remap_weight,
):
    devices = lax.axis_size("horiz")
    hours = air_temp.shape[0]
    sz = Sizes(devices, air_temp.shape[2] // devices, base_state.shape[1], base_state.shape[3])
    mixing = owner_mix[0]
    rows = sz.rows

    start = [
        (perturbation[:, row] + base_state[:, row]).transpose(1, 0, 2) for row in (0, rows - 1)
    ]
    edges = swap(*start)
    me = lax.axis_index("horiz").astype(jnp.int32).reshape(1)
    table, facts = pl.pallas_call(
        functools.partial(tables_kernel, sz),
        name="tables",
        in_specs=[pl.BlockSpec(memory_space=pltpu.SMEM)] * 6,
        out_specs=[pl.BlockSpec(memory_space=pltpu.SMEM)] * 2,
        out_shape=[
            jax.ShapeDtypeStruct((sz.slot_lines * WIDTH + WIDTH,), jnp.int32),
            jax.ShapeDtypeStruct((sz.facts, WIDTH), jnp.float32),
        ],
        scratch_shapes=[pltpu.SMEM((devices,), jnp.int32)],
    )(wet_list, wet_owner, remap_src, remap_tgt, remap_weight, me)

    mix = jnp.broadcast_to(
        chan_mix.transpose(1, 2, 0).reshape(CHANNELS * CHANNELS, LEVELS, 1),
        (CHANNELS * CHANNELS, LEVELS, WIDTH),
    )
    start_pert = to_bulk(perturbation)
    field = start_pert + to_bulk(base_state)
    target = to_bulk(target_state)
    target_surface = to_surface(sz, target_state[0])

    def all_channels(array):
        return to_surface(sz, jnp.broadcast_to(array[:, None, :], (rows, CHANNELS, sz.cells)))

    weight_surface = all_channels(cost_weight)
    diffusivity_surface = all_channels(diffusivity)
    diffusivity = diffusivity.reshape(rows, 1, sz.cells)
    weight = cost_weight.reshape(rows, 1, sz.cells)

    wider = (rows + 2, CHANNELS, LEVELS, sz.cells)
    row_surface = (sz.row_width, WIDTH)
    row_sems = pltpu.SemaphoreType.DMA((rows,))
    two_row_sems = pltpu.SemaphoreType.DMA((2, rows))
    edge_sems = pltpu.SemaphoreType.DMA((2,))

    saved = []
    surface = None
    told = None
    for hour in range(hours):
        first, last = hour == 0, hour == hours - 1
        inputs = anywhere(field, *edges) + near_by(diffusivity, mix) + scalars(table, facts)
        if first:
            inputs += near_by(facts)
        else:
            inputs += near_by(surface, *surface_edges)
        if last:
            inputs += near_by(target, weight)
        field, drive, surface, packed, *sends = call(
            functools.partial(forward_kernel, sz, first, last),
            "step",
            inputs,
            shipped=[
                sz.whole, sz.whole, sz.surface, sz.narrow, sz.told, sz.told, sz.edge, sz.edge
            ],
            scratch=[wider, row_sems, edge_sems],
        )
        arrived = exchange(packed, devices)
        got = swap(*sends[:2])
        if first:
            told = got
        flux, mixed_slope, flux_slope = call(
            functools.partial(owner_kernel, sz),
            "owners",
            near_by(arrived, mixing, air_temp[hour, 0], wind_speed[hour, 0])
            + scalars(coupler_mix),
            shipped=[sz.wide, sz.by_slot, sz.by_slot],
            scratch=[sz.narrow, (sz.slots, WIDTH)],
        )
        flux, *sends = lax.optimization_barrier((flux, *sends[2:]))
        flux = exchange(flux, devices)
        edges = swap(*sends)
        inputs = near_by(flux, surface, *got) + scalars(table, facts, *told)
        near = [sz.near, sz.near]
        if last:
            surface, slope, packed, *sends = call(
                functools.partial(surface_kernel, sz, True),
                "surface",
                inputs + near_by(target_surface, weight_surface),
                shipped=[sz.surface, sz.slope, sz.wide, sz.lats, sz.lats],
                scratch=near,
            )
        else:
            surface, *sends, slope = call(
                functools.partial(surface_kernel, sz, False),
                "surface",
                inputs,
                kept=[sz.surface, row_surface, row_surface],
                shipped=[sz.slope],
                scratch=near,
            )
            surface_edges = swap(*sends)
        saved.append((drive, slope, mixed_slope, flux_slope))

    edge_sends = None
    for hour in reversed(range(hours)):
        drive, slope, mixed_slope, flux_slope = saved[hour]
        arrived = exchange(packed, devices)
        got = swap(*sends)
        back = call(
            functools.partial(owner_back_kernel, sz),
            "owners_back",
            near_by(arrived, mixing, mixed_slope, flux_slope) + scalars(coupler_mix),
            shipped=[sz.narrow],
            scratch=[sz.narrow, (sz.slots, WIDTH)],
        )[0]
        if edge_sends is not None:
            back, *edge_sends = lax.optimization_barrier((back, *edge_sends))
            edges = swap(*edge_sends)
        back = exchange(back, devices)
        surface, *row_sends = call(
            functools.partial(merge_kernel, sz),
            "merge",
            near_by(back, surface, slope, *got)
            + scalars(table, facts)
            + near_by(diffusivity_surface),
            kept=[sz.surface, row_surface, row_surface],
        )
        surface_edges = swap(*row_sends)
        inputs = (
            anywhere(field)
            + near_by(surface)
            + anywhere(*edges)
            + near_by(*surface_edges)
            + anywhere(drive)
            + near_by(diffusivity, mix)
        )
        if hour > 0:
            field, surface, packed, *sends = call(
                functools.partial(backward_kernel, sz, False),
                "step_back",
                inputs + scalars(table, facts, *told) + near_by(saved[hour - 1][1]),
                shipped=[sz.whole, sz.surface, sz.wide, sz.lats, sz.lats, sz.edge, sz.edge],
                scratch=[sz.whole, sz.whole, wider, sz.near, sz.near, two_row_sems, edge_sems],
            )
            sends, edge_sends = sends[:2], sends[2:]
        else:
            gradient, sums = call(
                functools.partial(backward_kernel, sz, True),
                "step_back_sums",
                inputs + near_by(start_pert),
                shipped=[sz.whole, (devices, WIDTH)],
                scratch=[sz.whole, sz.whole, wider, two_row_sems, edge_sems],
            )

    everyones = lax.all_to_all(sums, "horiz", split_axis=0, concat_axis=0, tiled=True)
    block = perturbation.shape
    return call(
        functools.partial(final_kernel, perturbation.size * devices),
        "finish",
        near_by(everyones) + anywhere(perturbation, gradient.transpose(2, 0, 1, 3)),
        shipped=[block],
        scratch=[block, block, pltpu.SemaphoreType.DMA((2, block[0]))],
    )[0]


def solution(mesh):
    placed = (
        P("member", "horiz", None, None),
        P(None, "horiz", None, None),
        P(None, "horiz", None, None),
        P("horiz", None),
        P("horiz", None),
        P(),
        P(),
        P("horiz", None, None),
        P(None, "horiz", None, None),
        P(None, "horiz", None, None),
        P("horiz", None),
        P("horiz", None),
        P("horiz"),
        P("horiz"),
        P("horiz"),
    )
    return jax.shard_map(
        body,
        mesh=mesh,
        in_specs=placed,
        out_specs=P("member", "horiz", None, None),
        check_vma=False,
    )
```

time: 208 us -> 263 us (1.26)
  Pallas kernels: 18.8 us -> 59.7 us
  starting transfers between devices: 56.7 us -> 84.5 us
  local copies, waits for them, and re-layouts: 20 us -> 35.7 us
  blocking collectives: 65.6 us -> 54.1 us
  waiting for transfers between devices: 32.3 us -> 23.9 us
  other arithmetic: 9.93 us -> 1.92 us
    pallas_call x12 -> x14, Pallas kernels: 18.8 us -> 59.7 us  [the longest x13 55.2 us: call(): pl.pallas_call(run, name=name, in_specs=[pl.BlockSpec(memory_space=space)...]
    ppermute x8 -> x11, starting transfers between devices: 20.6 us -> 37.4 us  [swap(): lax.ppermute(high, 'horiz', upward)]
    all_to_all x1 -> x0, blocking collectives: 14.5 us -> none  [body(): lax.all_to_all(jnp.broadcast_to(local, (devices, WIDTH)), 'horiz', split_...]
    unnamed x68 -> x111, local copies, waits for them, and re-layouts: 13.3 us -> 25.3 us
    all_to_all x0 -> x1, starting transfers between devices: none -> 9.17 us  [body(): lax.all_to_all(sums, 'horiz', split_axis=0, concat_axis=0, tiled=True)]
    all_to_all x5, waiting for transfers between devices: 16.2 us -> 7.61 us  [exchange(): lax.all_to_all(split, 'horiz', split_axis=0, concat_axis=0, tiled=True)]
    all_to_all x0 -> x1, waiting for transfers between devices: none -> 4.8 us  [body(): lax.all_to_all(sums, 'horiz', split_axis=0, concat_axis=0, tiled=True)]
    ppermute x8 -> x11, waiting for transfers between devices: 16 us -> 11.4 us  [swap(): lax.ppermute(low, 'horiz', downward)]
  transfers between devices with their start and end apart: 21 -> 28, of which waited for: 12 -> 8; matrix products, arithmetic and copies ran while one was open for 4% -> 5% of each run, Pallas kernels for 0% -> 3%
where the time goes in v2:
time: 263 us; the launch traced here: 261 us
  starting transfers between devices  84.5 us (32%)
  Pallas kernels  59.7 us (23%)
  blocking collectives  54.1 us (21%)
  local copies, waits for them, and re-layouts  35.7 us (14%)
  waiting for transfers between devices  23.9 us (9%)
    pallas_call x13, Pallas kernels, call(): pl.pallas_call(run, name=name, in_specs=[pl.BlockSpec(memory_space=space)...  55.2 us
    all_to_all x3, blocking collectives, exchange(): lax.all_to_all(split, 'horiz', split_axis=0, concat_axis=0, tiled=True)  54.1 us
    ppermute x11, starting transfers between devices, swap(): lax.ppermute(high, 'horiz', upward)  37.4 us
    unnamed x111, local copies, waits for them, and re-layouts  25.3 us
    all_to_all x5, starting transfers between devices, exchange(): lax.all_to_all(split, 'horiz', split_axis=0, concat_axis=0, tiled=True)  23.4 us
    ppermute x11, starting transfers between devices, swap(): lax.ppermute(low, 'horiz', downward)  14.5 us
    ppermute x11, waiting for transfers between devices, swap(): lax.ppermute(low, 'horiz', downward)  11.4 us
    all_to_all x1, starting transfers between devices, body(): lax.all_to_all(sums, 'horiz', split_axis=0, concat_axis=0, tiled=True)  9.17 us
  transfers between devices with their start and end apart: 28, of which 8 were waited for; matrix products, arithmetic and copies ran while one was open for 5% of the time, Pallas kernels for 3%

profile of v2, /device:TPU:0, one launch (start us, length us, event | category | flops | bytes accessed | tf_op | source)
XLA Modules:
  0.0 260.5 jit_solution(10070839679622914944)
XLA Ops:
  0.0 1.5 copy.52
  2.5 2.4 collective-permute-start
  4.9 1.4 collective-permute-start.1
  6.3 1.2 bitcast_add_fusion.refs_0_
  7.6 4.5 %tables.1 = (s32[256]{0:T(256)}, f32[8,128]{1,0:T(8,128)}) custom-call(s32[1,75]{1,0:T(1,128)} %wet_list.1, s32[1,75]{1,0:T(1,128)} %wet_owner.1, s32[15]{0:T(128)} %remap_src.1, s32[15]{0:T(128)} %remap_tgt.1, f32[15]{0:T(128)} %remap_weight.1, s32[1]{0:T(128)} %bitcast.8.me), custom_call_target="tpu_custom_call" | custom-call | tf_op jit(solution)/shard_map/tables/pallas_call | solution.py:783
  12.2 1.3 copy-done.1
  14.8 8.4 %step.2 = (f32[5,4,8,1920]{3,2,1,0:T(8,128)S(1)}, f32[5,4,8,1920]{3,2,1,0:T(8,128)S(1)}, f32[304,128]{1,0:T(8,128)S(1)}, f32[320,128]{1,0:T(8,128)}, f32[40,128]...) custom-call(f32[5,4,8,1920]{3,2,1,0:T(8,128)S(1)} %copy-done.1, ...), custom_call_target="tpu_custom_call" | custom-call | tf_op jit(solution)/shard_map/step/pallas_call | solution.py:721
  23.3 1.0 copy-done.6
  24.3 1.0 copy-done.8
  26.7 9.3 %all-to-all-start = ((f32[16,5,4,128]{3,2,1,0:T(4,128)}), f32[16,5,4,128]{3,2,1,0:T(4,128)S(1)}, u32[]{:S(2)}, u32[]{:S(2)}) async-start(f32[16,5,4,128]{3,2,1,0:T(4,128)} %bitcast.9), calls=%async_computation | async-start | bytes 327680 | tf_op jit(solution)/shard_map/all_to_all | solution.py:751
  36.9 7.6 %all-to-all-done = f32[16,5,4,128]{3,2,1,0:T(4,128)S(1)} async-done(((f32[16,5,4,128]{3,2,1,0:T(4,128)}), f32[16,5,4,128]{3,2,1,0:T(4,128)S(1)}, u32[]{:S(2)}, u32[]{:S(2)}) %all-to-all-start) | async-done | bytes 163872 | tf_op jit(solution)/shard_map/all_to_all | solution.py:751
  44.5 2.1 owners.2
  47.3 3.5 %all-to-all-start.1 = ((f32[16,8,4,128]{3,2,1,0:T(4,128)}), f32[16,8,4,128]{3,2,1,0:T(4,128)S(1)}, u32[]{:S(2)}, u32[]{:S(2)}) async-start(f32[16,8,4,128]{3,2,1,0:T(4,128)} %bitcast.14), calls=%async_computation.1 | async-start | bytes 524288 | tf_op jit(solution)/shard_map/all_to_all | solution.py:751
  50.8 2.2 collective-permute-start.2
  53.0 1.3 collective-permute-start.3
  54.3 4.2 %collective-permute-start.4 = (f32[40,128]{1,0:T(8,128)}, f32[40,128]{1,0:T(8,128)S(1)}, u32[]{:S(2)}, u32[]{:S(2)}) collective-permute-start(f32[40,128]{1,0:T(8,128)} %get-tuple-element.73), channel_id=1, source_target_pairs={{0,1},{1,2},{2,3},{3,4},{4,5},{5,6},{6,7},{7,8},{8,9},{9,10},{10,1... | collective-permute-start | bytes 61448 | tf_op jit(solution)/shard_map/ppermute | solution.py:745
  58.5 1.3 collective-permute-start.5
  59.8 3.0 %collective-permute-done.5.refs_3_.refs_7_.refs_12_ = f32[40,128]{1,0:T(8,128)S(1)} collective-permute-done((f32[40,128]{1,0:T(8,128)S(1)}, f32[40,128]{1,0:T(8,128)S(1)}, u32[]{:S(2)}, u32[]{:S(2)}) %collective-permute-start.5) | collective-permute-done | bytes 20512 | tf_op jit(solution)/shard_map/ppermute | solution.py:745
  63.8 1.8 surface.2
  66.2 4.4 %collective-permute-start.6 = (f32[60,128]{1,0:T(8,128)S(1)}, f32[60,128]{1,0:T(8,128)S(1)}, u32[]{:S(2)}, u32[]{:S(2)}) collective-permute-start(f32[60,128]{1,0:T(8,128)S(1)} %get-tuple-element.76), channel_id=1, source_target_pairs={{0,1},{1,2},{2,3},{3,4},{4,5},{5,6},{6,7},{7,8},{8,9},{9,10},{10,1... | collective-permute-start | bytes 92168 | tf_op jit(solution)/shard_map/ppermute | solution.py:745
  70.7 1.4 collective-permute-start.7
  72.1 1.4 copy.51
  73.9 9.4 %step.3 = (f32[5,4,8,1920]{3,2,1,0:T(8,128)S(1)}, f32[5,4,8,1920]{3,2,1,0:T(8,128)S(1)}, f32[304,128]{1,0:T(8,128)S(1)}, f32[320,128]{1,0:T(8,128)S(1)}, f32[40,...) custom-call(f32[5,4,8,1920]{3,2,1,0:T(8,128)S(1)} %copy-done.7, ...), custom_call_target="tpu_custom_call" | custom-call | tf_op jit(solution)/shard_map/step/pallas_call | solution.py:721
  83.3 1.0 copy-done.2
  84.3 1.0 copy-done.4
  85.3 17.6 %all_to_all.51 = f32[16,5,4,128]{3,2,1,0:T(4,128)S(1)} all-to-all(f32[16,5,4,128]{3,2,1,0:T(4,128)S(1)} %bitcast.71), channel_id=1, replica_groups=mesh['member'=2,'horiz'=16] {'horiz'}, dimensions={0} | all-to-all | bytes 327680 | tf_op jit(solution)/shard_map/all_to_all | solution.py:751
  102.9 2.1 owners.3
  105.1 3.5 %all-to-all-start.3 = ((f32[16,8,4,128]{3,2,1,0:T(4,128)}), f32[16,8,4,128]{3,2,1,0:T(4,128)S(1)}, u32[]{:S(2)}, u32[]{:S(2)}) async-start(f32[16,8,4,128]{3,2,1,0:T(4,128)} %bitcast.21), calls=%async_computation.3 | async-start | bytes 524288 | tf_op jit(solution)/shard_map/all_to_all | solution.py:751
  108.6 2.8 %collective-permute-start.8 = (f32[40,128]{1,0:T(8,128)}, f32[40,128]{1,0:T(8,128)}, u32[]{:S(2)}, u32[]{:S(2)}) collective-permute-start(f32[40,128]{1,0:T(8,128)} %get-tuple-element.85), channel_id=1, source_target_pairs={{0,1},{1,2},{2,3},{3,4},{4,5},{5,6},{6,7},{7,8},{8,9},{9,10},{10,1... | collective-permute-start | bytes 61448 | tf_op jit(solution)/shard_map/ppermute | solution.py:745
  111.4 1.3 collective-permute-start.9
  112.7 1.6 slice.35
  119.7 2.6 surface.3
  123.6 17.4 %all_to_all.52 = f32[16,8,4,128]{3,2,1,0:T(4,128)S(1)} all-to-all(f32[16,8,4,128]{3,2,1,0:T(4,128)S(1)} %bitcast.70), channel_id=1, replica_groups=mesh['member'=2,'horiz'=16] {'horiz'}, dimensions={0} | all-to-all | bytes 524288 | tf_op jit(solution)/shard_map/all_to_all | solution.py:751
  141.7 1.6 owners_back.2
  143.3 3.5 %all-to-all-start.5 = ((f32[16,5,4,128]{3,2,1,0:T(4,128)}), f32[16,5,4,128]{3,2,1,0:T(4,128)S(1)}, u32[]{:S(2)}, u32[]{:S(2)}) async-start(f32[16,5,4,128]{3,2,1,0:T(4,128)} %bitcast.26), calls=%async_computation.5 | async-start | bytes 327680 | tf_op jit(solution)/shard_map/all_to_all | solution.py:751
  146.9 2.2 collective-permute-start.12
  149.1 1.3 collective-permute-start.13
  150.4 4.2 %collective-permute-start.10 = (f32[32,128]{1,0:T(8,128)S(1)}, f32[32,128]{1,0:T(8,128)S(1)}, u32[]{:S(2)}, u32[]{:S(2)}) collective-permute-start(f32[32,128]{1,0:T(8,128)S(1)} %copy-done.47), channel_id=1, source_target_pairs={{0,1},{1,2},{2,3},{3,4},{4,5},{5,6},{6,7},{7,8},{8,9},{9,10},{10,1... | collective-permute-start | bytes 49160 | tf_op jit(solution)/shard_map/ppermute | solution.py:745
  154.6 1.3 collective-permute-start.11
  157.6 1.5 collective-permute-done.11.refs_4_
  160.7 4.4 %collective-permute-start.14 = (f32[60,128]{1,0:T(8,128)S(1)}, f32[60,128]{1,0:T(8,128)S(1)}, u32[]{:S(2)}, u32[]{:S(2)}) collective-permute-start(f32[60,128]{1,0:T(8,128)S(1)} %get-tuple-element.97), channel_id=1, source_target_pairs={{0,1},{1,2},{2,3},{3,4},{4,5},{5,6},{6,7},{7,8},{8,9},{9,10},{10,1... | collective-permute-start | bytes 92168 | tf_op jit(solution)/shard_map/ppermute | solution.py:745
  165.1 1.3 collective-permute-start.15
  166.5 1.8 collective-permute-done.15.refs_5_
  168.2 1.3 copy-done.3
  169.5 1.3 copy-done.5
  170.8 10.9 %step_back.1 = (f32[5,4,8,1920]{3,2,1,0:T(8,128)S(1)}, f32[304,128]{1,0:T(8,128)S(1)}, f32[512,128]{1,0:T(8,128)S(1)}, f32[32,128]{1,0:T(8,128)S(1)}, f32[32,128...) custom-call(f32[5,4,8,1920]{3,2,1,0:T(8,128)S(1)} %copy-done.3, ...), custom_call_target="tpu_custom_call" | custom-call | tf_op jit(solution)/shard_map/step_back/pallas_call | solution.py:721
  182.8 19.1 %all_to_all.53 = f32[16,8,4,128]{3,2,1,0:T(4,128)S(1)} all-to-all(f32[16,8,4,128]{3,2,1,0:T(4,128)S(1)} %bitcast.69), channel_id=1, replica_groups=mesh['member'=2,'horiz'=16] {'horiz'}, dimensions={0} | all-to-all | bytes 524288 | tf_op jit(solution)/shard_map/all_to_all | solution.py:751
  201.9 1.6 owners_back.3
  203.5 3.5 %all-to-all-start.7 = ((f32[16,5,4,128]{3,2,1,0:T(4,128)}), f32[16,5,4,128]{3,2,1,0:T(4,128)S(1)}, u32[]{:S(2)}, u32[]{:S(2)}) async-start(f32[16,5,4,128]{3,2,1,0:T(4,128)} %bitcast.30), calls=%async_computation.7 | async-start | bytes 327680 | tf_op jit(solution)/shard_map/all_to_all | solution.py:751
  207.0 2.2 collective-permute-start.18
  209.2 1.3 collective-permute-start.19
  210.5 4.2 %collective-permute-start.16 = (f32[32,128]{1,0:T(8,128)S(1)}, f32[32,128]{1,0:T(8,128)S(1)}, u32[]{:S(2)}, u32[]{:S(2)}) collective-permute-start(f32[32,128]{1,0:T(8,128)S(1)} %get-tuple-element.109), channel_id=1, source_target_pairs={{0,1},{1,2},{2,3},{3,4},{4,5},{5,6},{6,7},{7,8},{8,9},{9,10},{10,1... | collective-permute-start | bytes 49160 | tf_op jit(solution)/shard_map/ppermute | solution.py:745
  214.7 1.3 collective-permute-start.17
  216.0 3.0 %collective-permute-done.17.refs_4_ = f32[32,128]{1,0:T(8,128)S(1)} collective-permute-done((f32[32,128]{1,0:T(8,128)S(1)}, f32[32,128]{1,0:T(8,128)S(1)}, u32[]{:S(2)}, u32[]{:S(2)}) %collective-permute-start.17) | collective-permute-done | bytes 16416 | tf_op jit(solution)/shard_map/ppermute | solution.py:745
  220.7 4.4 %collective-permute-start.20 = (f32[60,128]{1,0:T(8,128)S(1)}, f32[60,128]{1,0:T(8,128)S(1)}, u32[]{:S(2)}, u32[]{:S(2)}) collective-permute-start(f32[60,128]{1,0:T(8,128)S(1)} %get-tuple-element.114), channel_id=1, source_target_pairs={{0,1},{1,2},{2,3},{3,4},{4,5},{5,6},{6,7},{7,8},{8,9},{9,10},{10,1... | collective-permute-start | bytes 92168 | tf_op jit(solution)/shard_map/ppermute | solution.py:745
  225.1 1.3 collective-permute-start.21
  226.4 1.8 collective-permute-done.21.refs_5_
  228.2 1.3 copy-done.9
  229.5 1.3 copy-done.11
  230.8 8.7 %step_back_sums.1 = (f32[5,4,8,1920]{3,2,1,0:T(8,128)S(1)}, f32[16,128]{1,0:T(8,128)}) custom-call(f32[5,4,8,1920]{3,2,1,0:T(8,128)S(1)} %copy-done.11, f32[304,128]{1,0:T(8,128)S(1)} %get-tuple-element.111.refs_1_, f32[4,8,1920]{2,1,0:T(8,128)S(1)} %collective-permute-done.18.refs_2_, f32[4,8,1920]{2,1,0:T(8,128)} %collective-permute-done.19.refs_3_, ...), custom_call_target="tpu_custom_call" | custom-call | tf_op jit(solution)/shard_map/step_back_sums/pallas_call | solution.py:721
  240.5 9.2 %all-to-all-start.8 = ((f32[16,1,128]{2,1,0:T(1,128)}), f32[16,1,128]{2,1,0:T(1,128)S(1)}, u32[]{:S(2)}, u32[]{:S(2)}) async-start(f32[16,1,128]{2,1,0:T(1,128)} %bitcast.33), calls=%async_computation.8 | async-start | bytes 16384 | tf_op jit(solution)/shard_map/all_to_all | solution.py:927
  249.6 1.6 copy.50
  251.2 4.8 %all-to-all-done.8 = f32[16,1,128]{2,1,0:T(1,128)S(1)} async-done(((f32[16,1,128]{2,1,0:T(1,128)}), f32[16,1,128]{2,1,0:T(1,128)S(1)}, u32[]{:S(2)}, u32[]{:S(2)}) %all-to-all-start.8) | async-done | bytes 8224 | tf_op jit(solution)/shard_map/all_to_all | solution.py:927
  256.0 4.5 %finish.1 = f32[8,5,4,1920]{3,2,1,0:T(4,128)} custom-call(f32[16,128]{1,0:T(8,128)S(1)} %bitcast.72, f32[8,5,4,1920]{3,2,1,0:T(4,128)S(1)} %copy-done, f32[8,5,4,1920]{3,2,1,0:T(4,128)S(1)} %bitcast.56), custom_call_target="tpu_custom_call" | custom-call | tf_op jit(solution)/shard_map/finish/pallas_call | solution.py:721
  (137 shorter events, 21.7 us)
Async XLA Ops:
  0.0 1.7 copy-start.48
  1.7 4.6 %copy-start = (f32[8,5,4,1920]{3,2,1,0:T(4,128)S(1)}, f32[8,5,4,1920]{3,2,1,0:T(4,128)}, u32[]{:S(2)}) copy-start(f32[8,5,4,1920]{3,2,1,0:T(4,128)} %refs_1_.1) | copy-start | bytes 3686404
  2.5 9.5 %collective-permute-start = (f32[4,8,1920]{2,1,0:T(8,128)}, f32[4,8,1920]{2,1,0:T(8,128)S(1)}, u32[]{:S(2)}, u32[]{:S(2)}) collective-permute-start(f32[4,8,1920]{2,1,0:T(8,128)} %get-tuple-element.120), channel_id=1, source_target_pairs={{0,1},{1,2},{2,3},{3,4},{4,5},{5,6},{6,7},{7,8},{8,9},{9,10},{10,1... | collective-permute-start | bytes 737288 | tf_op jit(solution)/shard_map/ppermute | solution.py:745
  4.9 2.6 %copy-start.51 = (f32[5,1920]{1,0:T(8,128)S(1)}, f32[5,1920]{1,0:T(8,128)}, u32[]{:S(2)}) copy-start(f32[5,1920]{1,0:T(8,128)} %param.19) | copy-start | bytes 115204
  4.9 7.2 %copy-start.53 = (f32[8,4,4]{0,2,1:T(4,128)S(1)}, f32[8,4,4]{0,2,1:T(4,128)}, u32[]{:S(2)}) copy-start(f32[8,4,4]{0,2,1:T(4,128)} %param.20) | copy-start | bytes 1540
  4.9 7.2 %collective-permute-start.1 = (f32[4,8,1920]{2,1,0:T(8,128)S(1)}, f32[4,8,1920]{2,1,0:T(8,128)S(1)}, u32[]{:S(2)}, u32[]{:S(2)}) collective-permute-start(f32[4,8,1920]{2,1,0:T(8,128)S(1)} %get-tuple-element.119), channel_id=1, source_target_pairs={{1,0},{2,1},{3,2},{4,3},{5,4},{6,5},{7,6},{8,7},{9,8},{10,9},{11,1... | collective-permute-start | bytes 737288 | tf_op jit(solution)/shard_map/ppermute | solution.py:745
  12.2 1.3 copy-start.1
  14.8 29.6 %copy-start.13 = (f32[1,80,80]{2,1,0:T(8,128)S(1)}, f32[1,80,80]{2,1,0:T(8,128)}, u32[]{:S(2)}) copy-start(f32[1,80,80]{2,1,0:T(8,128)} %param.22) | copy-start | bytes 76804
  14.8 29.6 %copy-start.34 = (f32[4,4]{1,0:T(4,128)S(1)}, f32[4,4]{1,0:T(4,128)}, u32[]{:S(2)}) copy-start(f32[4,4]{1,0:T(4,128)} %refs_4_.7) | copy-start | bytes 196
  14.8 48.0 %copy-start.15 = (f32[8,128]{1,0:T(8,128)S(1)}, f32[8,128]{1,0:T(8,128)}, u32[]{:S(2)}) copy-start(f32[8,128]{1,0:T(8,128)} %get-tuple-element.63.refs_6_.refs_7_.refs_5_.refs_10_) | copy-start | bytes 12292
  14.8 48.0 %copy-start.33 = (s32[256]{0:T(256)S(1)}, s32[256]{0:T(256)}, u32[]{:S(2)}) copy-start(s32[256]{0:T(256)} %get-tuple-element.62.refs_5_.refs_4_.refs_9_) | copy-start | bytes 3076
  24.3 1.0 copy-start.8
  26.7 17.8 %copy-start.41 = (f32[4,8,1920]{2,1,0:T(8,128)}, f32[4,8,1920]{2,1,0:T(8,128)S(1)}, u32[]{:S(2)}) copy-start(f32[4,8,1920]{2,1,0:T(8,128)S(1)} %get-tuple-element.70) | copy-start | bytes 737284
  26.7 17.8 %all-to-all-start = ((f32[16,5,4,128]{3,2,1,0:T(4,128)}), f32[16,5,4,128]{3,2,1,0:T(4,128)S(1)}, u32[]{:S(2)}, u32[]{:S(2)}) async-start(f32[16,5,4,128]{3,2,1,0:T(4,128)} %bitcast.9), calls=%async_computation | async-start | bytes 327680 | tf_op jit(solution)/shard_map/all_to_all | solution.py:751
  46.6 4.2 %copy-start.18 = (f32[4,80,128]{2,1,0:T(8,128)}, f32[4,80,128]{2,1,0:T(8,128)S(1)}, u32[]{:S(2)}) copy-start(f32[4,80,128]{2,1,0:T(8,128)S(1)} %get-tuple-element.104.refs_3_) | copy-start | bytes 491524
  47.3 15.6 %all-to-all-start.1 = ((f32[16,8,4,128]{3,2,1,0:T(4,128)}), f32[16,8,4,128]{3,2,1,0:T(4,128)S(1)}, u32[]{:S(2)}, u32[]{:S(2)}) async-start(f32[16,8,4,128]{3,2,1,0:T(4,128)} %bitcast.14), calls=%async_computation.1 | async-start | bytes 524288 | tf_op jit(solution)/shard_map/all_to_all | solution.py:751
  50.8 22.7 %collective-permute-start.2 = (f32[4,8,1920]{2,1,0:T(8,128)}, f32[4,8,1920]{2,1,0:T(8,128)S(1)}, u32[]{:S(2)}, u32[]{:S(2)}) collective-permute-start(f32[4,8,1920]{2,1,0:T(8,128)} %copy-done.42), channel_id=1, source_target_pairs={{0,1},{1,2},{2,3},{3,4},{4,5},{5,6},{6,7},{7,8},{8,9},{9,10},{10,1... | collective-permute-start | bytes 737288 | tf_op jit(solution)/shard_map/ppermute | solution.py:745
  53.0 20.5 %collective-permute-start.3 = (f32[4,8,1920]{2,1,0:T(8,128)}, f32[4,8,1920]{2,1,0:T(8,128)S(1)}, u32[]{:S(2)}, u32[]{:S(2)}) collective-permute-start(f32[4,8,1920]{2,1,0:T(8,128)} %copy-done.41), channel_id=1, source_target_pairs={{1,0},{2,1},{3,2},{4,3},{5,4},{6,5},{7,6},{8,7},{9,8},{10,9},{11,1... | collective-permute-start | bytes 737288 | tf_op jit(solution)/shard_map/ppermute | solution.py:745
  54.3 5.5 %collective-permute-start.4 = (f32[40,128]{1,0:T(8,128)}, f32[40,128]{1,0:T(8,128)S(1)}, u32[]{:S(2)}, u32[]{:S(2)}) collective-permute-start(f32[40,128]{1,0:T(8,128)} %get-tuple-element.73), channel_id=1, source_target_pairs={{0,1},{1,2},{2,3},{3,4},{4,5},{5,6},{6,7},{7,8},{8,9},{9,10},{10,1... | collective-permute-start | bytes 61448 | tf_op jit(solution)/shard_map/ppermute | solution.py:745
  58.5 4.3 %collective-permute-start.5 = (f32[40,128]{1,0:T(8,128)S(1)}, f32[40,128]{1,0:T(8,128)S(1)}, u32[]{:S(2)}, u32[]{:S(2)}) collective-permute-start(f32[40,128]{1,0:T(8,128)S(1)} %get-tuple-element.74), channel_id=1, source_target_pairs={{1,0},{2,1},{3,2},{4,3},{5,4},{6,5},{7,6},{8,7},{9,8},{10,9},{11,1... | collective-permute-start | bytes 61448 | tf_op jit(solution)/shard_map/ppermute | solution.py:745
  66.2 7.3 %collective-permute-start.6 = (f32[60,128]{1,0:T(8,128)S(1)}, f32[60,128]{1,0:T(8,128)S(1)}, u32[]{:S(2)}, u32[]{:S(2)}) collective-permute-start(f32[60,128]{1,0:T(8,128)S(1)} %get-tuple-element.76), channel_id=1, source_target_pairs={{0,1},{1,2},{2,3},{3,4},{4,5},{5,6},{6,7},{7,8},{8,9},{9,10},{10,1... | collective-permute-start | bytes 92168 | tf_op jit(solution)/shard_map/ppermute | solution.py:745
  70.6 2.8 %copy-start.49 = (f32[5,1920]{1,0:T(8,128)S(1)}, f32[5,1920]{1,0:T(8,128)}, u32[]{:S(2)}) copy-start(f32[5,1920]{1,0:T(8,128)} %param.18) | copy-start | bytes 115204
  70.6 3.2 %copy-start.7 = (f32[5,4,8,1920]{3,2,1,0:T(8,128)S(1)}, f32[5,4,8,1920]{3,2,1,0:T(8,128)}, u32[]{:S(2)}) copy-start(f32[5,4,8,1920]{3,2,1,0:T(8,128)} %copy-done.6) | copy-start | bytes 3686404
  70.7 3.2 %collective-permute-start.7 = (f32[60,128]{1,0:T(8,128)S(1)}, f32[60,128]{1,0:T(8,128)S(1)}, u32[]{:S(2)}, u32[]{:S(2)}) collective-permute-start(f32[60,128]{1,0:T(8,128)S(1)} %get-tuple-element.77), channel_id=1, source_target_pairs={{1,0},{2,1},{3,2},{4,3},{5,4},{6,5},{7,6},{8,7},{9,8},{10,9},{11,1... | collective-permute-start | bytes 92168 | tf_op jit(solution)/shard_map/ppermute | solution.py:745
  85.3 19.7 %copy-start.24 = (f32[304,128]{1,0:T(8,128)}, f32[304,128]{1,0:T(8,128)S(1)}, u32[]{:S(2)}) copy-start(f32[304,128]{1,0:T(8,128)S(1)} %get-tuple-element.84.refs_1_) | copy-start | bytes 466948
  85.3 19.7 %copy-start.39 = (f32[4,8,1920]{2,1,0:T(8,128)}, f32[4,8,1920]{2,1,0:T(8,128)S(1)}, u32[]{:S(2)}) copy-start(f32[4,8,1920]{2,1,0:T(8,128)S(1)} %get-tuple-element.96) | copy-start | bytes 737284
  85.3 19.7 %copy-start.40 = (f32[4,8,1920]{2,1,0:T(8,128)}, f32[4,8,1920]{2,1,0:T(8,128)S(1)}, u32[]{:S(2)}) copy-start(f32[4,8,1920]{2,1,0:T(8,128)S(1)} %get-tuple-element.95) | copy-start | bytes 737284
  85.3 29.0 %copy-start.50 = (f32[5,1920]{1,0:T(8,128)S(1)}, f32[5,1920]{1,0:T(8,128)}, u32[]{:S(2)}) copy-start(f32[5,1920]{1,0:T(8,128)} %param.18) | copy-start | bytes 115204
  105.0 10.3 %copy-start.20 = (f32[4,80,128]{2,1,0:T(8,128)}, f32[4,80,128]{2,1,0:T(8,128)S(1)}, u32[]{:S(2)}) copy-start(f32[4,80,128]{2,1,0:T(8,128)S(1)} %get-tuple-element.89.refs_3_) | copy-start | bytes 491524
  105.1 13.7 %all-to-all-start.3 = ((f32[16,8,4,128]{3,2,1,0:T(4,128)}), f32[16,8,4,128]{3,2,1,0:T(4,128)S(1)}, u32[]{:S(2)}, u32[]{:S(2)}) async-start(f32[16,8,4,128]{3,2,1,0:T(4,128)} %bitcast.21), calls=%async_computation.3 | async-start | bytes 524288 | tf_op jit(solution)/shard_map/all_to_all | solution.py:751
  108.6 10.2 %collective-permute-start.8 = (f32[40,128]{1,0:T(8,128)}, f32[40,128]{1,0:T(8,128)}, u32[]{:S(2)}, u32[]{:S(2)}) collective-permute-start(f32[40,128]{1,0:T(8,128)} %get-tuple-element.85), channel_id=1, source_target_pairs={{0,1},{1,2},{2,3},{3,4},{4,5},{5,6},{6,7},{7,8},{8,9},{9,10},{10,1... | collective-permute-start | bytes 61448 | tf_op jit(solution)/shard_map/ppermute | solution.py:745
  111.4 7.4 %collective-permute-start.9 = (f32[40,128]{1,0:T(8,128)}, f32[40,128]{1,0:T(8,128)}, u32[]{:S(2)}, u32[]{:S(2)}) collective-permute-start(f32[40,128]{1,0:T(8,128)} %get-tuple-element.86), channel_id=1, source_target_pairs={{1,0},{2,1},{3,2},{4,3},{5,4},{6,5},{7,6},{8,7},{9,8},{10,9},{11,1... | collective-permute-start | bytes 61448 | tf_op jit(solution)/shard_map/ppermute | solution.py:745
  116.1 24.9 %copy-start.21 = (f32[4,80,128]{2,1,0:T(8,128)S(1)}, f32[4,80,128]{2,1,0:T(8,128)}, u32[]{:S(2)}) copy-start(f32[4,80,128]{2,1,0:T(8,128)} %copy-done.20) | copy-start | bytes 491524
  123.5 17.5 %copy-start.28 = (f32[304,128]{1,0:T(8,128)}, f32[304,128]{1,0:T(8,128)S(1)}, u32[]{:S(2)}) copy-start(f32[304,128]{1,0:T(8,128)S(1)} %get-tuple-element.90.refs_1_) | copy-start | bytes 466948
  123.5 19.8 %copy-start.45 = (f32[32,128]{1,0:T(8,128)}, f32[32,128]{1,0:T(8,128)S(1)}, u32[]{:S(2)}) copy-start(f32[32,128]{1,0:T(8,128)S(1)} %get-tuple-element.93) | copy-start | bytes 49156
  123.5 32.3 %copy-start.52 = (f32[5,1920]{1,0:T(8,128)S(1)}, f32[5,1920]{1,0:T(8,128)}, u32[]{:S(2)}) copy-start(f32[5,1920]{1,0:T(8,128)} %param.19) | copy-start | bytes 115204
  123.5 26.8 %copy-start.47 = (f32[32,128]{1,0:T(8,128)S(1)}, f32[32,128]{1,0:T(8,128)}, u32[]{:S(2)}) copy-start(f32[32,128]{1,0:T(8,128)} %copy-done.46) | copy-start | bytes 49156
  123.5 35.5 %copy-start.38 = (f32[64,128]{1,0:T(8,128)S(1)}, f32[64,128]{1,0:T(8,128)}, u32[]{:S(2)}) copy-start(f32[64,128]{1,0:T(8,128)} %copy-done.37) | copy-start | bytes 98308
  141.0 27.2 %copy-start.31 = (f32[64,128]{1,0:T(8,128)S(1)}, f32[64,128]{1,0:T(8,128)}, u32[]{:S(2)}) copy-start(f32[64,128]{1,0:T(8,128)} %copy-done.30) | copy-start | bytes 98308
  143.3 15.8 %all-to-all-start.5 = ((f32[16,5,4,128]{3,2,1,0:T(4,128)}), f32[16,5,4,128]{3,2,1,0:T(4,128)S(1)}, u32[]{:S(2)}, u32[]{:S(2)}) async-start(f32[16,5,4,128]{3,2,1,0:T(4,128)} %bitcast.26), calls=%async_computation.5 | async-start | bytes 327680 | tf_op jit(solution)/shard_map/all_to_all | solution.py:751
  146.9 19.6 %collective-permute-start.12 = (f32[4,8,1920]{2,1,0:T(8,128)}, f32[4,8,1920]{2,1,0:T(8,128)S(1)}, u32[]{:S(2)}, u32[]{:S(2)}) collective-permute-start(f32[4,8,1920]{2,1,0:T(8,128)} %copy-done.40), channel_id=1, source_target_pairs={{0,1},{1,2},{2,3},{3,4},{4,5},{5,6},{6,7},{7,8},{8,9},{9,10},{10,1... | collective-permute-start | bytes 737288 | tf_op jit(solution)/shard_map/ppermute | solution.py:745
  149.1 17.4 %collective-permute-start.13 = (f32[4,8,1920]{2,1,0:T(8,128)}, f32[4,8,1920]{2,1,0:T(8,128)}, u32[]{:S(2)}, u32[]{:S(2)}) collective-permute-start(f32[4,8,1920]{2,1,0:T(8,128)} %copy-done.39), channel_id=1, source_target_pairs={{1,0},{2,1},{3,2},{4,3},{5,4},{6,5},{7,6},{8,7},{9,8},{10,9},{11,1... | collective-permute-start | bytes 737288 | tf_op jit(solution)/shard_map/ppermute | solution.py:745
  150.4 7.2 %collective-permute-start.10 = (f32[32,128]{1,0:T(8,128)S(1)}, f32[32,128]{1,0:T(8,128)S(1)}, u32[]{:S(2)}, u32[]{:S(2)}) collective-permute-start(f32[32,128]{1,0:T(8,128)S(1)} %copy-done.47), channel_id=1, source_target_pairs={{0,1},{1,2},{2,3},{3,4},{4,5},{5,6},{6,7},{7,8},{8,9},{9,10},{10,1... | collective-permute-start | bytes 49160 | tf_op jit(solution)/shard_map/ppermute | solution.py:745
  154.6 4.5 %collective-permute-start.11 = (f32[32,128]{1,0:T(8,128)}, f32[32,128]{1,0:T(8,128)S(1)}, u32[]{:S(2)}, u32[]{:S(2)}) collective-permute-start(f32[32,128]{1,0:T(8,128)} %copy-done.45), channel_id=1, source_target_pairs={{1,0},{2,1},{3,2},{4,3},{5,4},{6,5},{7,6},{8,7},{9,8},{10,9},{11,1... | collective-permute-start | bytes 49160 | tf_op jit(solution)/shard_map/ppermute | solution.py:745
  160.7 5.7 %collective-permute-start.14 = (f32[60,128]{1,0:T(8,128)S(1)}, f32[60,128]{1,0:T(8,128)S(1)}, u32[]{:S(2)}, u32[]{:S(2)}) collective-permute-start(f32[60,128]{1,0:T(8,128)S(1)} %get-tuple-element.97), channel_id=1, source_target_pairs={{0,1},{1,2},{2,3},{3,4},{4,5},{5,6},{6,7},{7,8},{8,9},{9,10},{10,1... | collective-permute-start | bytes 92168 | tf_op jit(solution)/shard_map/ppermute | solution.py:745
  165.1 3.1 %collective-permute-start.15 = (f32[60,128]{1,0:T(8,128)S(1)}, f32[60,128]{1,0:T(8,128)S(1)}, u32[]{:S(2)}, u32[]{:S(2)}) collective-permute-start(f32[60,128]{1,0:T(8,128)S(1)} %get-tuple-element.98), channel_id=1, source_target_pairs={{1,0},{2,1},{3,2},{4,3},{5,4},{6,5},{7,6},{8,7},{9,8},{10,9},{11,1... | collective-permute-start | bytes 92168 | tf_op jit(solution)/shard_map/ppermute | solution.py:745
  168.2 1.3 copy-start.3
  169.5 1.3 copy-start.5
  170.8 31.1 %copy-start.17 = (f32[4,80,128]{2,1,0:T(8,128)S(1)}, f32[4,80,128]{2,1,0:T(8,128)}, u32[]{:S(2)}) copy-start(f32[4,80,128]{2,1,0:T(8,128)} %copy-done.16) | copy-start | bytes 491524
  170.8 31.1 %copy-start.19 = (f32[4,80,128]{2,1,0:T(8,128)S(1)}, f32[4,80,128]{2,1,0:T(8,128)}, u32[]{:S(2)}) copy-start(f32[4,80,128]{2,1,0:T(8,128)} %copy-done.18) | copy-start | bytes 491524
  170.8 31.1 %copy-start.36 = (f32[4,4]{1,0:T(4,128)S(1)}, f32[4,4]{1,0:T(4,128)}, u32[]{:S(2)}) copy-start(f32[4,4]{1,0:T(4,128)} %refs_4_.7) | copy-start | bytes 196
  182.8 20.7 %copy-start.26 = (f32[304,128]{1,0:T(8,128)}, f32[304,128]{1,0:T(8,128)S(1)}, u32[]{:S(2)}) copy-start(f32[304,128]{1,0:T(8,128)S(1)} %get-tuple-element.108.refs_1_) | copy-start | bytes 466948
  182.8 20.7 %copy-start.43 = (f32[4,8,1920]{2,1,0:T(8,128)}, f32[4,8,1920]{2,1,0:T(8,128)S(1)}, u32[]{:S(2)}) copy-start(f32[4,8,1920]{2,1,0:T(8,128)S(1)} %get-tuple-element.113) | copy-start | bytes 737284
  182.8 20.7 %copy-start.44 = (f32[4,8,1920]{2,1,0:T(8,128)}, f32[4,8,1920]{2,1,0:T(8,128)S(1)}, u32[]{:S(2)}) copy-start(f32[4,8,1920]{2,1,0:T(8,128)S(1)} %get-tuple-element.112) | copy-start | bytes 737284
  203.5 15.5 %all-to-all-start.7 = ((f32[16,5,4,128]{3,2,1,0:T(4,128)}), f32[16,5,4,128]{3,2,1,0:T(4,128)S(1)}, u32[]{:S(2)}, u32[]{:S(2)}) async-start(f32[16,5,4,128]{3,2,1,0:T(4,128)} %bitcast.30), calls=%async_computation.7 | async-start | bytes 327680 | tf_op jit(solution)/shard_map/all_to_all | solution.py:751
  207.0 19.3 %collective-permute-start.18 = (f32[4,8,1920]{2,1,0:T(8,128)}, f32[4,8,1920]{2,1,0:T(8,128)S(1)}, u32[]{:S(2)}, u32[]{:S(2)}) collective-permute-start(f32[4,8,1920]{2,1,0:T(8,128)} %copy-done.44), channel_id=1, source_target_pairs={{0,1},{1,2},{2,3},{3,4},{4,5},{5,6},{6,7},{7,8},{8,9},{9,10},{10,1... | collective-permute-start | bytes 737288 | tf_op jit(solution)/shard_map/ppermute | solution.py:745
  209.2 17.1 %collective-permute-start.19 = (f32[4,8,1920]{2,1,0:T(8,128)}, f32[4,8,1920]{2,1,0:T(8,128)}, u32[]{:S(2)}, u32[]{:S(2)}) collective-permute-start(f32[4,8,1920]{2,1,0:T(8,128)} %copy-done.43), channel_id=1, source_target_pairs={{1,0},{2,1},{3,2},{4,3},{5,4},{6,5},{7,6},{8,7},{9,8},{10,9},{11,1... | collective-permute-start | bytes 737288 | tf_op jit(solution)/shard_map/ppermute | solution.py:745
  210.5 5.5 %collective-permute-start.16 = (f32[32,128]{1,0:T(8,128)S(1)}, f32[32,128]{1,0:T(8,128)S(1)}, u32[]{:S(2)}, u32[]{:S(2)}) collective-permute-start(f32[32,128]{1,0:T(8,128)S(1)} %get-tuple-element.109), channel_id=1, source_target_pairs={{0,1},{1,2},{2,3},{3,4},{4,5},{5,6},{6,7},{7,8},{8,9},{9,10},{10,1... | collective-permute-start | bytes 49160 | tf_op jit(solution)/shard_map/ppermute | solution.py:745
  214.7 4.3 %collective-permute-start.17 = (f32[32,128]{1,0:T(8,128)S(1)}, f32[32,128]{1,0:T(8,128)S(1)}, u32[]{:S(2)}, u32[]{:S(2)}) collective-permute-start(f32[32,128]{1,0:T(8,128)S(1)} %get-tuple-element.110), channel_id=1, source_target_pairs={{1,0},{2,1},{3,2},{4,3},{5,4},{6,5},{7,6},{8,7},{9,8},{10,9},{11,1... | collective-permute-start | bytes 49160 | tf_op jit(solution)/shard_map/ppermute | solution.py:745
  220.7 5.7 %collective-permute-start.20 = (f32[60,128]{1,0:T(8,128)S(1)}, f32[60,128]{1,0:T(8,128)S(1)}, u32[]{:S(2)}, u32[]{:S(2)}) collective-permute-start(f32[60,128]{1,0:T(8,128)S(1)} %get-tuple-element.114), channel_id=1, source_target_pairs={{0,1},{1,2},{2,3},{3,4},{4,5},{5,6},{6,7},{7,8},{8,9},{9,10},{10,1... | collective-permute-start | bytes 92168 | tf_op jit(solution)/shard_map/ppermute | solution.py:745
  225.1 3.1 %collective-permute-start.21 = (f32[60,128]{1,0:T(8,128)S(1)}, f32[60,128]{1,0:T(8,128)S(1)}, u32[]{:S(2)}, u32[]{:S(2)}) collective-permute-start(f32[60,128]{1,0:T(8,128)S(1)} %get-tuple-element.115), channel_id=1, source_target_pairs={{1,0},{2,1},{3,2},{4,3},{5,4},{6,5},{7,6},{8,7},{9,8},{10,9},{11,1... | collective-permute-start | bytes 92168 | tf_op jit(solution)/shard_map/ppermute | solution.py:745
  228.2 1.3 copy-start.9
  229.5 1.3 copy-start.11
  240.5 15.6 %all-to-all-start.8 = ((f32[16,1,128]{2,1,0:T(1,128)}), f32[16,1,128]{2,1,0:T(1,128)S(1)}, u32[]{:S(2)}, u32[]{:S(2)}) async-start(f32[16,1,128]{2,1,0:T(1,128)} %bitcast.33), calls=%async_computation.8 | async-start | bytes 16384 | tf_op jit(solution)/shard_map/all_to_all | solution.py:927
  (18 other events, 14.7 us)

commit v3 on v2

--- a/solution.py
+++ b/solution.py
@@ -21,7 +21,7 @@
 ASCENT = 0.5
 EPSILON = 1e-06
 HIGHEST = lax.Precision.HIGHEST
-VMEM_BYTES = 32 * 1024 * 1024
+VMEM_BYTES = 60 * 1024 * 1024
 
 
 class Sizes:
@@ -121,48 +121,34 @@
             target[row, channel, 0:1, cols(tile)] = source[pl.ds(at, 1), :]
 
 
-def tables_kernel(sz, wet_list, wet_owner, remap_src, remap_tgt, remap_weight, me, tile_of, facts, used):
-    def clear(index, carry):
-        tile_of[index] = sz.tiles
-        return carry
-
-    lax.fori_loop(0, tile_of.shape[0], clear, 0)
-
-    def clear_used(index, carry):
-        used[index] = 0
-        return carry
-
-    lax.fori_loop(0, sz.devices, clear_used, 0)
-
-    def place(entry, carry):
-        owner = wet_owner[0, entry]
-        live = owner >= 0
-        owner = jnp.maximum(owner, 0)
-        rank = used[owner]
-        used[owner] = rank + live.astype(jnp.int32)
-        slot = jnp.where(live, owner * sz.capacity + rank, sz.slots)
-        tile_of[slot] = jnp.where(live, wet_list[0, entry], sz.tiles)
-        return carry
-
-    lax.fori_loop(0, wet_list.shape[1], place, 0)
+def as_column(row, size):
+    shape = (size, row.shape[1])
+    diagonal = lax.broadcasted_iota(jnp.int32, shape, 0) == lax.broadcasted_iota(jnp.int32, shape, 1)
+    return jnp.sum(jnp.where(diagonal, row, 0.0), axis=1, keepdims=True)
+
+
+def tables_kernel(sz, entries, remap_entries, wet, remap, table, facts):
+    tiles, owners = wet[0:1, :], wet[1:2, :]
+    size = -(-entries // SUBLANES) * SUBLANES
+    shape = (size, wet.shape[1])
+    tile_here, owner_here = as_column(tiles, size), as_column(owners, size)
+    earlier = lax.broadcasted_iota(jnp.int32, shape, 1) < lax.broadcasted_iota(jnp.int32, shape, 0)
+    same = (owner_here == owners) & earlier
+    rank = jnp.sum(jnp.where(same, 1.0, 0.0), axis=1, keepdims=True)
+    slot = jnp.where(owner_here >= 0.0, owner_here * sz.capacity + rank, -1.0)
+    facts[...] = jnp.zeros(facts.shape, jnp.float32)
     for line in range(sz.slot_lines):
-
-        def tell(index, carry, line=line):
-            facts[line, index] = (sz.tiles - tile_of[line * WIDTH + index]).astype(jnp.float32)
-            return carry
-
-        lax.fori_loop(0, min(WIDTH, sz.slots - line * WIDTH), tell, 0)
-    for index in range(NEAR_LAT * sz.rows):
-        facts[sz.slot_lines, index] = 0.0
-
-    def weigh_entry(entry, carry):
-        lat = remap_tgt[entry] - (me[0] * LAT_DEV - 1)
-        row = remap_src[entry] - me[0] * sz.rows
-        at = lat * sz.rows + row
-        facts[sz.slot_lines, at] = facts[sz.slot_lines, at] + remap_weight[entry]
-        return carry
-
-    lax.fori_loop(0, remap_src.shape[0], weigh_entry, 0)
+        place = lax.broadcasted_iota(jnp.int32, (size, WIDTH), 1) + line * WIDTH
+        match = slot.astype(jnp.int32) == place
+        told = jnp.sum(jnp.where(match, sz.tiles - tile_here, 0.0), axis=0, keepdims=True)
+        facts[line : line + 1, :] = told
+        table[line : line + 1, :] = sz.tiles - told.astype(jnp.int32)
+    size = -(-remap_entries // SUBLANES) * SUBLANES
+    at, weight = as_column(remap[0:1, :], size), as_column(remap[1:2, :], size)
+    place = lax.broadcasted_iota(jnp.int32, (size, WIDTH), 1)
+    facts[sz.slot_lines : sz.slot_lines + 1, :] = jnp.sum(
+        jnp.where(at.astype(jnp.int32) == place, weight, 0.0), axis=0, keepdims=True
+    )
 
 
 class Remap:
@@ -320,7 +306,7 @@
 
 def pack_slots(sz, table, surface, packed):
     for slot in range(sz.slots):
-        at = pl.multiple_of(table[slot] * CHANNELS, CHANNELS)
+        at = pl.multiple_of(table[slot // WIDTH, slot % WIDTH] * CHANNELS, CHANNELS)
         packed[slot * CHANNELS : (slot + 1) * CHANNELS, :] = surface[pl.ds(at, CHANNELS), :]
 
 
@@ -446,7 +432,7 @@
     for slot in range(sz.slots):
         owner, rank = slot // cap, slot % cap
         at = owner * sz.chunk + rank * CHANNELS
-        tile = pl.multiple_of(table[slot] * CHANNELS, CHANNELS)
+        tile = pl.multiple_of(table[slot // WIDTH, slot % WIDTH] * CHANNELS, CHANNELS)
         packed[at : at + CHANNELS, :] = surface[pl.ds(tile, CHANNELS), :]
         at = owner * sz.chunk + sz.own_rows + rank
         packed[at : at + 1, :] = near_low[pl.ds(remap.tile(remap.low, slot), 1), :]
@@ -473,7 +459,7 @@
     for slot in range(sz.slots):
         owner, rank = slot // cap, slot % cap
         at = owner * sz.chunk + rank * CHANNELS
-        tile = pl.multiple_of(table[slot] * CHANNELS, CHANNELS)
+        tile = pl.multiple_of(table[slot // WIDTH, slot % WIDTH] * CHANNELS, CHANNELS)
         block[pl.ds(tile, CHANNELS), :] = (
             before[pl.ds(tile, CHANNELS), :] + flux[at : at + CHANNELS, :]
         )
@@ -518,7 +504,7 @@
     remap = Remap(sz, facts, None, None)
     surface[...] = before[...]
     for slot in range(sz.slots):
-        tile = pl.multiple_of(table[slot] * CHANNELS, CHANNELS)
+        tile = pl.multiple_of(table[slot // WIDTH, slot % WIDTH] * CHANNELS, CHANNELS)
         surface[pl.ds(tile, CHANNELS), :] = (
             before[pl.ds(tile, CHANNELS), :] + back[slot * CHANNELS : (slot + 1) * CHANNELS, :]
         )
@@ -779,18 +765,22 @@
         (perturbation[:, row] + base_state[:, row]).transpose(1, 0, 2) for row in (0, rows - 1)
     ]
     edges = swap(*start)
-    me = lax.axis_index("horiz").astype(jnp.int32).reshape(1)
+    me = lax.axis_index("horiz").astype(jnp.int32)
+
+    def lined(first_row, second_row):
+        size = -(-first_row.shape[0] // WIDTH) * WIDTH
+        pair = jnp.stack([first_row.astype(jnp.float32), second_row.astype(jnp.float32)])
+        return jnp.pad(pair, ((0, 0), (0, size - pair.shape[1])), constant_values=-1.0)
+
+    remap_at = (remap_tgt - (me * LAT_DEV - 1)) * rows + remap_src - me * rows
     table, facts = pl.pallas_call(
-        functools.partial(tables_kernel, sz),
+        functools.partial(tables_kernel, sz, wet_list.shape[1], remap_src.shape[0]),
         name="tables",
-        in_specs=[pl.BlockSpec(memory_space=pltpu.SMEM)] * 6,
-        out_specs=[pl.BlockSpec(memory_space=pltpu.SMEM)] * 2,
         out_shape=[
-            jax.ShapeDtypeStruct((sz.slot_lines * WIDTH + WIDTH,), jnp.int32),
+            jax.ShapeDtypeStruct((sz.slot_lines, WIDTH), jnp.int32),
             jax.ShapeDtypeStruct((sz.facts, WIDTH), jnp.float32),
         ],
-        scratch_shapes=[pltpu.SMEM((devices,), jnp.int32)],
-    )(wet_list, wet_owner, remap_src, remap_tgt, remap_weight, me)
+    )(lined(wet_list[0], wet_owner[0]), lined(remap_at, remap_weight))
 
     mix = jnp.broadcast_to(
         chan_mix.transpose(1, 2, 0).reshape(CHANNELS * CHANNELS, LEVELS, 1),
@@ -838,6 +828,7 @@
         )
         arrived = exchange(packed, devices)
         got = swap(*sends[:2])
+        arrived, *got = lax.optimization_barrier((arrived, *got))
         if first:
             told = got
         flux, mixed_slope, flux_slope = call(
@@ -878,6 +869,7 @@
         drive, slope, mixed_slope, flux_slope = saved[hour]
         arrived = exchange(packed, devices)
         got = swap(*sends)
+        arrived, *got = lax.optimization_barrier((arrived, *got))
         back = call(
             functools.partial(owner_back_kernel, sz),
             "owners_back",

time: 263 us -> 221 us (0.84)
  blocking collectives: 54.1 us -> 0 us
  waiting for transfers between devices: 23.9 us -> 53.7 us
  local copies, waits for them, and re-layouts: 35.7 us -> 19.5 us
  Pallas kernels: 59.7 us -> 47.3 us
  starting transfers between devices: 84.5 us -> 95.5 us
    all_to_all x3 -> x0, blocking collectives: 54.1 us -> none  [exchange(): lax.all_to_all(split, 'horiz', split_axis=0, concat_axis=0, tiled=True)]
    all_to_all x5 -> x8, starting transfers between devices: 23.4 us -> 50.3 us  [exchange(): lax.all_to_all(split, 'horiz', split_axis=0, concat_axis=0, tiled=True)]
    all_to_all x5 -> x8, waiting for transfers between devices: 7.61 us -> 33.8 us  [exchange(): lax.all_to_all(split, 'horiz', split_axis=0, concat_axis=0, tiled=True)]
    ppermute x11, starting transfers between devices: 37.4 us -> 22.9 us  [swap(): lax.ppermute(high, 'horiz', upward)]
    unnamed x111 -> x103, local copies, waits for them, and re-layouts: 25.3 us -> 11.8 us
    pallas_call x13, Pallas kernels: 55.2 us -> 45.8 us  [call(): pl.pallas_call(run, name=name, in_specs=[pl.BlockSpec(memory_space=space)...]
    ppermute x11, waiting for transfers between devices: 11.4 us -> 16.1 us  [swap(): lax.ppermute(low, 'horiz', downward)]
    pallas_call x1, Pallas kernels: 4.49 us -> 1.45 us  [body(): pl.pallas_call(functools.partial(tables_kernel, sz, wet_list.shape[1], re...]
  transfers between devices with their start and end apart: 28 -> 31, of which waited for: 8 -> 17; matrix products, arithmetic and copies ran while one was open for 5% -> 5% of each run, Pallas kernels for 3% -> 4%
where the time goes in v3:
time: 221 us; the launch traced here: 219 us
  starting transfers between devices  95.5 us (43%)
  waiting for transfers between devices  53.7 us (24%)
  Pallas kernels  47.3 us (21%)
  local copies, waits for them, and re-layouts  19.5 us (9%)
    all_to_all x8, starting transfers between devices, exchange(): lax.all_to_all(split, 'horiz', split_axis=0, concat_axis=0, tiled=True)  50.3 us
    pallas_call x13, Pallas kernels, call(): pl.pallas_call(run, name=name, in_specs=[pl.BlockSpec(memory_space=space)...  45.8 us
    all_to_all x8, waiting for transfers between devices, exchange(): lax.all_to_all(split, 'horiz', split_axis=0, concat_axis=0, tiled=True)  33.8 us
    ppermute x11, starting transfers between devices, swap(): lax.ppermute(high, 'horiz', upward)  22.9 us
    ppermute x11, waiting for transfers between devices, swap(): lax.ppermute(low, 'horiz', downward)  16.1 us
    ppermute x11, starting transfers between devices, swap(): lax.ppermute(low, 'horiz', downward)  14.3 us
    unnamed x103, local copies, waits for them, and re-layouts  11.8 us
    all_to_all x1, starting transfers between devices, body(): lax.all_to_all(sums, 'horiz', split_axis=0, concat_axis=0, tiled=True)  7.99 us
  transfers between devices with their start and end apart: 31, of which 17 were waited for; matrix products, arithmetic and copies ran while one was open for 5% of the time, Pallas kernels for 4%

profile of v3, /device:TPU:0, one launch (start us, length us, event | category | flops | bytes accessed | tf_op | source)
XLA Modules:
  0.0 218.7 jit_solution(12150742148896233212)
XLA Ops:
  0.0 1.5 copy.52
  2.8 2.5 %collective-permute-start = (f32[4,8,1920]{2,1,0:T(8,128)S(1)}, f32[4,8,1920]{2,1,0:T(8,128)S(1)}, u32[]{:S(2)}, u32[]{:S(2)}) collective-permute-start(f32[4,8,1920]{2,1,0:T(8,128)S(1)} %get-tuple-element.144), channel_id=1, source_target_pairs={{0,1},{1,2},{2,3},{3,4},{4,5},{5,6},{6,7},{7,8},{8,9},{9,10},{10,1... | collective-permute-start | bytes 737288 | tf_op jit(solution)/shard_map/ppermute | solution.py:731
  5.3 1.3 collective-permute-start.1
  6.7 1.2 bitcast_add_fusion.refs_0_
  9.1 1.5 tables.1
  11.5 5.0 %step.2 = (f32[5,4,8,1920]{3,2,1,0:T(8,128)}, f32[5,4,8,1920]{3,2,1,0:T(8,128)}, f32[304,128]{1,0:T(8,128)}, f32[320,128]{1,0:T(8,128)}, f32[40,128]{1,0:T(8,128...) custom-call(f32[5,4,8,1920]{3,2,1,0:T(8,128)} %bitcast_add_fusion.refs_0_, ...), custom_call_target="tpu_custom_call" | custom-call | tf_op jit(solution)/shard_map/step/pallas_call | solution.py:707
  16.5 10.2 %all-to-all-start = ((f32[16,5,4,128]{3,2,1,0:T(4,128)}), f32[16,5,4,128]{3,2,1,0:T(4,128)S(1)}, u32[]{:S(2)}, u32[]{:S(2)}) async-start(f32[16,5,4,128]{3,2,1,0:T(4,128)} %bitcast.78), calls=%async_computation | async-start | bytes 327680 | tf_op jit(solution)/shard_map/all_to_all | solution.py:737
  26.7 2.3 %collective-permute-start.2 = (f32[40,128]{1,0:T(8,128)}, f32[40,128]{1,0:T(8,128)S(1)}, u32[]{:S(2)}, u32[]{:S(2)}) collective-permute-start(f32[40,128]{1,0:T(8,128)} %get-tuple-element.78), channel_id=1, source_target_pairs={{0,1},{1,2},{2,3},{3,4},{4,5},{5,6},{6,7},{7,8},{8,9},{9,10},{10,1... | collective-permute-start | bytes 61448 | tf_op jit(solution)/shard_map/ppermute | solution.py:731
  29.0 1.3 collective-permute-start.3
  31.0 2.4 %collective-permute-done.3.refs_3_.refs_7_.refs_12_ = f32[40,128]{1,0:T(8,128)S(1)} collective-permute-done((f32[40,128]{1,0:T(8,128)}, f32[40,128]{1,0:T(8,128)S(1)}, u32[]{:S(2)}, u32[]{:S(2)}) %collective-permute-start.3) | collective-permute-done | bytes 20512 | tf_op jit(solution)/shard_map/ppermute | solution.py:731
  33.5 1.7 all-to-all-done
  35.9 2.2 owners.2
  38.0 6.0 %all-to-all-start.1 = ((f32[16,8,4,128]{3,2,1,0:T(4,128)}), f32[16,8,4,128]{3,2,1,0:T(4,128)S(1)}, u32[]{:S(2)}, u32[]{:S(2)}) async-start(f32[16,8,4,128]{3,2,1,0:T(4,128)} %bitcast.77), calls=%async_computation.1 | async-start | bytes 524288 | tf_op jit(solution)/shard_map/all_to_all | solution.py:737
  44.0 2.3 %collective-permute-start.4 = (f32[4,8,1920]{2,1,0:T(8,128)}, f32[4,8,1920]{2,1,0:T(8,128)S(1)}, u32[]{:S(2)}, u32[]{:S(2)}) collective-permute-start(f32[4,8,1920]{2,1,0:T(8,128)} %get-tuple-element.84), channel_id=1, source_target_pairs={{0,1},{1,2},{2,3},{3,4},{4,5},{5,6},{6,7},{7,8},{8,9},{9,10},{10,1... | collective-permute-start | bytes 737288 | tf_op jit(solution)/shard_map/ppermute | solution.py:731
  46.4 1.3 collective-permute-start.5
  47.7 6.4 %all-to-all-done.1 = f32[16,8,4,128]{3,2,1,0:T(4,128)S(1)} async-done(((f32[16,8,4,128]{3,2,1,0:T(4,128)}), f32[16,8,4,128]{3,2,1,0:T(4,128)S(1)}, u32[]{:S(2)}, u32[]{:S(2)}) %all-to-all-start.1) | async-done | bytes 262176 | tf_op jit(solution)/shard_map/all_to_all | solution.py:737
  54.8 3.3 %surface.2 = (f32[304,128]{1,0:T(8,128)}, f32[60,128]{1,0:T(8,128)}, f32[60,128]{1,0:T(8,128)}, f32[64,128]{1,0:T(8,128)}) custom-call(f32[512,128]{1,0:T(8,128)} %bitcast.61, f32[304,128]{1,0:T(8,128)} %get-tuple-element.87.refs_1_, f32[40,128]{1,0:T(8,128)} %copy-done.12, f32[40,128]{1,0:T(8,128)} %copy-done.13, ...), custom_call_target="tpu_custom_call" | custom-call | tf_op jit(solution)/shard_map/surface/pallas_call | solution.py:707
  58.1 1.7 collective-permute-start.6
  59.9 1.4 collective-permute-start.7
  61.3 1.1 copy.51
  64.0 5.7 %step.3 = (f32[5,4,8,1920]{3,2,1,0:T(8,128)}, f32[5,4,8,1920]{3,2,1,0:T(8,128)}, f32[304,128]{1,0:T(8,128)}, f32[320,128]{1,0:T(8,128)}, f32[40,128]{1,0:T(8,128...) custom-call(f32[5,4,8,1920]{3,2,1,0:T(8,128)} %get-tuple-element.76.refs_0_, ...), custom_call_target="tpu_custom_call" | custom-call | tf_op jit(solution)/shard_map/step/pallas_call | solution.py:707
  69.7 7.2 %all-to-all-start.2 = ((f32[16,5,4,128]{3,2,1,0:T(4,128)}), f32[16,5,4,128]{3,2,1,0:T(4,128)S(1)}, u32[]{:S(2)}, u32[]{:S(2)}) async-start(f32[16,5,4,128]{3,2,1,0:T(4,128)} %bitcast.79), calls=%async_computation.2 | async-start | bytes 327680 | tf_op jit(solution)/shard_map/all_to_all | solution.py:737
  76.9 2.3 %collective-permute-start.8 = (f32[40,128]{1,0:T(8,128)}, f32[40,128]{1,0:T(8,128)S(1)}, u32[]{:S(2)}, u32[]{:S(2)}) collective-permute-start(f32[40,128]{1,0:T(8,128)} %get-tuple-element.95), channel_id=1, source_target_pairs={{0,1},{1,2},{2,3},{3,4},{4,5},{5,6},{6,7},{7,8},{8,9},{9,10},{10,1... | collective-permute-start | bytes 61448 | tf_op jit(solution)/shard_map/ppermute | solution.py:731
  79.2 1.3 collective-permute-start.9
  80.5 3.1 %collective-permute-done.9.refs_3_ = f32[40,128]{1,0:T(8,128)S(1)} collective-permute-done((f32[40,128]{1,0:T(8,128)}, f32[40,128]{1,0:T(8,128)S(1)}, u32[]{:S(2)}, u32[]{:S(2)}) %collective-permute-start.9) | collective-permute-done | bytes 20512 | tf_op jit(solution)/shard_map/ppermute | solution.py:731
  83.6 1.7 all-to-all-done.2
  86.0 2.2 owners.3
  88.2 6.0 %all-to-all-start.3 = ((f32[16,8,4,128]{3,2,1,0:T(4,128)}), f32[16,8,4,128]{3,2,1,0:T(4,128)S(1)}, u32[]{:S(2)}, u32[]{:S(2)}) async-start(f32[16,8,4,128]{3,2,1,0:T(4,128)} %bitcast.76), calls=%async_computation.3 | async-start | bytes 524288 | tf_op jit(solution)/shard_map/all_to_all | solution.py:737
  95.9 8.4 %all-to-all-done.3 = f32[16,8,4,128]{3,2,1,0:T(4,128)S(1)} async-done(((f32[16,8,4,128]{3,2,1,0:T(4,128)}), f32[16,8,4,128]{3,2,1,0:T(4,128)S(1)}, u32[]{:S(2)}, u32[]{:S(2)}) %all-to-all-start.3) | async-done | bytes 262176 | tf_op jit(solution)/shard_map/all_to_all | solution.py:737
  104.9 3.2 %surface.3 = (f32[304,128]{1,0:T(8,128)}, f32[64,128]{1,0:T(8,128)}, f32[512,128]{1,0:T(8,128)}, f32[32,128]{1,0:T(8,128)}, f32[32,128]{1,0:T(8,128)}) custom-call(f32[512,128]{1,0:T(8,128)} %bitcast.62, f32[304,128]{1,0:T(8,128)} %get-tuple-element.102.refs_1_, f32[40,128]{1,0:T(8,128)} %copy-done.33, f32[40,128]{1,0:T(8,128)} %copy-done.34, ...), custom_call_target="tpu_custom_call" | custom-call | tf_op jit(solution)/shard_map/surface/pallas_call | solution.py:707
  108.1 3.5 %all-to-all-start.4 = ((f32[16,8,4,128]{3,2,1,0:T(4,128)}), f32[16,8,4,128]{3,2,1,0:T(4,128)S(1)}, u32[]{:S(2)}, u32[]{:S(2)}) async-start(f32[16,8,4,128]{3,2,1,0:T(4,128)} %bitcast.75), calls=%async_computation.4 | async-start | bytes 524288 | tf_op jit(solution)/shard_map/all_to_all | solution.py:737
  111.7 2.2 collective-permute-start.10
  113.9 1.3 collective-permute-start.11
  115.2 3.1 %collective-permute-done.11.refs_4_ = f32[32,128]{1,0:T(8,128)S(1)} collective-permute-done((f32[32,128]{1,0:T(8,128)}, f32[32,128]{1,0:T(8,128)S(1)}, u32[]{:S(2)}, u32[]{:S(2)}) %collective-permute-start.11) | collective-permute-done | bytes 16416 | tf_op jit(solution)/shard_map/ppermute | solution.py:731
  118.3 3.4 %all-to-all-done.4 = f32[16,8,4,128]{3,2,1,0:T(4,128)S(1)} async-done(((f32[16,8,4,128]{3,2,1,0:T(4,128)}), f32[16,8,4,128]{3,2,1,0:T(4,128)S(1)}, u32[]{:S(2)}, u32[]{:S(2)}) %all-to-all-start.4) | async-done | bytes 262176 | tf_op jit(solution)/shard_map/all_to_all | solution.py:737
  122.4 2.1 owners_back.2
  124.5 4.3 %all-to-all-start.5 = ((f32[16,5,4,128]{3,2,1,0:T(4,128)}), f32[16,5,4,128]{3,2,1,0:T(4,128)S(1)}, u32[]{:S(2)}, u32[]{:S(2)}) async-start(f32[16,5,4,128]{3,2,1,0:T(4,128)} %bitcast.72), calls=%async_computation.5 | async-start | bytes 327680 | tf_op jit(solution)/shard_map/all_to_all | solution.py:737
  128.9 2.3 %collective-permute-start.12 = (f32[4,8,1920]{2,1,0:T(8,128)S(1)}, f32[4,8,1920]{2,1,0:T(8,128)S(1)}, u32[]{:S(2)}, u32[]{:S(2)}) collective-permute-start(f32[4,8,1920]{2,1,0:T(8,128)S(1)} %copy-done.44), channel_id=1, source_target_pairs={{0,1},{1,2},{2,3},{3,4},{4,5},{5,6},{6,7},{7,8},{8,9},{9,10},{10,1... | collective-permute-start | bytes 737288 | tf_op jit(solution)/shard_map/ppermute | solution.py:731
  131.2 1.3 collective-permute-start.13
  133.3 4.0 %all-to-all-done.5 = f32[16,5,4,128]{3,2,1,0:T(4,128)S(1)} async-done(((f32[16,5,4,128]{3,2,1,0:T(4,128)}), f32[16,5,4,128]{3,2,1,0:T(4,128)S(1)}, u32[]{:S(2)}, u32[]{:S(2)}) %all-to-all-start.5) | async-done | bytes 163872 | tf_op jit(solution)/shard_map/all_to_all | solution.py:737
  138.0 1.9 merge.2
  140.0 1.3 collective-permute-start.14
  141.2 1.3 collective-permute-start.15
  142.6 2.0 collective-permute-done.15.refs_5_
  145.2 6.6 %step_back.1 = (f32[5,4,8,1920]{3,2,1,0:T(8,128)}, f32[304,128]{1,0:T(8,128)}, f32[512,128]{1,0:T(8,128)}, f32[32,128]{1,0:T(8,128)}, f32[32,128]{1,0:T(8,128)},...) custom-call(f32[5,4,8,1920]{3,2,1,0:T(8,128)} %get-tuple-element.93.refs_0_, f32[304,128]{1,0:T(8,128)} %get-tuple-element.115.refs_1_, ...), custom_call_target="tpu_custom_call" | custom-call | tf_op jit(solution)/shard_map/step_back/pallas_call | solution.py:707
  151.9 8.8 %all-to-all-start.6 = ((f32[16,8,4,128]{3,2,1,0:T(4,128)}), f32[16,8,4,128]{3,2,1,0:T(4,128)S(1)}, u32[]{:S(2)}, u32[]{:S(2)}) async-start(f32[16,8,4,128]{3,2,1,0:T(4,128)} %bitcast.74), calls=%async_computation.6 | async-start | bytes 524288 | tf_op jit(solution)/shard_map/all_to_all | solution.py:737
  160.7 2.3 %collective-permute-start.16 = (f32[32,128]{1,0:T(8,128)}, f32[32,128]{1,0:T(8,128)S(1)}, u32[]{:S(2)}, u32[]{:S(2)}) collective-permute-start(f32[32,128]{1,0:T(8,128)} %get-tuple-element.124), channel_id=1, source_target_pairs={{0,1},{1,2},{2,3},{3,4},{4,5},{5,6},{6,7},{7,8},{8,9},{9,10},{10,1... | collective-permute-start | bytes 49160 | tf_op jit(solution)/shard_map/ppermute | solution.py:731
  163.0 1.3 collective-permute-start.17
  164.4 3.1 %collective-permute-done.17.refs_4_ = f32[32,128]{1,0:T(8,128)S(1)} collective-permute-done((f32[32,128]{1,0:T(8,128)}, f32[32,128]{1,0:T(8,128)S(1)}, u32[]{:S(2)}, u32[]{:S(2)}) %collective-permute-start.17) | collective-permute-done | bytes 16416 | tf_op jit(solution)/shard_map/ppermute | solution.py:731
  167.5 3.3 %all-to-all-done.6 = f32[16,8,4,128]{3,2,1,0:T(4,128)S(1)} async-done(((f32[16,8,4,128]{3,2,1,0:T(4,128)}), f32[16,8,4,128]{3,2,1,0:T(4,128)S(1)}, u32[]{:S(2)}, u32[]{:S(2)}) %all-to-all-start.6) | async-done | bytes 262176 | tf_op jit(solution)/shard_map/all_to_all | solution.py:737
  171.5 2.1 owners_back.3
  173.6 4.3 %all-to-all-start.7 = ((f32[16,5,4,128]{3,2,1,0:T(4,128)}), f32[16,5,4,128]{3,2,1,0:T(4,128)S(1)}, u32[]{:S(2)}, u32[]{:S(2)}) async-start(f32[16,5,4,128]{3,2,1,0:T(4,128)} %bitcast.73), calls=%async_computation.7 | async-start | bytes 327680 | tf_op jit(solution)/shard_map/all_to_all | solution.py:737
  178.0 2.3 %collective-permute-start.18 = (f32[4,8,1920]{2,1,0:T(8,128)S(1)}, f32[4,8,1920]{2,1,0:T(8,128)S(1)}, u32[]{:S(2)}, u32[]{:S(2)}) collective-permute-start(f32[4,8,1920]{2,1,0:T(8,128)S(1)} %copy-done.47), channel_id=1, source_target_pairs={{0,1},{1,2},{2,3},{3,4},{4,5},{5,6},{6,7},{7,8},{8,9},{9,10},{10,1... | collective-permute-start | bytes 737288 | tf_op jit(solution)/shard_map/ppermute | solution.py:731
  180.3 1.3 collective-permute-start.19
  181.6 4.8 %all-to-all-done.7 = f32[16,5,4,128]{3,2,1,0:T(4,128)S(1)} async-done(((f32[16,5,4,128]{3,2,1,0:T(4,128)}), f32[16,5,4,128]{3,2,1,0:T(4,128)S(1)}, u32[]{:S(2)}, u32[]{:S(2)}) %all-to-all-start.7) | async-done | bytes 163872 | tf_op jit(solution)/shard_map/all_to_all | solution.py:737
  187.1 1.9 merge.3
  189.0 1.3 collective-permute-start.20
  190.3 1.3 collective-permute-start.21
  191.7 1.9 collective-permute-done.21.refs_5_
  194.2 6.2 %step_back_sums.1 = (f32[5,4,8,1920]{3,2,1,0:T(8,128)}, f32[16,128]{1,0:T(8,128)}) custom-call(f32[5,4,8,1920]{3,2,1,0:T(8,128)} %get-tuple-element.122.refs_0_, f32[304,128]{1,0:T(8,128)} %get-tuple-element.135.refs_1_, f32[4,8,1920]{2,1,0:T(8,128)} %copy-done.17, f32[4,8,1920]{2,1,0:T(8,128)} %copy-done.19, f32[60,128]{1,0:T(8,128)} %copy-done.29, ...), custom_call_target="tpu_custom_call" | custom-call | tf_op jit(solution)/shard_map/step_back_sums/pallas_call | solution.py:707
  200.4 8.0 %all-to-all-start.8 = ((f32[16,1,128]{2,1,0:T(1,128)}), f32[16,1,128]{2,1,0:T(1,128)S(1)}, u32[]{:S(2)}, u32[]{:S(2)}) async-start(f32[16,1,128]{2,1,0:T(1,128)} %bitcast.82), calls=%async_computation.8 | async-start | bytes 16384 | tf_op jit(solution)/shard_map/all_to_all | solution.py:919
  208.4 2.6 %copy.50 = f32[5,4,8,1920]{3,1,0,2:T(4,128)} copy(f32[5,4,8,1920]{3,2,1,0:T(8,128)} %get-tuple-element.142) | data formatting | bytes 2457600 | tf_op jit(solution)/shard_map/step_back_sums/pallas_call | solution.py:707
  211.1 3.8 %all-to-all-done.8 = f32[16,1,128]{2,1,0:T(1,128)S(1)} async-done(((f32[16,1,128]{2,1,0:T(1,128)}), f32[16,1,128]{2,1,0:T(1,128)S(1)}, u32[]{:S(2)}, u32[]{:S(2)}) %all-to-all-start.8) | async-done | bytes 8224 | tf_op jit(solution)/shard_map/all_to_all | solution.py:919
  215.4 3.3 %finish.1 = f32[8,5,4,1920]{3,2,1,0:T(4,128)} custom-call(f32[16,128]{1,0:T(8,128)} %bitcast.80, f32[8,5,4,1920]{3,2,1,0:T(4,128)} %refs_1_.1, f32[8,5,4,1920]{3,2,1,0:T(4,128)} %bitcast.57), custom_call_target="tpu_custom_call" | custom-call | tf_op jit(solution)/shard_map/finish/pallas_call | solution.py:707
  (137 shorter events, 15.4 us)
Async XLA Ops:
  0.0 1.7 copy-start.2
  2.7 3.9 %copy-start = (f32[8,5,4,1920]{3,2,1,0:T(4,128)S(1)}, f32[8,5,4,1920]{3,2,1,0:T(4,128)}, u32[]{:S(2)}) copy-start(f32[8,5,4,1920]{3,2,1,0:T(4,128)} %refs_1_.1) | copy-start | bytes 3686404
  2.8 7.8 %collective-permute-start = (f32[4,8,1920]{2,1,0:T(8,128)S(1)}, f32[4,8,1920]{2,1,0:T(8,128)S(1)}, u32[]{:S(2)}, u32[]{:S(2)}) collective-permute-start(f32[4,8,1920]{2,1,0:T(8,128)S(1)} %get-tuple-element.144), channel_id=1, source_target_pairs={{0,1},{1,2},{2,3},{3,4},{4,5},{5,6},{6,7},{7,8},{8,9},{9,10},{10,1... | collective-permute-start | bytes 737288 | tf_op jit(solution)/shard_map/ppermute | solution.py:731
  5.3 5.5 %collective-permute-start.1 = (f32[4,8,1920]{2,1,0:T(8,128)S(1)}, f32[4,8,1920]{2,1,0:T(8,128)S(1)}, u32[]{:S(2)}, u32[]{:S(2)}) collective-permute-start(f32[4,8,1920]{2,1,0:T(8,128)S(1)} %get-tuple-element.143), channel_id=1, source_target_pairs={{1,0},{2,1},{3,2},{4,3},{5,4},{6,5},{7,6},{8,7},{9,8},{10,9},{11,1... | collective-permute-start | bytes 737288 | tf_op jit(solution)/shard_map/ppermute | solution.py:731
  6.6 1.3 copy-start.48
  6.6 1.3 copy-start.49
  6.6 1.3 copy-start.23
  6.6 1.9 copy-start.40
  6.6 1.9 copy-start.41
  6.6 1.9 copy-start.42
  6.6 4.1 %copy-start.39 = (f32[8,4,4]{0,2,1:T(4,128)S(1)}, f32[8,4,4]{0,2,1:T(4,128)}, u32[]{:S(2)}) copy-start(f32[8,4,4]{0,2,1:T(4,128)} %param.20) | copy-start | bytes 1540
  7.8 22.5 %copy-start.24 = (f32[2,1,80,128]{3,2,1,0:T(8,128)S(1)}, f32[2,1,80,128]{3,2,1,0:T(8,128)}, u32[]{:S(2)}) copy-start(f32[2,1,80,128]{3,2,1,0:T(8,128)} %param.24) | copy-start | bytes 245764
  7.8 22.5 %copy-start.25 = (f32[2,1,80,128]{3,2,1,0:T(8,128)S(1)}, f32[2,1,80,128]{3,2,1,0:T(8,128)}, u32[]{:S(2)}) copy-start(f32[2,1,80,128]{3,2,1,0:T(8,128)} %param.23) | copy-start | bytes 245764
  16.5 29.8 %copy-start.46 = (f32[4,8,1920]{2,1,0:T(8,128)S(1)}, f32[4,8,1920]{2,1,0:T(8,128)}, u32[]{:S(2)}) copy-start(f32[4,8,1920]{2,1,0:T(8,128)} %get-tuple-element.85) | copy-start | bytes 737284
  16.5 44.8 %copy-start.3 = (f32[8,5,4,1920]{3,2,1,0:T(4,128)S(1)}, f32[8,5,4,1920]{3,2,1,0:T(4,128)}, u32[]{:S(2)}) copy-start(f32[8,5,4,1920]{3,2,1,0:T(4,128)} %param.17) | copy-start | bytes 3686404
  16.5 18.7 %all-to-all-start = ((f32[16,5,4,128]{3,2,1,0:T(4,128)}), f32[16,5,4,128]{3,2,1,0:T(4,128)S(1)}, u32[]{:S(2)}, u32[]{:S(2)}) async-start(f32[16,5,4,128]{3,2,1,0:T(4,128)} %bitcast.78), calls=%async_computation | async-start | bytes 327680 | tf_op jit(solution)/shard_map/all_to_all | solution.py:737
  26.7 4.3 %collective-permute-start.2 = (f32[40,128]{1,0:T(8,128)}, f32[40,128]{1,0:T(8,128)S(1)}, u32[]{:S(2)}, u32[]{:S(2)}) collective-permute-start(f32[40,128]{1,0:T(8,128)} %get-tuple-element.78), channel_id=1, source_target_pairs={{0,1},{1,2},{2,3},{3,4},{4,5},{5,6},{6,7},{7,8},{8,9},{9,10},{10,1... | collective-permute-start | bytes 61448 | tf_op jit(solution)/shard_map/ppermute | solution.py:731
  29.0 4.4 %collective-permute-start.3 = (f32[40,128]{1,0:T(8,128)}, f32[40,128]{1,0:T(8,128)S(1)}, u32[]{:S(2)}, u32[]{:S(2)}) collective-permute-start(f32[40,128]{1,0:T(8,128)} %get-tuple-element.79), channel_id=1, source_target_pairs={{1,0},{2,1},{3,2},{4,3},{5,4},{6,5},{7,6},{8,7},{9,8},{10,9},{11,1... | collective-permute-start | bytes 61448 | tf_op jit(solution)/shard_map/ppermute | solution.py:731
  31.0 23.0 %copy-start.12 = (f32[40,128]{1,0:T(8,128)}, f32[40,128]{1,0:T(8,128)S(1)}, u32[]{:S(2)}) copy-start(f32[40,128]{1,0:T(8,128)S(1)} %collective-permute-done.2.refs_2_.refs_6_.refs_11_) | copy-start | bytes 61444
  33.5 20.6 %copy-start.13 = (f32[40,128]{1,0:T(8,128)}, f32[40,128]{1,0:T(8,128)S(1)}, u32[]{:S(2)}) copy-start(f32[40,128]{1,0:T(8,128)S(1)} %collective-permute-done.3.refs_3_.refs_7_.refs_12_) | copy-start | bytes 61444
  38.0 16.0 %all-to-all-start.1 = ((f32[16,8,4,128]{3,2,1,0:T(4,128)}), f32[16,8,4,128]{3,2,1,0:T(4,128)S(1)}, u32[]{:S(2)}, u32[]{:S(2)}) async-start(f32[16,8,4,128]{3,2,1,0:T(4,128)} %bitcast.77), calls=%async_computation.1 | async-start | bytes 524288 | tf_op jit(solution)/shard_map/all_to_all | solution.py:737
  44.0 19.1 %collective-permute-start.4 = (f32[4,8,1920]{2,1,0:T(8,128)}, f32[4,8,1920]{2,1,0:T(8,128)S(1)}, u32[]{:S(2)}, u32[]{:S(2)}) collective-permute-start(f32[4,8,1920]{2,1,0:T(8,128)} %get-tuple-element.84), channel_id=1, source_target_pairs={{0,1},{1,2},{2,3},{3,4},{4,5},{5,6},{6,7},{7,8},{8,9},{9,10},{10,1... | collective-permute-start | bytes 737288 | tf_op jit(solution)/shard_map/ppermute | solution.py:731
  46.4 16.7 %collective-permute-start.5 = (f32[4,8,1920]{2,1,0:T(8,128)S(1)}, f32[4,8,1920]{2,1,0:T(8,128)S(1)}, u32[]{:S(2)}, u32[]{:S(2)}) collective-permute-start(f32[4,8,1920]{2,1,0:T(8,128)S(1)} %copy-done.46), channel_id=1, source_target_pairs={{1,0},{2,1},{3,2},{4,3},{5,4},{6,5},{7,6},{8,7},{9,8},{10,9},{11,1... | collective-permute-start | bytes 737288 | tf_op jit(solution)/shard_map/ppermute | solution.py:731
  58.1 5.0 %collective-permute-start.6 = (f32[60,128]{1,0:T(8,128)}, f32[60,128]{1,0:T(8,128)S(1)}, u32[]{:S(2)}, u32[]{:S(2)}) collective-permute-start(f32[60,128]{1,0:T(8,128)} %get-tuple-element.91), channel_id=1, source_target_pairs={{0,1},{1,2},{2,3},{3,4},{4,5},{5,6},{6,7},{7,8},{8,9},{9,10},{10,1... | collective-permute-start | bytes 92168 | tf_op jit(solution)/shard_map/ppermute | solution.py:731
  59.9 2.6 %copy-start.22 = (f32[5,1920]{1,0:T(8,128)S(1)}, f32[5,1920]{1,0:T(8,128)}, u32[]{:S(2)}) copy-start(f32[5,1920]{1,0:T(8,128)} %param.18) | copy-start | bytes 115204
  59.9 3.4 %collective-permute-start.7 = (f32[60,128]{1,0:T(8,128)}, f32[60,128]{1,0:T(8,128)S(1)}, u32[]{:S(2)}, u32[]{:S(2)}) collective-permute-start(f32[60,128]{1,0:T(8,128)} %get-tuple-element.92), channel_id=1, source_target_pairs={{1,0},{2,1},{3,2},{4,3},{5,4},{6,5},{7,6},{8,7},{9,8},{10,9},{11,1... | collective-permute-start | bytes 92168 | tf_op jit(solution)/shard_map/ppermute | solution.py:731
  69.7 24.5 %slice-start = ((f32[8,5,4,1920]{3,2,1,0:T(4,128)}), f32[1,5,4,1920]{3,2,1,0:T(4,128)S(1)}, s32[]{:S(2)}) async-start(f32[8,5,4,1920]{3,2,1,0:T(4,128)} %param.17), calls=%async_computation.9 | async-start | bytes 307200 | tf_op jit(solution)/shard_map/slice | solution.py:792
  69.7 15.6 %all-to-all-start.2 = ((f32[16,5,4,128]{3,2,1,0:T(4,128)}), f32[16,5,4,128]{3,2,1,0:T(4,128)S(1)}, u32[]{:S(2)}, u32[]{:S(2)}) async-start(f32[16,5,4,128]{3,2,1,0:T(4,128)} %bitcast.79), calls=%async_computation.2 | async-start | bytes 327680 | tf_op jit(solution)/shard_map/all_to_all | solution.py:737
  76.9 3.6 %collective-permute-start.8 = (f32[40,128]{1,0:T(8,128)}, f32[40,128]{1,0:T(8,128)S(1)}, u32[]{:S(2)}, u32[]{:S(2)}) collective-permute-start(f32[40,128]{1,0:T(8,128)} %get-tuple-element.95), channel_id=1, source_target_pairs={{0,1},{1,2},{2,3},{3,4},{4,5},{5,6},{6,7},{7,8},{8,9},{9,10},{10,1... | collective-permute-start | bytes 61448 | tf_op jit(solution)/shard_map/ppermute | solution.py:731
  79.2 4.4 %collective-permute-start.9 = (f32[40,128]{1,0:T(8,128)}, f32[40,128]{1,0:T(8,128)S(1)}, u32[]{:S(2)}, u32[]{:S(2)}) collective-permute-start(f32[40,128]{1,0:T(8,128)} %get-tuple-element.96), channel_id=1, source_target_pairs={{1,0},{2,1},{3,2},{4,3},{5,4},{6,5},{7,6},{8,7},{9,8},{10,9},{11,1... | collective-permute-start | bytes 61448 | tf_op jit(solution)/shard_map/ppermute | solution.py:731
  80.5 23.7 %copy-start.33 = (f32[40,128]{1,0:T(8,128)}, f32[40,128]{1,0:T(8,128)S(1)}, u32[]{:S(2)}) copy-start(f32[40,128]{1,0:T(8,128)S(1)} %collective-permute-done.8.refs_2_) | copy-start | bytes 61444
  83.6 20.6 %copy-start.34 = (f32[40,128]{1,0:T(8,128)}, f32[40,128]{1,0:T(8,128)S(1)}, u32[]{:S(2)}) copy-start(f32[40,128]{1,0:T(8,128)S(1)} %collective-permute-done.9.refs_3_) | copy-start | bytes 61444
  88.2 16.0 %all-to-all-start.3 = ((f32[16,8,4,128]{3,2,1,0:T(4,128)}), f32[16,8,4,128]{3,2,1,0:T(4,128)S(1)}, u32[]{:S(2)}, u32[]{:S(2)}) async-start(f32[16,8,4,128]{3,2,1,0:T(4,128)} %bitcast.76), calls=%async_computation.3 | async-start | bytes 524288 | tf_op jit(solution)/shard_map/all_to_all | solution.py:737
  104.9 24.0 %copy-start.44 = (f32[4,8,1920]{2,1,0:T(8,128)S(1)}, f32[4,8,1920]{2,1,0:T(8,128)}, u32[]{:S(2)}) copy-start(f32[4,8,1920]{2,1,0:T(8,128)} %get-tuple-element.116) | copy-start | bytes 737284
  104.9 26.3 %copy-start.43 = (f32[4,8,1920]{2,1,0:T(8,128)S(1)}, f32[4,8,1920]{2,1,0:T(8,128)}, u32[]{:S(2)}) copy-start(f32[4,8,1920]{2,1,0:T(8,128)} %get-tuple-element.117) | copy-start | bytes 737284
  108.1 13.6 %all-to-all-start.4 = ((f32[16,8,4,128]{3,2,1,0:T(4,128)}), f32[16,8,4,128]{3,2,1,0:T(4,128)S(1)}, u32[]{:S(2)}, u32[]{:S(2)}) async-start(f32[16,8,4,128]{3,2,1,0:T(4,128)} %bitcast.75), calls=%async_computation.4 | async-start | bytes 524288 | tf_op jit(solution)/shard_map/all_to_all | solution.py:737
  111.7 3.5 %collective-permute-start.10 = (f32[32,128]{1,0:T(8,128)}, f32[32,128]{1,0:T(8,128)S(1)}, u32[]{:S(2)}, u32[]{:S(2)}) collective-permute-start(f32[32,128]{1,0:T(8,128)} %get-tuple-element.106), channel_id=1, source_target_pairs={{0,1},{1,2},{2,3},{3,4},{4,5},{5,6},{6,7},{7,8},{8,9},{9,10},{10,1... | collective-permute-start | bytes 49160 | tf_op jit(solution)/shard_map/ppermute | solution.py:731
  113.9 4.4 %collective-permute-start.11 = (f32[32,128]{1,0:T(8,128)}, f32[32,128]{1,0:T(8,128)S(1)}, u32[]{:S(2)}, u32[]{:S(2)}) collective-permute-start(f32[32,128]{1,0:T(8,128)} %get-tuple-element.107), channel_id=1, source_target_pairs={{1,0},{2,1},{3,2},{4,3},{5,4},{6,5},{7,6},{8,7},{9,8},{10,9},{11,1... | collective-permute-start | bytes 49160 | tf_op jit(solution)/shard_map/ppermute | solution.py:731
  115.2 22.2 %copy-start.35 = (f32[32,128]{1,0:T(8,128)}, f32[32,128]{1,0:T(8,128)S(1)}, u32[]{:S(2)}) copy-start(f32[32,128]{1,0:T(8,128)S(1)} %collective-permute-done.10.refs_3_) | copy-start | bytes 49156
  118.3 19.0 %copy-start.36 = (f32[32,128]{1,0:T(8,128)}, f32[32,128]{1,0:T(8,128)S(1)}, u32[]{:S(2)}) copy-start(f32[32,128]{1,0:T(8,128)S(1)} %collective-permute-done.11.refs_4_) | copy-start | bytes 49156
  124.5 12.8 %all-to-all-start.5 = ((f32[16,5,4,128]{3,2,1,0:T(4,128)}), f32[16,5,4,128]{3,2,1,0:T(4,128)S(1)}, u32[]{:S(2)}, u32[]{:S(2)}) async-start(f32[16,5,4,128]{3,2,1,0:T(4,128)} %bitcast.72), calls=%async_computation.5 | async-start | bytes 327680 | tf_op jit(solution)/shard_map/all_to_all | solution.py:737
  128.9 13.7 %collective-permute-start.12 = (f32[4,8,1920]{2,1,0:T(8,128)S(1)}, f32[4,8,1920]{2,1,0:T(8,128)S(1)}, u32[]{:S(2)}, u32[]{:S(2)}) collective-permute-start(f32[4,8,1920]{2,1,0:T(8,128)S(1)} %copy-done.44), channel_id=1, source_target_pairs={{0,1},{1,2},{2,3},{3,4},{4,5},{5,6},{6,7},{7,8},{8,9},{9,10},{10,1... | collective-permute-start | bytes 737288 | tf_op jit(solution)/shard_map/ppermute | solution.py:731
  131.2 11.3 %collective-permute-start.13 = (f32[4,8,1920]{2,1,0:T(8,128)S(1)}, f32[4,8,1920]{2,1,0:T(8,128)S(1)}, u32[]{:S(2)}, u32[]{:S(2)}) collective-permute-start(f32[4,8,1920]{2,1,0:T(8,128)S(1)} %copy-done.43), channel_id=1, source_target_pairs={{1,0},{2,1},{3,2},{4,3},{5,4},{6,5},{7,6},{8,7},{9,8},{10,9},{11,1... | collective-permute-start | bytes 737288 | tf_op jit(solution)/shard_map/ppermute | solution.py:731
  140.0 2.6 %collective-permute-start.14 = (f32[60,128]{1,0:T(8,128)}, f32[60,128]{1,0:T(8,128)S(1)}, u32[]{:S(2)}, u32[]{:S(2)}) collective-permute-start(f32[60,128]{1,0:T(8,128)} %get-tuple-element.118), channel_id=1, source_target_pairs={{0,1},{1,2},{2,3},{3,4},{4,5},{5,6},{6,7},{7,8},{8,9},{9,10},{10,1... | collective-permute-start | bytes 92168 | tf_op jit(solution)/shard_map/ppermute | solution.py:731
  141.2 3.4 %collective-permute-start.15 = (f32[60,128]{1,0:T(8,128)}, f32[60,128]{1,0:T(8,128)S(1)}, u32[]{:S(2)}, u32[]{:S(2)}) collective-permute-start(f32[60,128]{1,0:T(8,128)} %get-tuple-element.119), channel_id=1, source_target_pairs={{1,0},{2,1},{3,2},{4,3},{5,4},{6,5},{7,6},{8,7},{9,8},{10,9},{11,1... | collective-permute-start | bytes 92168 | tf_op jit(solution)/shard_map/ppermute | solution.py:731
  142.6 2.1 copy-start.14
  142.6 2.1 copy-start.15
  142.6 2.0 copy-start.26
  151.9 26.1 %copy-start.47 = (f32[4,8,1920]{2,1,0:T(8,128)S(1)}, f32[4,8,1920]{2,1,0:T(8,128)}, u32[]{:S(2)}) copy-start(f32[4,8,1920]{2,1,0:T(8,128)} %get-tuple-element.136) | copy-start | bytes 737284
  151.9 28.4 %copy-start.45 = (f32[4,8,1920]{2,1,0:T(8,128)S(1)}, f32[4,8,1920]{2,1,0:T(8,128)}, u32[]{:S(2)}) copy-start(f32[4,8,1920]{2,1,0:T(8,128)} %get-tuple-element.137) | copy-start | bytes 737284
  151.9 18.9 %all-to-all-start.6 = ((f32[16,8,4,128]{3,2,1,0:T(4,128)}), f32[16,8,4,128]{3,2,1,0:T(4,128)S(1)}, u32[]{:S(2)}, u32[]{:S(2)}) async-start(f32[16,8,4,128]{3,2,1,0:T(4,128)} %bitcast.74), calls=%async_computation.6 | async-start | bytes 524288 | tf_op jit(solution)/shard_map/all_to_all | solution.py:737
  160.7 3.6 %collective-permute-start.16 = (f32[32,128]{1,0:T(8,128)}, f32[32,128]{1,0:T(8,128)S(1)}, u32[]{:S(2)}, u32[]{:S(2)}) collective-permute-start(f32[32,128]{1,0:T(8,128)} %get-tuple-element.124), channel_id=1, source_target_pairs={{0,1},{1,2},{2,3},{3,4},{4,5},{5,6},{6,7},{7,8},{8,9},{9,10},{10,1... | collective-permute-start | bytes 49160 | tf_op jit(solution)/shard_map/ppermute | solution.py:731
  163.0 4.4 %collective-permute-start.17 = (f32[32,128]{1,0:T(8,128)}, f32[32,128]{1,0:T(8,128)S(1)}, u32[]{:S(2)}, u32[]{:S(2)}) collective-permute-start(f32[32,128]{1,0:T(8,128)} %get-tuple-element.125), channel_id=1, source_target_pairs={{1,0},{2,1},{3,2},{4,3},{5,4},{6,5},{7,6},{8,7},{9,8},{10,9},{11,1... | collective-permute-start | bytes 49160 | tf_op jit(solution)/shard_map/ppermute | solution.py:731
  164.4 22.1 %copy-start.37 = (f32[32,128]{1,0:T(8,128)}, f32[32,128]{1,0:T(8,128)S(1)}, u32[]{:S(2)}) copy-start(f32[32,128]{1,0:T(8,128)S(1)} %collective-permute-done.16.refs_3_) | copy-start | bytes 49156
  167.5 19.0 %copy-start.38 = (f32[32,128]{1,0:T(8,128)}, f32[32,128]{1,0:T(8,128)S(1)}, u32[]{:S(2)}) copy-start(f32[32,128]{1,0:T(8,128)S(1)} %collective-permute-done.17.refs_4_) | copy-start | bytes 49156
  173.6 12.8 %all-to-all-start.7 = ((f32[16,5,4,128]{3,2,1,0:T(4,128)}), f32[16,5,4,128]{3,2,1,0:T(4,128)S(1)}, u32[]{:S(2)}, u32[]{:S(2)}) async-start(f32[16,5,4,128]{3,2,1,0:T(4,128)} %bitcast.73), calls=%async_computation.7 | async-start | bytes 327680 | tf_op jit(solution)/shard_map/all_to_all | solution.py:737
  178.0 13.6 %collective-permute-start.18 = (f32[4,8,1920]{2,1,0:T(8,128)S(1)}, f32[4,8,1920]{2,1,0:T(8,128)S(1)}, u32[]{:S(2)}, u32[]{:S(2)}) collective-permute-start(f32[4,8,1920]{2,1,0:T(8,128)S(1)} %copy-done.47), channel_id=1, source_target_pairs={{0,1},{1,2},{2,3},{3,4},{4,5},{5,6},{6,7},{7,8},{8,9},{9,10},{10,1... | collective-permute-start | bytes 737288 | tf_op jit(solution)/shard_map/ppermute | solution.py:731
  180.3 11.3 %collective-permute-start.19 = (f32[4,8,1920]{2,1,0:T(8,128)S(1)}, f32[4,8,1920]{2,1,0:T(8,128)S(1)}, u32[]{:S(2)}, u32[]{:S(2)}) collective-permute-start(f32[4,8,1920]{2,1,0:T(8,128)S(1)} %copy-done.45), channel_id=1, source_target_pairs={{1,0},{2,1},{3,2},{4,3},{5,4},{6,5},{7,6},{8,7},{9,8},{10,9},{11,1... | collective-permute-start | bytes 737288 | tf_op jit(solution)/shard_map/ppermute | solution.py:731
  189.0 2.6 %collective-permute-start.20 = (f32[60,128]{1,0:T(8,128)}, f32[60,128]{1,0:T(8,128)S(1)}, u32[]{:S(2)}, u32[]{:S(2)}) collective-permute-start(f32[60,128]{1,0:T(8,128)} %get-tuple-element.138), channel_id=1, source_target_pairs={{0,1},{1,2},{2,3},{3,4},{4,5},{5,6},{6,7},{7,8},{8,9},{9,10},{10,1... | collective-permute-start | bytes 92168 | tf_op jit(solution)/shard_map/ppermute | solution.py:731
  190.3 3.3 %collective-permute-start.21 = (f32[60,128]{1,0:T(8,128)}, f32[60,128]{1,0:T(8,128)S(1)}, u32[]{:S(2)}, u32[]{:S(2)}) collective-permute-start(f32[60,128]{1,0:T(8,128)} %get-tuple-element.139), channel_id=1, source_target_pairs={{1,0},{2,1},{3,2},{4,3},{5,4},{6,5},{7,6},{8,7},{9,8},{10,9},{11,1... | collective-permute-start | bytes 92168 | tf_op jit(solution)/shard_map/ppermute | solution.py:731
  191.6 2.0 copy-start.17
  191.6 2.0 copy-start.19
  191.7 2.0 copy-start.29
  200.4 14.4 %all-to-all-start.8 = ((f32[16,1,128]{2,1,0:T(1,128)}), f32[16,1,128]{2,1,0:T(1,128)S(1)}, u32[]{:S(2)}, u32[]{:S(2)}) async-start(f32[16,1,128]{2,1,0:T(1,128)} %bitcast.82), calls=%async_computation.8 | async-start | bytes 16384 | tf_op jit(solution)/shard_map/all_to_all | solution.py:919
  (18 other events, 13.0 us)
